TPU v7x, 128 devices: a whole 4x4x4 slice. The times are simulated.
128 devices in a mesh: row: 8 (over x, z_lo), col: 16 (over z_hi, y, core).
Axes of the slice: x: 4, y: 4, z: 4 (z_hi: 2, z_lo: 2; z = z_hi * 2 + z_lo), core: 2. Of those that a mesh axis runs over, the one named last changes fastest.
Arguments:
- inputs: bfloat16 [2048, 16384], P('col', 'row'), may hold values from -0.25 to 0.25
- weight: bfloat16 [16384, 18432], P('row', 'col'), may hold values from -0.046875 to 0.046875
- out_grad: bfloat16 [2048, 18432], P('row', 'col'), may hold values from -3 to 3
Outputs:
- input_grad: bfloat16 [2048, 16384], P('col', 'row')
- weight_grad: float32 [16384, 18432], P('row', 'col')
All inputs are finite; a program needn't handle non-finite values.
Results may differ from a plain program's by a relative error of at most 0.019.
Values may be sent and summed in bfloat16 or wider, within the bound.
No kernel may reach another device: no remote copies, remote signals or barrier semaphores. Data moves between devices by JAX's collectives and lax.ppermute only.
A program may use at most 128 MiB of HBM per device.

v0:
```python
import jax
import jax.numpy as jnp
from jax import lax
from jax.sharding import PartitionSpec as P


def on_device(inputs, weight, out_grad):
    gathered = lax.all_gather(out_grad, "row", axis=0, tiled=True)
    grads = gathered
    summed = lax.psum_scatter(
        lax.dot_general(
            grads, weight, (((1,), (1,)), ((), ())), preferred_element_type=jnp.float32
        ).astype(jnp.bfloat16),
        "col",
        scatter_dimension=0,
        tiled=True,
    )
    grads = gathered
    weight_grad = lax.dot_general(
        lax.all_gather(inputs, "col", axis=0, tiled=True),
        grads,
        (((0,), (0,)), ((), ())),
        preferred_element_type=jnp.float32,
    )
    return (summed, weight_grad)


def solution(mesh):
    placed = (P("col", "row"), P("row", "col"), P("row", "col"))
    return jax.shard_map(
        on_device,
        mesh=mesh,
        in_specs=placed,
        out_specs=(P("col", "row"), P("row", "col")),
        check_vma=False,
    )
```

profile of v0, /device:TPU:24, one launch (start us, length us, event | category | flops | bytes accessed | tf_op | source)
XLA Modules:
  0.0 299.1 jit_solution(17948049294770521187)
XLA Ops:
  7.2 0.0 all-gather.3.cloned.1.call-start
  7.2 0.7 all-gather.3.cloned.1.call-update
  7.9 0.0 all-gather.5.cloned.1.call-start
  7.9 0.7 all-gather.5.cloned.1.call-update
  8.6 0.0 reduce-scatter.2.cloned.1.call-start
  8.7 102.7 %all-gather.3.cloned.1.call-done = bf16[2048,1152]{1,0:T(8,128)(2,1)} async-done(((bf16[256,1152]{1,0:T(8,128)(2,1)}), bf16[2048,1152]{1,0:T(8,128)(2,1)}) %all-gather.3.cloned.1.call-update) | async-done | bytes 4718608 | tf_op jit(solution)/shard_map/all_gather | solution.py:8
  111.4 16.4 %convolution_convert_fusion = bf16[2048,2048]{1,0:T(8,128)(2,1)} fusion(bf16[2048,1152]{1,0:T(8,128)(2,1)} %all-gather.3.cloned.1.call-done, bf16[2048,1152]{1,0:T(8,128)(2,1)} %param.4), kind=kOutput, calls=%fused_computation | convolution fusion | flops 9667870720 | bytes 17825792 | tf_op jit(solution)/shard_map/dot_general | solution.py:11
  127.8 0.0 reduce-scatter.2.cloned.1.call-update
  127.8 57.9 %all-gather.5.cloned.1.call-done = bf16[2048,2048]{1,0:T(8,128)(2,1)} async-done(((bf16[128,2048]{1,0:T(8,128)(2,1)}), bf16[2048,2048]{1,0:T(8,128)(2,1)}) %all-gather.5.cloned.1.call-update) | async-done | bytes 8388624 | tf_op jit(solution)/shard_map/all_gather | solution.py:20
  185.8 17.2 %fusion = f32[2048,1152]{1,0:T(8,128)} fusion(bf16[2048,2048]{1,0:T(8,128)(2,1)} %all-gather.5.cloned.1.call-done, bf16[2048,1152]{1,0:T(8,128)(2,1)} %all-gather.3.cloned.1.call-done), kind=kOutput, calls=%fused_computation.1 | convolution fusion | flops 9663676416 | bytes 22544384 | tf_op jit(solution)/shard_map/dot_general | solution.py:19
  202.9 89.6 %reduce-scatter.2.cloned.1.call-done = bf16[128,2048]{1,0:T(8,128)(2,1)} async-done(((bf16[2048,2048]{1,0:T(8,128)(2,1)}), bf16[128,2048]{1,0:T(8,128)(2,1)}) %reduce-scatter.2.cloned.1.call-update) | async-done | bytes 524304 | tf_op jit(solution)/shard_map/reduce_scatter | solution.py:10
Async XLA Ops:
  7.2 104.2 %all-gather.3.cloned.1.call-start = ((), (), s32[]{:S(2)}) async-start(), calls=%async_computation.1 | async-start | bytes 5308416 | tf_op jit(solution)/shard_map/all_gather | solution.py:8
  7.9 177.9 %all-gather.5.cloned.1.call-start = ((), (), s32[]{:S(2)}) async-start(), calls=%async_computation.3 | async-start | bytes 8912896 | tf_op jit(solution)/shard_map/all_gather | solution.py:20
  8.6 283.9 %reduce-scatter.2.cloned.1.call-start = ((), (), s32[]{:S(2)}) async-start(), calls=%async_computation.2 | async-start | bytes 8912896 | tf_op jit(solution)/shard_map/reduce_scatter | solution.py:10
Sparse Core Ops, SparseCore 0:
  9.6 101.7 all-gather.2
  113.8 71.8 all-gather.4
  190.7 101.8 reduce-scatter.1
where the time goes:
time: 300 us; the launch traced here: 299 us
  waiting for transfers between devices  252 us (84%)
  matrix products  33.5 us (11%)
  between operations  13.7 us (5%)
    all_gather x1, waiting for transfers between devices, on_device(): gathered = lax.all_gather(out_grad, 'row', axis=0, tiled=True)  103 us
    reduce_scatter x1, waiting for transfers between devices, on_device(): lax.psum_scatter(lax.dot_general(grads, weight, (((1,), (1,)), ((), ())),...  89.6 us
    all_gather x1, waiting for transfers between devices, on_device(): lax.all_gather(inputs, 'col', axis=0, tiled=True)  57.9 us
    dot_general x1, matrix products, on_device(): lax.dot_general(lax.all_gather(inputs, 'col', axis=0, tiled=True), grads,...  17.2 us
    dot_general x1, matrix products, on_device(): lax.dot_general(grads, weight, (((1,), (1,)), ((), ())), preferred_elemen...  16.4 us
  transfers between devices with their start and end apart: 3, of which 3 were waited for; matrix products, arithmetic and copies ran while one was open for 11% of the time, Pallas kernels for 0%

commit v1 on v0

v1 whole, which is shorter than its diff:
```python
import jax
import jax.numpy as jnp
from jax import lax
from jax.sharding import Mesh
from jax.sharding import PartitionSpec as P

AXES = ("x", "zl", "zh", "y", "core")
SIZES = (4, 2, 2, 4, 2)


def shift(value, axis, step):
    return lax.ppermute(value, axis, [(i, (i + step) % 4) for i in range(4)])


def swap(value, axis):
    return lax.ppermute(value, axis, [(0, 1), (1, 0)])


def after(value, *others):
    return lax.optimization_barrier((value, *others))[0]


def dot_nt(a, b):
    return lax.dot_general(a, b, (((1,), (1,)), ((), ())), preferred_element_type=jnp.float32)


def on_device(inputs, weight, out_grad):
    bf16, f32 = jnp.bfloat16, jnp.float32
    x, zl, zh, y, core = (lax.axis_index(axis) for axis in AXES)

    g = out_grad
    g1, g3, g2 = shift(g, "x", 1), shift(g, "x", -1), shift(g, "x", 2)
    h = swap(g, "zl")
    h1, h3 = shift(h, "x", 1), shift(h, "x", -1)
    h2 = swap(g2, "zl")

    a = inputs
    a1 = shift(a, "y", 1)
    a3 = shift(after(a, a1), "y", -1)
    b = swap(after(a, h), "zh")
    a2 = shift(after(a, a3), "y", 2)
    b1 = shift(after(b, h1), "y", 1)
    b3 = shift(after(b, a2), "y", -1)
    b2 = shift(after(b, b1), "y", 2)

    grads = jnp.zeros((2, 8, 128, 1152), bf16)
    for block, dx, dz in ((g, 0, 0), (g1, 3, 0), (g3, 1, 0), (g2, 2, 0), (h, 0, 1), (h1, 3, 1), (h3, 1, 1), (h2, 2, 1)):
        bx, bz = (x + dx) & 3, zl ^ dz
        slot = (zh ^ (bx >> 1)) * 4 + ((((bx & 1) << 1) + bz - y) & 3)
        block = block.reshape(2, 1, 1, 128, 1152)
        for dc in range(2):
            half = lax.dynamic_index_in_dim(block, core ^ dc, 0, keepdims=False)
            grads = lax.dynamic_update_slice(grads, half, (dc, slot, 0, 0))
    mine, theirs = grads[0].reshape(1024, 1152), grads[1].reshape(1024, 1152)

    def partial(w):
        other = swap(dot_nt(theirs, w).astype(bf16), "core")
        return (dot_nt(mine, w) + other.astype(f32)).astype(bf16).reshape(2, 4, 128, 1024)

    def over_y(p):
        return p[:, 0], shift(p[:, 1], "y", 1), shift(p[:, 3], "y", -1), shift(p[:, 2], "y", 2)

    def over_zh(p):
        return p[0], swap(p[1], "zh")

    def total(parts):
        return sum(part.astype(f32) for part in parts)

    pa, pb = partial(weight[:1024]), partial(weight[1024:])
    sa, sb = over_y(pa), over_zh(pb)

    own = jnp.concatenate([a, a3, a2, a1, b, b3, b2, b1], axis=0)
    own = after(own, pb)
    tokens = jnp.concatenate([own, swap(own, "core")], axis=0)
    weight_grad = lax.dot_general(
        tokens, grads.reshape(2048, 1152), (((0,), (0,)), ((), ())), preferred_element_type=f32
    )

    sa, sb, weight_grad = lax.optimization_barrier((sa, sb, weight_grad))
    sa, sb = over_zh(total(sa).astype(bf16)), over_y(total(sb).astype(bf16)[None])
    input_grad = jnp.concatenate([total(sa), total(sb)[0]], axis=1).astype(bf16)
    return input_grad, weight_grad


def solution(mesh):
    fine = Mesh(mesh.devices.reshape(SIZES), AXES)
    row, col = ("x", "zl"), ("zh", "y", "core")
    return jax.shard_map(
        on_device,
        mesh=fine,
        in_specs=(P(col, row), P(row, col), P(row, col)),
        out_specs=(P(col, row), P(row, col)),
        check_vma=False,
    )
```

time: 300 us -> 148 us (0.49)
  waiting for transfers between devices: 252 us -> 52.8 us
  starting transfers between devices: 0.11 us -> 41.1 us
  local copies, waits for them, and re-layouts: 0 us -> 21.4 us
  between operations: 13.7 us -> 0.87 us
  matrix products: 33.5 us -> 28.7 us
    all_gather x2 -> x0, waiting for transfers between devices: 161 us -> none  [the longest x1 103 us: on_device(): gathered = lax.all_gather(out_grad, 'row', axis=0, tiled=True)]
    reduce_scatter x1 -> x0, waiting for transfers between devices: 89.6 us -> none  [on_device(): lax.psum_scatter(lax.dot_general(grads, weight, (((1,), (1,)), ((), ())),...]
    ppermute x0 -> x25, waiting for transfers between devices: none -> 52.8 us  [the longest x17 40.6 us: shift(): return lax.ppermute(value, axis, [(i, (i + step) % 4) for i in range(4)])]
    ppermute x0 -> x25, starting transfers between devices: none -> 41.1 us  [the longest x17 26 us: shift(): return lax.ppermute(value, axis, [(i, (i + step) % 4) for i in range(4)])]
    dynamic_update_slice x0 -> x16, local copies, waits for them, and re-layouts: none -> 11.8 us  [on_device(): grads = lax.dynamic_update_slice(grads, half, (dc, slot, 0, 0))]
    dot_general x2 -> x5, matrix products: 33.5 us -> 28.7 us  [the longest x1 16.2 us: on_device(): lax.dot_general(tokens, grads.reshape(2048, 1152), (((0,), (0,)), ((), ()...]
    slice x0 -> x2, local copies, waits for them, and re-layouts: none -> 3.38 us  [the longest x1 3.2 us: on_device(): mine, theirs = (grads[0].reshape(1024, 1152), grads[1].reshape(1024, 1152))]
    unnamed x0 -> x17, local copies, waits for them, and re-layouts: none -> 3.19 us
  transfers between devices with their start and end apart: 3 -> 25, of which waited for: 3 -> 12; matrix products, arithmetic and copies ran while one was open for 11% -> 34% of each run, Pallas kernels for 0% -> 0%
where the time goes in v1:
time: 148 us; the launch traced here: 147 us
  waiting for transfers between devices  52.8 us (36%)
  starting transfers between devices  41.1 us (28%)
  matrix products  28.7 us (19%)
  local copies, waits for them, and re-layouts  21.4 us (14%)
  other arithmetic  1.85 us (1%)
    ppermute x17, waiting for transfers between devices, shift(): return lax.ppermute(value, axis, [(i, (i + step) % 4) for i in range(4)])  40.6 us
    ppermute x17, starting transfers between devices, shift(): return lax.ppermute(value, axis, [(i, (i + step) % 4) for i in range(4)])  26 us
    dot_general x1, matrix products, on_device(): lax.dot_general(tokens, grads.reshape(2048, 1152), (((0,), (0,)), ((), ()...  16.2 us
    ppermute x8, starting transfers between devices, swap(): return lax.ppermute(value, axis, [(0, 1), (1, 0)])  15.1 us
    dot_general x4, matrix products, dot_nt(): lax.dot_general(a, b, (((1,), (1,)), ((), ())), preferred_element_type=jn...  12.5 us
    ppermute x8, waiting for transfers between devices, swap(): return lax.ppermute(value, axis, [(0, 1), (1, 0)])  12.2 us
    dynamic_update_slice x16, local copies, waits for them, and re-layouts, on_device(): grads = lax.dynamic_update_slice(grads, half, (dc, slot, 0, 0))  11.8 us
    slice x1, local copies, waits for them, and re-layouts, on_device(): mine, theirs = (grads[0].reshape(1024, 1152), grads[1].reshape(1024, 1152))  3.2 us
  transfers between devices with their start and end apart: 25, of which 12 were waited for; matrix products, arithmetic and copies ran while one was open for 34% of the time, Pallas kernels for 0%

profile of v1, /device:TPU:24, one launch (start us, length us, event | category | flops | bytes accessed | tf_op | source)
XLA Modules:
  0.0 146.8 jit_solution(8452507920842375636)
XLA Ops:
  0.6 2.8 %collective-permute-start.1 = (bf16[256,1152]{1,0:T(8,128)(2,1)}, bf16[256,1152]{1,0:T(8,128)(2,1)S(1)}, u32[]{:S(2)}, u32[]{:S(2)}) collective-permute-start(bf16[256,1152]{1,0:T(8,128)(2,1)} %param.5), channel_id=1, source_target_pairs={{0,96},{32,0},{64,32},{96,64},{1,97},{33,1},{65,33},{97,65},{2,98}... | collective-permute-start | bytes 1769480 | tf_op jit(solution)/shard_map/ppermute | solution.py:12
  3.5 1.9 %collective-permute-start.3 = (bf16[256,1152]{1,0:T(8,128)(2,1)}, bf16[256,1152]{1,0:T(8,128)(2,1)S(1)}, u32[]{:S(2)}, u32[]{:S(2)}) collective-permute-start(bf16[256,1152]{1,0:T(8,128)(2,1)} %param.5), channel_id=1, source_target_pairs={{0,16},{16,0},{1,17},{17,1},{2,18},{18,2},{3,19},{19,3},{4,20},{20... | collective-permute-start | bytes 1769480 | tf_op jit(solution)/shard_map/ppermute | solution.py:16
  5.4 2.3 %collective-permute-start.2 = (bf16[256,1152]{1,0:T(8,128)(2,1)}, bf16[256,1152]{1,0:T(8,128)(2,1)S(1)}, u32[]{:S(2)}, u32[]{:S(2)}) collective-permute-start(bf16[256,1152]{1,0:T(8,128)(2,1)} %param.5), channel_id=1, source_target_pairs={{0,64},{32,96},{64,0},{96,32},{1,65},{33,97},{65,1},{97,33},{2,66}... | collective-permute-start | bytes 1769480 | tf_op jit(solution)/shard_map/ppermute | solution.py:12
  7.7 0.2 collective-permute-start.13
  7.9 1.9 %constant_dynamic-update-slice_fusion.7 = bf16[1024,2048]{1,0:T(8,128)(2,1)} fusion(bf16[128,2048]{1,0:T(8,128)(2,1)} %param.3), kind=kLoop, calls=%fused_computation.60 | loop fusion | bytes 1048576
  9.8 2.8 %broadcast_in_dim.6 = bf16[2,8,128,1152]{3,2,1,0:T(8,128)(2,1)} broadcast(bf16[]{:T(256)} %constant.56.clone.1), dimensions={} | broadcast | bytes 4718594 | tf_op jit(solution)/shard_map/broadcast_in_dim | solution.py:46
  12.6 0.7 bitcast_dynamic-update-slice_fusion.15
  13.3 0.7 bitcast_dynamic-update-slice_fusion.14
  14.1 6.5 %collective-permute-done.13 = bf16[128,2048]{1,0:T(8,128)(2,1)} collective-permute-done((bf16[128,2048]{1,0:T(8,128)(2,1)}, bf16[128,2048]{1,0:T(8,128)(2,1)}, u32[]{:S(2)}, u32[]{:S(2)}) %collective-permute-start.13) | collective-permute-done | bytes 524320 | tf_op jit(solution)/shard_map/ppermute | solution.py:12
  20.5 0.7 collective-permute-start.14
  21.3 3.6 %collective-permute-start.16 = (bf16[128,2048]{1,0:T(8,128)(2,1)S(1)}, bf16[128,2048]{1,0:T(8,128)(2,1)S(1)}, u32[]{:S(2)}, u32[]{:S(2)}) collective-permute-start(bf16[128,2048]{1,0:T(8,128)(2,1)S(1)} %copy-done.1), channel_id=1, source_target_pairs={{0,8},{8,0},{1,9},{9,1},{2,10},{10,2},{3,11},{11,3},{4,12},{12,4},... | collective-permute-start | bytes 1572872 | tf_op jit(solution)/shard_map/ppermute | solution.py:16
  24.9 7.4 %collective-permute-done = bf16[256,1152]{1,0:T(8,128)(2,1)S(1)} collective-permute-done((bf16[256,1152]{1,0:T(8,128)(2,1)}, bf16[256,1152]{1,0:T(8,128)(2,1)S(1)}, u32[]{:S(2)}, u32[]{:S(2)}) %collective-permute-start) | collective-permute-done | bytes 589856 | tf_op jit(solution)/shard_map/ppermute | solution.py:12
  32.3 0.7 bitcast_dynamic-update-slice_fusion.13
  33.1 0.7 bitcast_dynamic-update-slice_fusion.12
  33.8 0.7 bitcast_dynamic-update-slice_fusion.11
  34.5 0.7 bitcast_dynamic-update-slice_fusion.10
  35.3 0.8 bitcast_dynamic-update-slice_fusion.9
  36.1 0.7 bitcast_dynamic-update-slice_fusion.8
  36.8 0.7 bitcast_dynamic-update-slice_fusion.7
  37.5 3.2 %collective-permute-start.5 = (bf16[256,1152]{1,0:T(8,128)(2,1)S(1)}, bf16[256,1152]{1,0:T(8,128)(2,1)S(1)}, u32[]{:S(2)}, u32[]{:S(2)}) collective-permute-start(bf16[256,1152]{1,0:T(8,128)(2,1)S(1)} %collective-permute-done.3), channel_id=1, source_target_pairs={{0,96},{32,0},{64,32},{96,64},{1,97},{33,1},{65,33},{97,65},{2,98}... | collective-permute-start | bytes 1769480 | tf_op jit(solution)/shard_map/ppermute | solution.py:12
  40.8 1.9 %collective-permute-start.6 = (bf16[256,1152]{1,0:T(8,128)(2,1)S(1)}, bf16[256,1152]{1,0:T(8,128)(2,1)S(1)}, u32[]{:S(2)}, u32[]{:S(2)}) collective-permute-start(bf16[256,1152]{1,0:T(8,128)(2,1)S(1)} %collective-permute-done.2), channel_id=1, source_target_pairs={{0,16},{16,0},{1,17},{17,1},{2,18},{18,2},{3,19},{19,3},{4,20},{20... | collective-permute-start | bytes 1769480 | tf_op jit(solution)/shard_map/ppermute | solution.py:16
  42.6 0.7 bitcast_dynamic-update-slice_fusion.6
  43.4 1.3 collective-permute-start.15
  44.7 3.3 %collective-permute-done.4 = bf16[256,1152]{1,0:T(8,128)(2,1)S(1)} collective-permute-done((bf16[256,1152]{1,0:T(8,128)(2,1)S(1)}, bf16[256,1152]{1,0:T(8,128)(2,1)S(1)}, u32[]{:S(2)}, u32[]{:S(2)}) %collective-permute-start.4) | collective-permute-done | bytes 589856 | tf_op jit(solution)/shard_map/ppermute | solution.py:12
  48.0 0.2 collective-permute-start.18
  48.2 0.7 bitcast_dynamic-update-slice_fusion.5
  49.0 0.7 bitcast_dynamic-update-slice_fusion.4
  49.7 0.7 bitcast_dynamic-update-slice_fusion.3
  50.4 0.7 bitcast_dynamic-update-slice_fusion.2
  51.2 0.7 bitcast_dynamic-update-slice_fusion.1
  51.9 0.7 bitcast_dynamic-update-slice_fusion
  52.7 3.2 %fusion.29 = (bf16[1,8,128,1152]{3,2,1,0:T(8,128)(2,1)S(1)}, bf16[1,8,128,1152]{3,2,1,0:T(8,128)(2,1)S(1)}) fusion(bf16[2,8,128,1152]{3,2,1,0:T(8,128)(2,1)} %bitcast_dynamic-update-slice_fusion), kind=kLoop, calls=%fused_computation.62 | loop fusion | bytes 9437184 | tf_op jit(solution)/shard_map/slice | solution.py:54
  55.9 3.3 %collective-permute-start.17 = (bf16[128,2048]{1,0:T(8,128)(2,1)S(1)}, bf16[128,2048]{1,0:T(8,128)(2,1)S(1)}, u32[]{:S(2)}, u32[]{:S(2)}) collective-permute-start(bf16[128,2048]{1,0:T(8,128)(2,1)S(1)} %collective-permute-done.16), channel_id=1, source_target_pairs={{0,6},{2,0},{4,2},{6,4},{1,7},{3,1},{5,3},{7,5},{8,14},{10,8},{12,... | collective-permute-start | bytes 1572872 | tf_op jit(solution)/shard_map/ppermute | solution.py:12
  59.2 2.3 %collective-permute-done.18 = bf16[128,2048]{1,0:T(8,128)(2,1)S(1)} collective-permute-done((bf16[128,2048]{1,0:T(8,128)(2,1)S(1)}, bf16[128,2048]{1,0:T(8,128)(2,1)S(1)}, u32[]{:S(2)}, u32[]{:S(2)}) %collective-permute-start.18) | collective-permute-done | bytes 524320 | tf_op jit(solution)/shard_map/ppermute | solution.py:12
  61.5 3.8 %collective-permute-start.19 = (bf16[128,2048]{1,0:T(8,128)(2,1)S(1)}, bf16[128,2048]{1,0:T(8,128)(2,1)S(1)}, u32[]{:S(2)}, u32[]{:S(2)}) collective-permute-start(bf16[128,2048]{1,0:T(8,128)(2,1)S(1)} %collective-permute-done.16), channel_id=1, source_target_pairs={{0,4},{2,6},{4,0},{6,2},{1,5},{3,7},{5,1},{7,3},{8,12},{10,14},{12... | collective-permute-start | bytes 1572872 | tf_op jit(solution)/shard_map/ppermute | solution.py:12
  65.4 1.1 constant_dynamic-update-slice_fusion.4
  66.5 4.1 %collective-permute-done.17 = bf16[128,2048]{1,0:T(8,128)(2,1)S(1)} collective-permute-done((bf16[128,2048]{1,0:T(8,128)(2,1)S(1)}, bf16[128,2048]{1,0:T(8,128)(2,1)S(1)}, u32[]{:S(2)}, u32[]{:S(2)}) %collective-permute-start.17) | collective-permute-done | bytes 524320 | tf_op jit(solution)/shard_map/ppermute | solution.py:12
  70.6 7.9 %collective-permute-done.19 = bf16[128,2048]{1,0:T(8,128)(2,1)S(1)} collective-permute-done((bf16[128,2048]{1,0:T(8,128)(2,1)S(1)}, bf16[128,2048]{1,0:T(8,128)(2,1)S(1)}, u32[]{:S(2)}, u32[]{:S(2)}) %collective-permute-start.19) | collective-permute-done | bytes 524320 | tf_op jit(solution)/shard_map/ppermute | solution.py:12
  78.7 3.1 %fusion.12 = bf16[1024,1024]{1,0:T(8,128)(2,1)S(1)} fusion(bf16[1024,1152]{1,0:T(8,128)(2,1)S(1)} %bitcast.92, bf16[2048,1152]{1,0:T(8,128)(2,1)S(1)} %bitcast.113), kind=kOutput, calls=%fused_computation.15 | convolution fusion | flops 2416967680 | bytes 6815744 | tf_op jit(solution)/shard_map/dot_general | solution.py:24
  81.9 0.5 collective-permute-start.7
  82.4 3.1 %fusion.15 = bf16[1024,1024]{1,0:T(8,128)(2,1)S(1)} fusion(bf16[1024,1152]{1,0:T(8,128)(2,1)S(1)} %bitcast.93, bf16[2048,1152]{1,0:T(8,128)(2,1)S(1)} %bitcast.113), kind=kOutput, calls=%fused_computation.16 | convolution fusion | flops 2416967680 | bytes 6815744 | tf_op jit(solution)/shard_map/dot_general | solution.py:24
  85.5 0.1 collective-permute-start.11
  85.7 3.2 %collective-permute-done.7 = bf16[1024,1024]{1,0:T(8,128)(2,1)S(1)} collective-permute-done((bf16[1024,1024]{1,0:T(8,128)(2,1)S(1)}, bf16[1024,1024]{1,0:T(8,128)(2,1)S(1)}, u32[]{:S(2)}, u32[]{:S(2)}) %collective-permute-start.7) | collective-permute-done | bytes 2097184 | tf_op jit(solution)/shard_map/ppermute | solution.py:16
  88.8 3.1 %add_convert_fusion.1 = bf16[1024,1024]{1,0:T(8,128)(2,1)S(1)} fusion(bf16[1024,1024]{1,0:T(8,128)(2,1)S(1)} %collective-permute-done.7, bf16[1024,1152]{1,0:T(8,128)(2,1)S(1)} %bitcast.90, bf16[2048,1152]{1,0:T(8,128)(2,1)S(1)} %bitcast.113), kind=kOutput, calls=%fused_computation.5 | convolution fusion | flops 2419064832 | bytes 8912896 | tf_op jit(solution)/shard_map/dot_general | solution.py:24
  92.0 0.2 slice_bitcast_fusion
  92.2 2.7 %collective-permute-start.10 = (bf16[2,128,1024]{2,1,0:T(8,128)(2,1)S(1)}, bf16[2,128,1024]{2,1,0:T(8,128)(2,1)S(1)}, u32[]{:S(2)}, u32[]{:S(2)}) collective-permute-start(bf16[2,128,1024]{2,1,0:T(8,128)(2,1)S(1)} %get-tuple-element.32), channel_id=1, source_target_pairs={{0,4},{2,6},{4,0},{6,2},{1,5},{3,7},{5,1},{7,3},{8,12},{10,14},{12... | collective-permute-start | bytes 1572872 | tf_op jit(solution)/shard_map/ppermute | solution.py:12
  94.9 3.2 %collective-permute-start.8 = (bf16[2,128,1024]{2,1,0:T(8,128)(2,1)S(1)}, bf16[2,128,1024]{2,1,0:T(8,128)(2,1)S(1)}, u32[]{:S(2)}, u32[]{:S(2)}) collective-permute-start(bf16[2,128,1024]{2,1,0:T(8,128)(2,1)S(1)} %get-tuple-element.34), channel_id=1, source_target_pairs={{0,2},{2,4},{4,6},{6,0},{1,3},{3,5},{5,7},{7,1},{8,10},{10,12},{12... | collective-permute-start | bytes 1572872 | tf_op jit(solution)/shard_map/ppermute | solution.py:12
  98.1 3.1 %add_convert_fusion = bf16[1024,1024]{1,0:T(8,128)(2,1)S(1)} fusion(bf16[1024,1024]{1,0:T(8,128)(2,1)S(1)} %collective-permute-done.11, bf16[1024,1152]{1,0:T(8,128)(2,1)S(1)} %bitcast.91, bf16[2048,1152]{1,0:T(8,128)(2,1)S(1)} %bitcast.113), kind=kOutput, calls=%fused_computation.4 | convolution fusion | flops 2419064832 | bytes 8912896 | tf_op jit(solution)/shard_map/dot_general | solution.py:24
  101.3 0.2 fusion.30
  101.4 3.7 %collective-permute-start.12 = (bf16[4,128,1024]{2,1,0:T(8,128)(2,1)S(1)}, bf16[4,128,1024]{2,1,0:T(8,128)(2,1)S(1)}, u32[]{:S(2)}, u32[]{:S(2)}) collective-permute-start(bf16[4,128,1024]{2,1,0:T(8,128)(2,1)S(1)} %bitcast.95), channel_id=1, source_target_pairs={{0,8},{8,0},{1,9},{9,1},{2,10},{10,2},{3,11},{11,3},{4,12},{12,4},... | collective-permute-start | bytes 3145736 | tf_op jit(solution)/shard_map/ppermute | solution.py:16
  105.1 16.2 %fusion = f32[2048,1152]{1,0:T(8,128)} fusion(bf16[2048,1152]{1,0:T(8,128)(2,1)} %bitcast.33, bf16[1024,2048]{1,0:T(8,128)(2,1)S(1)} %collective-permute-done.20, bf16[1024,2048]{1,0:T(8,128)(2,1)S(1)} %constant_dynamic-update-slice_fusion), kind=kOutput, calls=%fused_computation | convolution fusion | flops 9680453632 | bytes 22544384 | tf_op jit(solution)/shard_map/dot_general | solution.py:75
  121.3 6.5 %collective-permute-done.12 = bf16[4,128,1024]{2,1,0:T(8,128)(2,1)S(1)} collective-permute-done((bf16[4,128,1024]{2,1,0:T(8,128)(2,1)S(1)}, bf16[4,128,1024]{2,1,0:T(8,128)(2,1)S(1)}, u32[]{:S(2)}, u32[]{:S(2)}) %collective-permute-start.12) | collective-permute-done | bytes 1048608 | tf_op jit(solution)/shard_map/ppermute | solution.py:16
  127.8 0.4 add_convert_fusion.3
  128.2 3.3 %collective-permute-start.21 = (bf16[128,1024]{1,0:T(8,128)(2,1)S(1)}, bf16[128,1024]{1,0:T(8,128)(2,1)S(1)}, u32[]{:S(2)}, u32[]{:S(2)}) collective-permute-start(bf16[128,1024]{1,0:T(8,128)(2,1)S(1)} %slice_bitcast_fusion.8), channel_id=1, source_target_pairs={{0,8},{8,0},{1,9},{9,1},{2,10},{10,2},{3,11},{11,3},{4,12},{12,4},... | collective-permute-start | bytes 786440 | tf_op jit(solution)/shard_map/ppermute | solution.py:16
  131.5 0.4 fusion.22
  132.0 0.4 collective-permute-start.22
  132.3 0.9 collective-permute-start.24
  133.2 0.9 collective-permute-start.23
  134.1 2.6 %collective-permute-done.21 = bf16[128,1024]{1,0:T(8,128)(2,1)S(1)} collective-permute-done((bf16[128,1024]{1,0:T(8,128)(2,1)S(1)}, bf16[128,1024]{1,0:T(8,128)(2,1)S(1)}, u32[]{:S(2)}, u32[]{:S(2)}) %collective-permute-start.21) | collective-permute-done | bytes 262176 | tf_op jit(solution)/shard_map/ppermute | solution.py:16
  136.7 4.5 %collective-permute-done.22 = bf16[1,128,1024]{2,1,0:T(8,128)(2,1)S(1)} collective-permute-done((bf16[1,128,1024]{2,1,0:T(8,128)(2,1)S(1)}, bf16[1,128,1024]{2,1,0:T(8,128)(2,1)S(1)}, u32[]{:S(2)}, u32[]{:S(2)}) %collective-permute-start.22) | collective-permute-done | bytes 262176 | tf_op jit(solution)/shard_map/ppermute | solution.py:12
  141.2 1.8 %collective-permute-done.24 = bf16[1,128,1024]{2,1,0:T(8,128)(2,1)S(1)} collective-permute-done((bf16[1,128,1024]{2,1,0:T(8,128)(2,1)S(1)}, bf16[1,128,1024]{2,1,0:T(8,128)(2,1)S(1)}, u32[]{:S(2)}, u32[]{:S(2)}) %collective-permute-start.24) | collective-permute-done | bytes 262176 | tf_op jit(solution)/shard_map/ppermute | solution.py:12
  143.0 2.8 %collective-permute-done.23 = bf16[1,128,1024]{2,1,0:T(8,128)(2,1)S(1)} collective-permute-done((bf16[1,128,1024]{2,1,0:T(8,128)(2,1)S(1)}, bf16[1,128,1024]{2,1,0:T(8,128)(2,1)S(1)}, u32[]{:S(2)}, u32[]{:S(2)}) %collective-permute-start.23) | collective-permute-done | bytes 262176 | tf_op jit(solution)/shard_map/ppermute | solution.py:12
  145.8 0.2 fusion.27
  145.9 0.8 pad_maximum_fusion
  (37 shorter events, 0.5 us)
Async XLA Ops:
  0.6 12.0 %copy-start = (bf16[256,1152]{1,0:T(8,128)(2,1)S(1)}, bf16[256,1152]{1,0:T(8,128)(2,1)}, u32[]{:S(2)}) copy-start(bf16[256,1152]{1,0:T(8,128)(2,1)} %param.5) | copy-start | bytes 1769476
  0.6 19.9 %copy-start.1 = (bf16[128,2048]{1,0:T(8,128)(2,1)S(1)}, bf16[128,2048]{1,0:T(8,128)(2,1)}, u32[]{:S(2)}) copy-start(bf16[128,2048]{1,0:T(8,128)(2,1)} %param.3) | copy-start | bytes 1572868
  0.6 33.2 %collective-permute-start.1 = (bf16[256,1152]{1,0:T(8,128)(2,1)}, bf16[256,1152]{1,0:T(8,128)(2,1)S(1)}, u32[]{:S(2)}, u32[]{:S(2)}) collective-permute-start(bf16[256,1152]{1,0:T(8,128)(2,1)} %param.5), channel_id=1, source_target_pairs={{0,96},{32,0},{64,32},{96,64},{1,97},{33,1},{65,33},{97,65},{2,98}... | collective-permute-start | bytes 1769480 | tf_op jit(solution)/shard_map/ppermute | solution.py:12
  3.5 28.8 %collective-permute-start = (bf16[256,1152]{1,0:T(8,128)(2,1)}, bf16[256,1152]{1,0:T(8,128)(2,1)S(1)}, u32[]{:S(2)}, u32[]{:S(2)}) collective-permute-start(bf16[256,1152]{1,0:T(8,128)(2,1)} %param.5), channel_id=1, source_target_pairs={{0,32},{32,64},{64,96},{96,0},{1,33},{33,65},{65,97},{97,1},{2,34}... | collective-permute-start | bytes 1769480 | tf_op jit(solution)/shard_map/ppermute | solution.py:12
  3.5 17.8 %collective-permute-start.3 = (bf16[256,1152]{1,0:T(8,128)(2,1)}, bf16[256,1152]{1,0:T(8,128)(2,1)S(1)}, u32[]{:S(2)}, u32[]{:S(2)}) collective-permute-start(bf16[256,1152]{1,0:T(8,128)(2,1)} %param.5), channel_id=1, source_target_pairs={{0,16},{16,0},{1,17},{17,1},{2,18},{18,2},{3,19},{19,3},{4,20},{20... | collective-permute-start | bytes 1769480 | tf_op jit(solution)/shard_map/ppermute | solution.py:16
  5.4 29.9 %collective-permute-start.2 = (bf16[256,1152]{1,0:T(8,128)(2,1)}, bf16[256,1152]{1,0:T(8,128)(2,1)S(1)}, u32[]{:S(2)}, u32[]{:S(2)}) collective-permute-start(bf16[256,1152]{1,0:T(8,128)(2,1)} %param.5), channel_id=1, source_target_pairs={{0,64},{32,96},{64,0},{96,32},{1,65},{33,97},{65,1},{97,33},{2,66}... | collective-permute-start | bytes 1769480 | tf_op jit(solution)/shard_map/ppermute | solution.py:12
  7.7 12.9 %collective-permute-start.13 = (bf16[128,2048]{1,0:T(8,128)(2,1)}, bf16[128,2048]{1,0:T(8,128)(2,1)}, u32[]{:S(2)}, u32[]{:S(2)}) collective-permute-start(bf16[128,2048]{1,0:T(8,128)(2,1)} %param.3), channel_id=1, source_target_pairs={{0,2},{2,4},{4,6},{6,0},{1,3},{3,5},{5,7},{7,1},{8,10},{10,12},{12... | collective-permute-start | bytes 1572872 | tf_op jit(solution)/shard_map/ppermute | solution.py:12
  14.1 30.6 %copy-start.2 = (bf16[1024,2048]{1,0:T(8,128)(2,1)S(1)}, bf16[1024,2048]{1,0:T(8,128)(2,1)}, u32[]{:S(2)}) copy-start(bf16[1024,2048]{1,0:T(8,128)(2,1)} %constant_dynamic-update-slice_fusion.7) | copy-start | bytes 12582916
  20.5 22.8 %collective-permute-start.14 = (bf16[128,2048]{1,0:T(8,128)(2,1)S(1)}, bf16[128,2048]{1,0:T(8,128)(2,1)S(1)}, u32[]{:S(2)}, u32[]{:S(2)}) collective-permute-start(bf16[128,2048]{1,0:T(8,128)(2,1)S(1)} %copy-done.1), channel_id=1, source_target_pairs={{0,6},{2,0},{4,2},{6,4},{1,7},{3,1},{5,3},{7,5},{8,14},{10,8},{12,... | collective-permute-start | bytes 1572872 | tf_op jit(solution)/shard_map/ppermute | solution.py:12
  21.3 23.4 %collective-permute-start.16 = (bf16[128,2048]{1,0:T(8,128)(2,1)S(1)}, bf16[128,2048]{1,0:T(8,128)(2,1)S(1)}, u32[]{:S(2)}, u32[]{:S(2)}) collective-permute-start(bf16[128,2048]{1,0:T(8,128)(2,1)S(1)} %copy-done.1), channel_id=1, source_target_pairs={{0,8},{8,0},{1,9},{9,1},{2,10},{10,2},{3,11},{11,3},{4,12},{12,4},... | collective-permute-start | bytes 1572872 | tf_op jit(solution)/shard_map/ppermute | solution.py:16
  36.8 11.2 %collective-permute-start.4 = (bf16[256,1152]{1,0:T(8,128)(2,1)S(1)}, bf16[256,1152]{1,0:T(8,128)(2,1)S(1)}, u32[]{:S(2)}, u32[]{:S(2)}) collective-permute-start(bf16[256,1152]{1,0:T(8,128)(2,1)S(1)} %collective-permute-done.3), channel_id=1, source_target_pairs={{0,32},{32,64},{64,96},{96,0},{1,33},{33,65},{65,97},{97,1},{2,34}... | collective-permute-start | bytes 1769480 | tf_op jit(solution)/shard_map/ppermute | solution.py:12
  37.5 12.2 %collective-permute-start.5 = (bf16[256,1152]{1,0:T(8,128)(2,1)S(1)}, bf16[256,1152]{1,0:T(8,128)(2,1)S(1)}, u32[]{:S(2)}, u32[]{:S(2)}) collective-permute-start(bf16[256,1152]{1,0:T(8,128)(2,1)S(1)} %collective-permute-done.3), channel_id=1, source_target_pairs={{0,96},{32,0},{64,32},{96,64},{1,97},{33,1},{65,33},{97,65},{2,98}... | collective-permute-start | bytes 1769480 | tf_op jit(solution)/shard_map/ppermute | solution.py:12
  40.8 10.4 %collective-permute-start.6 = (bf16[256,1152]{1,0:T(8,128)(2,1)S(1)}, bf16[256,1152]{1,0:T(8,128)(2,1)S(1)}, u32[]{:S(2)}, u32[]{:S(2)}) collective-permute-start(bf16[256,1152]{1,0:T(8,128)(2,1)S(1)} %collective-permute-done.2), channel_id=1, source_target_pairs={{0,16},{16,0},{1,17},{17,1},{2,18},{18,2},{3,19},{19,3},{4,20},{20... | collective-permute-start | bytes 1769480 | tf_op jit(solution)/shard_map/ppermute | solution.py:16
  43.4 12.5 %collective-permute-start.15 = (bf16[128,2048]{1,0:T(8,128)(2,1)S(1)}, bf16[128,2048]{1,0:T(8,128)(2,1)S(1)}, u32[]{:S(2)}, u32[]{:S(2)}) collective-permute-start(bf16[128,2048]{1,0:T(8,128)(2,1)S(1)} %copy-done.1), channel_id=1, source_target_pairs={{0,4},{2,6},{4,0},{6,2},{1,5},{3,7},{5,1},{7,3},{8,12},{10,14},{12... | collective-permute-start | bytes 1572872 | tf_op jit(solution)/shard_map/ppermute | solution.py:12
  48.0 13.5 %collective-permute-start.18 = (bf16[128,2048]{1,0:T(8,128)(2,1)S(1)}, bf16[128,2048]{1,0:T(8,128)(2,1)S(1)}, u32[]{:S(2)}, u32[]{:S(2)}) collective-permute-start(bf16[128,2048]{1,0:T(8,128)(2,1)S(1)} %collective-permute-done.16), channel_id=1, source_target_pairs={{0,2},{2,4},{4,6},{6,0},{1,3},{3,5},{5,7},{7,1},{8,10},{10,12},{12... | collective-permute-start | bytes 1572872 | tf_op jit(solution)/shard_map/ppermute | solution.py:12
  51.9 26.8 %slice-start = ((s8[4718592]{0:T(1024)(128)(4,1)}), s8[4194304]{0:T(1024)(128)(4,1)S(1)}, s32[]{:S(2)}) async-start(s8[4718592]{0:T(1024)(128)(4,1)} %bitcast.112), calls=%async_computation | async-start | bytes 8388608
  52.7 26.0 %slice-start.1 = ((s8[4718592]{0:T(1024)(128)(4,1)}), s8[524288]{0:T(1024)(128)(4,1)S(1)}, s32[]{:S(2)}) async-start(s8[4718592]{0:T(1024)(128)(4,1)} %bitcast.112), calls=%async_computation.1 | async-start | bytes 1048576
  55.9 14.7 %collective-permute-start.17 = (bf16[128,2048]{1,0:T(8,128)(2,1)S(1)}, bf16[128,2048]{1,0:T(8,128)(2,1)S(1)}, u32[]{:S(2)}, u32[]{:S(2)}) collective-permute-start(bf16[128,2048]{1,0:T(8,128)(2,1)S(1)} %collective-permute-done.16), channel_id=1, source_target_pairs={{0,6},{2,0},{4,2},{6,4},{1,7},{3,1},{5,3},{7,5},{8,14},{10,8},{12,... | collective-permute-start | bytes 1572872 | tf_op jit(solution)/shard_map/ppermute | solution.py:12
  61.5 17.0 %collective-permute-start.19 = (bf16[128,2048]{1,0:T(8,128)(2,1)S(1)}, bf16[128,2048]{1,0:T(8,128)(2,1)S(1)}, u32[]{:S(2)}, u32[]{:S(2)}) collective-permute-start(bf16[128,2048]{1,0:T(8,128)(2,1)S(1)} %collective-permute-done.16), channel_id=1, source_target_pairs={{0,4},{2,6},{4,0},{6,2},{1,5},{3,7},{5,1},{7,3},{8,12},{10,14},{12... | collective-permute-start | bytes 1572872 | tf_op jit(solution)/shard_map/ppermute | solution.py:12
  78.6 26.5 %collective-permute-start.20 = (bf16[1024,2048]{1,0:T(8,128)(2,1)S(1)}, bf16[1024,2048]{1,0:T(8,128)(2,1)S(1)}, u32[]{:S(2)}, u32[]{:S(2)}) collective-permute-start(bf16[1024,2048]{1,0:T(8,128)(2,1)S(1)} %constant_dynamic-update-slice_fusion), channel_id=1, source_target_pairs={{0,1},{1,0},{2,3},{3,2},{4,5},{5,4},{6,7},{7,6},{8,9},{9,8},{10,11... | collective-permute-start | bytes 12582920 | tf_op jit(solution)/shard_map/ppermute | solution.py:16
  81.9 7.0 %collective-permute-start.7 = (bf16[1024,1024]{1,0:T(8,128)(2,1)S(1)}, bf16[1024,1024]{1,0:T(8,128)(2,1)S(1)}, u32[]{:S(2)}, u32[]{:S(2)}) collective-permute-start(bf16[1024,1024]{1,0:T(8,128)(2,1)S(1)} %fusion.12), channel_id=1, source_target_pairs={{0,1},{1,0},{2,3},{3,2},{4,5},{5,4},{6,7},{7,6},{8,9},{9,8},{10,11... | collective-permute-start | bytes 6291464 | tf_op jit(solution)/shard_map/ppermute | solution.py:16
  85.5 12.6 %collective-permute-start.11 = (bf16[1024,1024]{1,0:T(8,128)(2,1)S(1)}, bf16[1024,1024]{1,0:T(8,128)(2,1)S(1)}, u32[]{:S(2)}, u32[]{:S(2)}) collective-permute-start(bf16[1024,1024]{1,0:T(8,128)(2,1)S(1)} %fusion.15), channel_id=1, source_target_pairs={{0,1},{1,0},{2,3},{3,2},{4,5},{5,4},{6,7},{7,6},{8,9},{9,8},{10,11... | collective-permute-start | bytes 6291464 | tf_op jit(solution)/shard_map/ppermute | solution.py:16
  92.2 29.1 %collective-permute-start.10 = (bf16[2,128,1024]{2,1,0:T(8,128)(2,1)S(1)}, bf16[2,128,1024]{2,1,0:T(8,128)(2,1)S(1)}, u32[]{:S(2)}, u32[]{:S(2)}) collective-permute-start(bf16[2,128,1024]{2,1,0:T(8,128)(2,1)S(1)} %get-tuple-element.32), channel_id=1, source_target_pairs={{0,4},{2,6},{4,0},{6,2},{1,5},{3,7},{5,1},{7,3},{8,12},{10,14},{12... | collective-permute-start | bytes 1572872 | tf_op jit(solution)/shard_map/ppermute | solution.py:12
  94.9 26.4 %collective-permute-start.9 = (bf16[2,128,1024]{2,1,0:T(8,128)(2,1)S(1)}, bf16[2,128,1024]{2,1,0:T(8,128)(2,1)S(1)}, u32[]{:S(2)}, u32[]{:S(2)}) collective-permute-start(bf16[2,128,1024]{2,1,0:T(8,128)(2,1)S(1)} %get-tuple-element.33), channel_id=1, source_target_pairs={{0,6},{2,0},{4,2},{6,4},{1,7},{3,1},{5,3},{7,5},{8,14},{10,8},{12,... | collective-permute-start | bytes 1572872 | tf_op jit(solution)/shard_map/ppermute | solution.py:12
  94.9 26.4 %collective-permute-start.8 = (bf16[2,128,1024]{2,1,0:T(8,128)(2,1)S(1)}, bf16[2,128,1024]{2,1,0:T(8,128)(2,1)S(1)}, u32[]{:S(2)}, u32[]{:S(2)}) collective-permute-start(bf16[2,128,1024]{2,1,0:T(8,128)(2,1)S(1)} %get-tuple-element.34), channel_id=1, source_target_pairs={{0,2},{2,4},{4,6},{6,0},{1,3},{3,5},{5,7},{7,1},{8,10},{10,12},{12... | collective-permute-start | bytes 1572872 | tf_op jit(solution)/shard_map/ppermute | solution.py:12
  101.4 26.3 %collective-permute-start.12 = (bf16[4,128,1024]{2,1,0:T(8,128)(2,1)S(1)}, bf16[4,128,1024]{2,1,0:T(8,128)(2,1)S(1)}, u32[]{:S(2)}, u32[]{:S(2)}) collective-permute-start(bf16[4,128,1024]{2,1,0:T(8,128)(2,1)S(1)} %bitcast.95), channel_id=1, source_target_pairs={{0,8},{8,0},{1,9},{9,1},{2,10},{10,2},{3,11},{11,3},{4,12},{12,4},... | collective-permute-start | bytes 3145736 | tf_op jit(solution)/shard_map/ppermute | solution.py:16
  128.2 8.5 %collective-permute-start.21 = (bf16[128,1024]{1,0:T(8,128)(2,1)S(1)}, bf16[128,1024]{1,0:T(8,128)(2,1)S(1)}, u32[]{:S(2)}, u32[]{:S(2)}) collective-permute-start(bf16[128,1024]{1,0:T(8,128)(2,1)S(1)} %slice_bitcast_fusion.8), channel_id=1, source_target_pairs={{0,8},{8,0},{1,9},{9,1},{2,10},{10,2},{3,11},{11,3},{4,12},{12,4},... | collective-permute-start | bytes 786440 | tf_op jit(solution)/shard_map/ppermute | solution.py:16
  132.0 9.2 %collective-permute-start.22 = (bf16[1,128,1024]{2,1,0:T(8,128)(2,1)S(1)}, bf16[1,128,1024]{2,1,0:T(8,128)(2,1)S(1)}, u32[]{:S(2)}, u32[]{:S(2)}) collective-permute-start(bf16[1,128,1024]{2,1,0:T(8,128)(2,1)S(1)} %get-tuple-element.36), channel_id=1, source_target_pairs={{0,2},{2,4},{4,6},{6,0},{1,3},{3,5},{5,7},{7,1},{8,10},{10,12},{12... | collective-permute-start | bytes 786440 | tf_op jit(solution)/shard_map/ppermute | solution.py:12
  132.3 10.7 %collective-permute-start.24 = (bf16[1,128,1024]{2,1,0:T(8,128)(2,1)S(1)}, bf16[1,128,1024]{2,1,0:T(8,128)(2,1)S(1)}, u32[]{:S(2)}, u32[]{:S(2)}) collective-permute-start(bf16[1,128,1024]{2,1,0:T(8,128)(2,1)S(1)} %get-tuple-element.37), channel_id=1, source_target_pairs={{0,4},{2,6},{4,0},{6,2},{1,5},{3,7},{5,1},{7,3},{8,12},{10,14},{12... | collective-permute-start | bytes 786440 | tf_op jit(solution)/shard_map/ppermute | solution.py:12
  133.2 12.6 %collective-permute-start.23 = (bf16[1,128,1024]{2,1,0:T(8,128)(2,1)S(1)}, bf16[1,128,1024]{2,1,0:T(8,128)(2,1)S(1)}, u32[]{:S(2)}, u32[]{:S(2)}) collective-permute-start(bf16[1,128,1024]{2,1,0:T(8,128)(2,1)S(1)} %get-tuple-element.38), channel_id=1, source_target_pairs={{0,6},{2,0},{4,2},{6,4},{1,7},{3,1},{5,3},{7,5},{8,14},{10,8},{12,... | collective-permute-start | bytes 786440 | tf_op jit(solution)/shard_map/ppermute | solution.py:12

commit v2 on v0

v2 whole, which is shorter than its diff:
```python
import jax
import jax.numpy as jnp
from jax import lax
from jax.experimental import pallas as pl
from jax.experimental.pallas import tpu as pltpu
from jax.experimental.layout import Layout, with_layout_constraint
from jax.sharding import Mesh
from jax.sharding import PartitionSpec as P

AXES = ("x", "zl", "zh", "y", "core")
SIZES = (4, 2, 2, 4, 2)


def shift(value, axis, step):
    return lax.ppermute(value, axis, [(i, (i + step) % 4) for i in range(4)])


def swap(value, axis):
    return lax.ppermute(value, axis, [(0, 1), (1, 0)])


def after(value, *others):
    return lax.optimization_barrier((value, *others))[0]


def dot_nt(a, b):
    return lax.dot_general(a, b, (((1,), (1,)), ((), ())), preferred_element_type=jnp.float32)


def dot_tn(a, b):
    return lax.dot_general(a, b, (((0,), (0,)), ((), ())), preferred_element_type=jnp.float32)


def kernel_of(kernel, name, operands, shapes, waits=()):
    whole, anywhere = pl.BlockSpec(), pl.BlockSpec(memory_space=pl.ANY)
    n = len(operands)
    return pl.pallas_call(
        lambda *refs: kernel(*refs[:n], *refs[n + len(waits) :]),
        name=name,
        out_shape=[jax.ShapeDtypeStruct(shape, jnp.bfloat16) for shape in shapes],
        in_specs=[whole] * n + [anywhere] * len(waits),
        out_specs=[whole] * len(shapes),
        compiler_params=pltpu.CompilerParams(vmem_limit_bytes=16 * 2**20),
    )(*operands, *waits)


def place_grads(g0, g1, g2, g3, h0, h1, h2, h3, mine, theirs, *parts):
    x, zl, zh, y, core = (lax.axis_index(axis) for axis in AXES)
    for i, block in enumerate((g0, g1, g2, g3, h0, h1, h2, h3)):
        bx, bz = (x + i) & 3, zl ^ (i >> 2)
        dz, dy = zh ^ (bx >> 1), (((bx & 1) << 1) + bz - y) & 3
        first = block[pl.ds(pl.multiple_of(core * 128, 128), 128)]
        second = block[pl.ds(pl.multiple_of(128 - core * 128, 128), 128)]
        mine[dz * 4 + dy] = first
        theirs[dz * 4 + dy] = second
        for at in range(2):

            @pl.when(dz == at)
            def _():
                parts[at][dy] = first
                parts[2 + at][dy] = second


def sum_blocks(first, second, *outs):
    for i, out in enumerate(outs):
        out[...] = (first[i].astype(jnp.float32) + second[i].astype(jnp.float32)).astype(jnp.bfloat16)


def sum_four(q0, q1, q2, q3, *outs):
    for i, out in enumerate(outs):
        total = sum(q[i].astype(jnp.float32) for q in (q0, q1, q2, q3))
        out[...] = total.astype(jnp.bfloat16)


def sum_last(a0, a1, b0, b1, b2, b3, out):
    f32 = jnp.float32
    out[:, :1024] = (a0[...].astype(f32) + a1[...].astype(f32)).astype(jnp.bfloat16)
    total = b0[...].astype(f32) + b1[...].astype(f32) + b2[...].astype(f32) + b3[...].astype(f32)
    out[:, 1024:] = total.astype(jnp.bfloat16)


def relay(block, out):
    out[...] = block[...]


def pair(a, b, out):
    out[0] = a[...]
    out[1] = b[...]


def halves(behind, ahead, first, second):
    first[...] = behind[:, :64]
    second[...] = ahead[:, 64:]


def near_first(ab, ahead, behind, first, second, out):
    for dz in range(2):
        out[dz * 4] = ab[dz]
        out[dz * 4 + 1] = ahead[dz]
        out[dz * 4 + 2, :64] = first[dz]
        out[dz * 4 + 2, 64:] = second[dz]
        out[dz * 4 + 3] = behind[dz]


def cut(p, *outs):
    for i, out in enumerate(outs):
        out[...] = p[:, i]


def on_device(inputs, weight, out_grad):
    bf16, f32 = jnp.bfloat16, jnp.float32

    g, h = out_grad, swap(out_grad, "zl")
    g1, g3, g2 = shift(g, "x", 1), shift(g, "x", -1), shift(g, "x", 2)

    (ab,) = kernel_of(pair, "pair", (inputs, swap(inputs, "zh")), [(2, 128, 2048)])
    behind, ahead = shift(ab, "y", 1), shift(ab, "y", -1)
    first, second = kernel_of(halves, "halves", (behind, ahead), [(2, 64, 2048)] * 2)

    (h,) = kernel_of(relay, "relay", (h,), [(256, 1152)], (ab, g1, g3))
    h1, h3, h2 = shift(h, "x", 1), shift(h, "x", -1), swap(g2, "zl")
    blocks = [(8, 128, 1152)] * 2 + [(4, 128, 1152)] * 4
    grads = kernel_of(place_grads, "place_grads", (g, g3, g2, g1, h, h3, h2, h1), blocks, (first,))
    mine, theirs, mine_near, mine_far, theirs_near, theirs_far = (part.reshape(-1, 1152) for part in grads)

    wa, wb = weight[:1024], weight[1024:]

    def partial(rows, w, part):
        return (dot_nt(rows, w) + part.astype(f32)).astype(bf16).reshape(-1, 4, 128, 1024)

    tb1 = dot_nt(theirs_far, wb).astype(bf16)
    ta = dot_nt(after(theirs, tb1), wa).astype(bf16)
    pb1 = partial(mine_far, wb, swap(tb1, "core"))
    pa = partial(after(mine, pb1), wa, swap(ta, "core"))
    qb = swap(pb1[0], "zh")
    q0, q1, q2, q3 = kernel_of(cut, "cut", (pa,), [(2, 128, 1024)] * 4)
    q1, q3, q2 = shift(q1, "y", 1), shift(q3, "y", -1), shift(q2, "y", 2)
    tb0 = dot_nt(theirs_near, wb).astype(bf16)
    pb0 = partial(mine_near, wb, swap(tb0, "core"))

    first, second = shift(first, "y", 1), shift(second, "y", -1)
    waits = (q1, q2, q3, first, second)
    s0, s1, s2, s3 = kernel_of(sum_blocks, "sum_zh", (pb0[0], qb), [(128, 1024)] * 4, waits)
    r1, r3, r2 = shift(s1, "y", 1), shift(s3, "y", -1), shift(s2, "y", 2)
    a0, a1 = kernel_of(sum_four, "sum_y", (q0, q1, q2, q3), [(128, 1024)] * 2)
    a1 = swap(a1, "zh")

    (own,) = kernel_of(near_first, "near_first", (ab, ahead, behind, first, second), [(8, 128, 2048)], (s1, a1))
    own = own.reshape(1024, 2048)
    weight_grad = dot_tn(own, mine) + dot_tn(swap(own, "core"), theirs)
    weight_grad = with_layout_constraint(weight_grad, Layout((0, 1)))

    parts = (a0, a1, s0, r1, r3, r2)
    (input_grad,) = kernel_of(sum_last, "sum_last", parts, [(128, 2048)], (weight_grad,))
    return input_grad, weight_grad


def solution(mesh):
    fine = Mesh(mesh.devices.reshape(SIZES), AXES)
    row, col = ("x", "zl"), ("zh", "y", "core")
    return jax.shard_map(
        on_device,
        mesh=fine,
        in_specs=(P(col, row), P(row, col), P(row, col)),
        out_specs=(P(col, row), P(row, col)),
        check_vma=False,
    )
```

time: 300 us -> 131 us (0.44)
  the two profiles are of different devices: /device:TPU:24 before, /device:TPU:54 now
where the time goes in v2:
time: 131 us
  waiting for transfers between devices  64.4 us (49%)
  starting transfers between devices  32.8 us (25%)
  matrix products  24.2 us (18%)
  local copies, waits for them, and re-layouts  5.06 us (4%)
  Pallas kernels  3.28 us (3%)
    ppermute x15, waiting for transfers between devices, shift(): return lax.ppermute(value, axis, [(i, (i + step) % 4) for i in range(4)])  52.5 us
    ppermute x15, starting transfers between devices, shift(): return lax.ppermute(value, axis, [(i, (i + step) % 4) for i in range(4)])  20.8 us
    dot_general x6, matrix products, dot_nt(): lax.dot_general(a, b, (((1,), (1,)), ((), ())), preferred_element_type=jn...  12.5 us
    ppermute x9, starting transfers between devices, swap(): return lax.ppermute(value, axis, [(0, 1), (1, 0)])  12 us
    ppermute x9, waiting for transfers between devices, swap(): return lax.ppermute(value, axis, [(0, 1), (1, 0)])  11.9 us
    dot_general x2, matrix products, dot_tn(): lax.dot_general(a, b, (((0,), (0,)), ((), ())), preferred_element_type=jn...  11.7 us
    unnamed x8, local copies, waits for them, and re-layouts  5.06 us
    pallas_call x9, Pallas kernels, kernel_of(): pl.pallas_call(lambda *refs: kernel(*refs[:n], *refs[n + len(waits):]), n...  3.28 us
  transfers between devices with their start and end apart: 24, of which 11 were waited for; matrix products, arithmetic and copies ran while one was open for 15% of the time, Pallas kernels for 1%

profile of v2, /device:TPU:54, one launch (start us, length us, event | category | flops | bytes accessed | tf_op | source)
XLA Modules:
  0.0 130.6 jit_solution(9134474910690428378)
XLA Ops:
  0.6 0.9 collective-permute-start
  1.5 3.0 %collective-permute-start.4 = (bf16[128,2048]{1,0:T(8,128)(2,1)}, bf16[128,2048]{1,0:T(8,128)(2,1)S(1)}, u32[]{:S(2)}, u32[]{:S(2)}) collective-permute-start(bf16[128,2048]{1,0:T(8,128)(2,1)} %refs_0_.2), channel_id=1, source_target_pairs={{0,8},{8,0},{1,9},{9,1},{2,10},{10,2},{3,11},{11,3},{4,12},{12,4},... | collective-permute-start | bytes 1572872 | tf_op jit(solution)/shard_map/ppermute | solution.py:19
  4.5 2.4 %collective-permute-start.2 = (bf16[256,1152]{1,0:T(8,128)(2,1)}, bf16[256,1152]{1,0:T(8,128)(2,1)S(1)}, u32[]{:S(2)}, u32[]{:S(2)}) collective-permute-start(bf16[256,1152]{1,0:T(8,128)(2,1)} %refs_0_.3), channel_id=1, source_target_pairs={{0,32},{32,64},{64,96},{96,0},{1,33},{33,65},{65,97},{97,1},{2,34}... | collective-permute-start | bytes 1769480 | tf_op jit(solution)/shard_map/ppermute | solution.py:15
  6.9 1.0 collective-permute-start.3
  7.9 0.2 collective-permute-start.1
  8.1 10.0 %collective-permute-done.4.refs_1_ = bf16[128,2048]{1,0:T(8,128)(2,1)S(1)} collective-permute-done((bf16[128,2048]{1,0:T(8,128)(2,1)}, bf16[128,2048]{1,0:T(8,128)(2,1)S(1)}, u32[]{:S(2)}, u32[]{:S(2)}) %collective-permute-start.4) | collective-permute-done | bytes 524320 | tf_op jit(solution)/shard_map/ppermute | solution.py:19
  18.1 1.0 copy-done.2
  19.1 0.1 pair.1.refs_1_.refs_0_
  19.2 0.0 copy-start.1
  19.2 1.4 %collective-permute-start.8 = (bf16[2,128,2048]{2,1,0:T(8,128)(2,1)S(1)}, bf16[2,128,2048]{2,1,0:T(8,128)(2,1)S(1)}, u32[]{:S(2)}, u32[]{:S(2)}) collective-permute-start(bf16[2,128,2048]{2,1,0:T(8,128)(2,1)S(1)} %pair.1.refs_1_.refs_0_), channel_id=1, source_target_pairs={{0,2},{2,4},{4,6},{6,0},{1,3},{3,5},{5,7},{7,1},{8,10},{10,12},{12... | collective-permute-start | bytes 3145736 | tf_op jit(solution)/shard_map/ppermute | solution.py:15
  20.6 9.3 %collective-permute-done.refs_3_.refs_1_ = bf16[256,1152]{1,0:T(8,128)(2,1)S(1)} collective-permute-done((bf16[256,1152]{1,0:T(8,128)(2,1)}, bf16[256,1152]{1,0:T(8,128)(2,1)S(1)}, u32[]{:S(2)}, u32[]{:S(2)}) %collective-permute-start) | collective-permute-done | bytes 589856 | tf_op jit(solution)/shard_map/ppermute | solution.py:15
  29.8 0.5 collective-permute-start.9
  30.3 1.6 %collective-permute-done.2.refs_2_.refs_3_ = bf16[256,1152]{1,0:T(8,128)(2,1)S(1)} collective-permute-done((bf16[256,1152]{1,0:T(8,128)(2,1)}, bf16[256,1152]{1,0:T(8,128)(2,1)S(1)}, u32[]{:S(2)}, u32[]{:S(2)}) %collective-permute-start.2) | collective-permute-done | bytes 589856 | tf_op jit(solution)/shard_map/ppermute | solution.py:15
  31.9 0.0 collective-permute-done.3.refs_0_
  32.0 0.1 collective-permute-start.5
  32.1 1.1 collective-permute-start.6
  33.2 3.6 %collective-permute-start.7 = (bf16[256,1152]{1,0:T(8,128)(2,1)S(1)}, bf16[256,1152]{1,0:T(8,128)(2,1)S(1)}, u32[]{:S(2)}, u32[]{:S(2)}) collective-permute-start(bf16[256,1152]{1,0:T(8,128)(2,1)S(1)} %relay.1.refs_4_), channel_id=1, source_target_pairs={{0,32},{32,64},{64,96},{96,0},{1,33},{33,65},{65,97},{97,1},{2,34}... | collective-permute-start | bytes 1769480 | tf_op jit(solution)/shard_map/ppermute | solution.py:15
  36.7 4.8 %collective-permute-done.8.refs_0_.refs_2_ = bf16[2,128,2048]{2,1,0:T(8,128)(2,1)S(1)} collective-permute-done((bf16[2,128,2048]{2,1,0:T(8,128)(2,1)S(1)}, bf16[2,128,2048]{2,1,0:T(8,128)(2,1)S(1)}, u32[]{:S(2)}, u32[]{:S(2)}) %collective-permute-start.8) | collective-permute-done | bytes 1048608 | tf_op jit(solution)/shard_map/ppermute | solution.py:15
  41.5 12.3 %collective-permute-done.9.refs_1_ = bf16[2,128,2048]{2,1,0:T(8,128)(2,1)S(1)} collective-permute-done((bf16[2,128,2048]{2,1,0:T(8,128)(2,1)S(1)}, bf16[2,128,2048]{2,1,0:T(8,128)(2,1)S(1)}, u32[]{:S(2)}, u32[]{:S(2)}) %collective-permute-start.9) | collective-permute-done | bytes 1048608 | tf_op jit(solution)/shard_map/ppermute | solution.py:15
  53.9 0.1 halves.1
  53.9 0.0 collective-permute-done.5.refs_5_
  53.9 0.0 collective-permute-done.7.refs_7_
  54.0 0.0 copy-start.3
  54.0 1.0 place_grads.1
  55.0 1.3 %copy-done.3 = bf16[2048,1152]{1,0:T(8,128)(2,1)S(1)} copy-done((bf16[2048,1152]{1,0:T(8,128)(2,1)S(1)}, bf16[2048,1152]{1,0:T(8,128)(2,1)}, u32[]{:S(2)}) %copy-start.3) | copy-done | bytes 4718616
  56.3 1.5 %fusion.17 = bf16[512,1024]{1,0:T(8,128)(2,1)S(1)} fusion(bf16[512,1152]{1,0:T(8,128)(2,1)S(1)} %bitcast.31, bf16[2048,1152]{1,0:T(8,128)(2,1)S(1)} %copy-done.3), kind=kOutput, calls=%fused_computation.17 | convolution fusion | flops 1208483840 | bytes 4587520 | tf_op jit(solution)/shard_map/dot_general | solution.py:27
  57.9 3.1 %fusion.4 = bf16[1024,1024]{1,0:T(8,128)(2,1)S(1)} fusion(bf16[1024,1152]{1,0:T(8,128)(2,1)S(1)} %bitcast.25, bf16[2048,1152]{1,0:T(8,128)(2,1)S(1)} %copy-done.3), kind=kOutput, calls=%fused_computation.8 | convolution fusion | flops 2416967680 | bytes 6815744 | tf_op jit(solution)/shard_map/dot_general | solution.py:27
  61.0 0.1 collective-permute-start.10
  61.1 0.5 collective-permute-start.16
  61.6 1.5 %fusion.20 = bf16[512,1024]{1,0:T(8,128)(2,1)S(1)} fusion(bf16[512,1152]{1,0:T(8,128)(2,1)S(1)} %bitcast.30, bf16[2048,1152]{1,0:T(8,128)(2,1)S(1)} %copy-done.3), kind=kOutput, calls=%fused_computation.18 | convolution fusion | flops 1208483840 | bytes 4587520 | tf_op jit(solution)/shard_map/dot_general | solution.py:27
  63.2 0.2 collective-permute-start.15
  63.3 1.9 %collective-permute-done.10 = bf16[1024,1024]{1,0:T(8,128)(2,1)S(1)} collective-permute-done((bf16[1024,1024]{1,0:T(8,128)(2,1)S(1)}, bf16[1024,1024]{1,0:T(8,128)(2,1)S(1)}, u32[]{:S(2)}, u32[]{:S(2)}) %collective-permute-start.10) | collective-permute-done | bytes 2097184 | tf_op jit(solution)/shard_map/ppermute | solution.py:19
  65.3 3.1 %add_convert_fusion = bf16[1024,1024]{1,0:T(8,128)(2,1)S(1)} fusion(bf16[1024,1024]{1,0:T(8,128)(2,1)S(1)} %collective-permute-done.10, bf16[1024,1152]{1,0:T(8,128)(2,1)S(1)} %bitcast.27, bf16[2048,1152]{1,0:T(8,128)(2,1)S(1)} %copy-done.3), kind=kOutput, calls=%fused_computation.1 | convolution fusion | flops 2419064832 | bytes 8912896 | tf_op jit(solution)/shard_map/dot_general | solution.py:27
  68.4 0.1 cut.1
  68.5 2.6 %collective-permute-start.11 = (bf16[2,128,1024]{2,1,0:T(8,128)(2,1)S(1)}, bf16[2,128,1024]{2,1,0:T(8,128)(2,1)S(1)}, u32[]{:S(2)}, u32[]{:S(2)}) collective-permute-start(bf16[2,128,1024]{2,1,0:T(8,128)(2,1)S(1)} %get-tuple-element.27), channel_id=1, source_target_pairs={{0,2},{2,4},{4,6},{6,0},{1,3},{3,5},{5,7},{7,1},{8,10},{10,12},{12... | collective-permute-start | bytes 1572872 | tf_op jit(solution)/shard_map/ppermute | solution.py:15
  71.1 0.0 collective-permute-start.12
  71.1 0.0 collective-permute-done.16
  71.1 1.6 %add_convert_fusion.1 = bf16[512,1024]{1,0:T(8,128)(2,1)S(1)} fusion(bf16[512,1024]{1,0:T(8,128)(2,1)S(1)} %collective-permute-done.16, bf16[512,1152]{1,0:T(8,128)(2,1)S(1)} %bitcast.29, bf16[2048,1152]{1,0:T(8,128)(2,1)S(1)} %copy-done.3), kind=kOutput, calls=%fused_computation.2 | convolution fusion | flops 1209532416 | bytes 5636096 | tf_op jit(solution)/shard_map/dot_general | solution.py:27
  72.7 3.1 %collective-permute-start.17 = (bf16[4,128,1024]{2,1,0:T(8,128)(2,1)S(1)}, bf16[4,128,1024]{2,1,0:T(8,128)(2,1)S(1)}, u32[]{:S(2)}, u32[]{:S(2)}) collective-permute-start(bf16[4,128,1024]{2,1,0:T(8,128)(2,1)S(1)} %bitcast.32), channel_id=1, source_target_pairs={{0,8},{8,0},{1,9},{9,1},{2,10},{10,2},{3,11},{11,3},{4,12},{12,4},... | collective-permute-start | bytes 3145736 | tf_op jit(solution)/shard_map/ppermute | solution.py:19
  75.7 1.6 %collective-permute-start.13 = (bf16[2,128,1024]{2,1,0:T(8,128)(2,1)S(1)}, bf16[2,128,1024]{2,1,0:T(8,128)(2,1)S(1)}, u32[]{:S(2)}, u32[]{:S(2)}) collective-permute-start(bf16[2,128,1024]{2,1,0:T(8,128)(2,1)S(1)} %get-tuple-element.29), channel_id=1, source_target_pairs={{0,6},{2,0},{4,2},{6,4},{1,7},{3,1},{5,3},{7,5},{8,14},{10,8},{12,... | collective-permute-start | bytes 1572872 | tf_op jit(solution)/shard_map/ppermute | solution.py:15
  77.3 15.8 %collective-permute-done.11.refs_1_.refs_2_ = bf16[2,128,1024]{2,1,0:T(8,128)(2,1)S(1)} collective-permute-done((bf16[2,128,1024]{2,1,0:T(8,128)(2,1)S(1)}, bf16[2,128,1024]{2,1,0:T(8,128)(2,1)S(1)}, u32[]{:S(2)}, u32[]{:S(2)}) %collective-permute-start.11) | collective-permute-done | bytes 524320 | tf_op jit(solution)/shard_map/ppermute | solution.py:15
  93.1 0.0 collective-permute-start.18
  93.1 1.6 %collective-permute-done.12.refs_2_.refs_3_ = bf16[2,128,1024]{2,1,0:T(8,128)(2,1)S(1)} collective-permute-done((bf16[2,128,1024]{2,1,0:T(8,128)(2,1)S(1)}, bf16[2,128,1024]{2,1,0:T(8,128)(2,1)S(1)}, u32[]{:S(2)}, u32[]{:S(2)}) %collective-permute-start.12) | collective-permute-done | bytes 524320 | tf_op jit(solution)/shard_map/ppermute | solution.py:15
  94.7 0.4 collective-permute-start.19
  95.1 0.6 collective-permute-done.13.refs_3_.refs_4_
  95.6 0.3 sum_y.1
  95.9 3.1 %collective-permute-start.14 = (bf16[128,1024]{1,0:T(8,128)(2,1)S(1)}, bf16[128,1024]{1,0:T(8,128)(2,1)S(1)}, u32[]{:S(2)}, u32[]{:S(2)}) collective-permute-start(bf16[128,1024]{1,0:T(8,128)(2,1)S(1)} %get-tuple-element.31), channel_id=1, source_target_pairs={{0,8},{8,0},{1,9},{9,1},{2,10},{10,2},{3,11},{11,3},{4,12},{12,4},... | collective-permute-start | bytes 786440 | tf_op jit(solution)/shard_map/ppermute | solution.py:19
  99.0 0.0 collective-permute-done.15
  99.0 1.6 %add_convert_fusion.2 = bf16[512,1024]{1,0:T(8,128)(2,1)S(1)} fusion(bf16[512,1024]{1,0:T(8,128)(2,1)S(1)} %collective-permute-done.15, bf16[512,1152]{1,0:T(8,128)(2,1)S(1)} %bitcast.28, bf16[2048,1152]{1,0:T(8,128)(2,1)S(1)} %copy-done.3), kind=kOutput, calls=%fused_computation.3 | convolution fusion | flops 1209532416 | bytes 5636096 | tf_op jit(solution)/shard_map/dot_general | solution.py:27
  100.5 4.6 %collective-permute-done.18.refs_5_.refs_3_ = bf16[2,64,2048]{2,1,0:T(8,128)(2,1)S(1)} collective-permute-done((bf16[2,64,2048]{2,1,0:T(8,128)(2,1)S(1)}, bf16[2,64,2048]{2,1,0:T(8,128)(2,1)S(1)}, u32[]{:S(2)}, u32[]{:S(2)}) %collective-permute-start.18) | collective-permute-done | bytes 524320 | tf_op jit(solution)/shard_map/ppermute | solution.py:15
  105.1 1.9 %collective-permute-done.19.refs_6_.refs_4_ = bf16[2,64,2048]{2,1,0:T(8,128)(2,1)S(1)} collective-permute-done((bf16[2,64,2048]{2,1,0:T(8,128)(2,1)S(1)}, bf16[2,64,2048]{2,1,0:T(8,128)(2,1)S(1)}, u32[]{:S(2)}, u32[]{:S(2)}) %collective-permute-start.19) | collective-permute-done | bytes 524320 | tf_op jit(solution)/shard_map/ppermute | solution.py:15
  107.0 0.0 collective-permute-done.17.refs_1_
  107.0 0.2 sum_zh.1
  107.2 0.0 collective-permute-done.14.refs_6_.refs_1_
  107.3 0.3 near_first.1
  107.5 0.1 collective-permute-start.23
  107.6 3.5 %collective-permute-start.20 = (bf16[128,1024]{1,0:T(8,128)(2,1)S(1)}, bf16[128,1024]{1,0:T(8,128)(2,1)S(1)}, u32[]{:S(2)}, u32[]{:S(2)}) collective-permute-start(bf16[128,1024]{1,0:T(8,128)(2,1)S(1)} %get-tuple-element.37.refs_5_), channel_id=1, source_target_pairs={{0,2},{2,4},{4,6},{6,0},{1,3},{3,5},{5,7},{7,1},{8,10},{10,12},{12... | collective-permute-start | bytes 786440 | tf_op jit(solution)/shard_map/ppermute | solution.py:15
  111.1 3.8 %collective-permute-start.22 = (bf16[128,1024]{1,0:T(8,128)(2,1)S(1)}, bf16[128,1024]{1,0:T(8,128)(2,1)S(1)}, u32[]{:S(2)}, u32[]{:S(2)}) collective-permute-start(bf16[128,1024]{1,0:T(8,128)(2,1)S(1)} %get-tuple-element.39), channel_id=1, source_target_pairs={{0,4},{2,6},{4,0},{6,2},{1,5},{3,7},{5,1},{7,3},{8,12},{10,14},{12... | collective-permute-start | bytes 786440 | tf_op jit(solution)/shard_map/ppermute | solution.py:15
  114.9 5.9 %fusion.27 = f32[2048,1152,1]{1,0,2:T(8,128)S(1)} fusion(bf16[8,128,2048]{2,1,0:T(8,128)(2,1)S(1)} %near_first.1, bf16[8,128,1152]{2,1,0:T(8,128)(2,1)S(1)} %get-tuple-element.22), kind=kOutput, calls=%fused_computation.19 | convolution fusion | flops 4831838208 | bytes 15990784 | tf_op jit(solution)/shard_map/dot_general | solution.py:31
  120.9 5.8 %bitcast_add_fusion.refs_6_ = f32[2048,1152]{1,0:T(8,128)S(1)} fusion(f32[2048,1152,1]{1,0,2:T(8,128)S(1)} %fusion.27, bf16[1024,2048]{1,0:T(8,128)(2,1)S(1)} %collective-permute-done.23, bf16[1024,1152]{1,0:T(8,128)(2,1)S(1)} %bitcast.26), kind=kOutput, calls=%fused_computation | convolution fusion | flops 4834197504 | bytes 25427968 | tf_op jit(solution)/shard_map/dot_general | solution.py:31
  126.7 0.0 copy-start
  126.7 0.0 collective-permute-done.22.refs_5_
  126.7 1.2 sum_last.1
  127.9 2.7 %copy-done = f32[2048,1152]{1,0:T(8,128)} copy-done((f32[2048,1152]{1,0:T(8,128)}, f32[2048,1152]{1,0:T(8,128)S(1)}, u32[]{:S(2)}) %copy-start) | copy-done | bytes 9437208
  (9 shorter events, 0.1 us)
Async XLA Ops:
  0.6 29.2 %collective-permute-start = (bf16[256,1152]{1,0:T(8,128)(2,1)}, bf16[256,1152]{1,0:T(8,128)(2,1)S(1)}, u32[]{:S(2)}, u32[]{:S(2)}) collective-permute-start(bf16[256,1152]{1,0:T(8,128)(2,1)} %refs_0_.3), channel_id=1, source_target_pairs={{0,96},{32,0},{64,32},{96,64},{1,97},{33,1},{65,33},{97,65},{2,98}... | collective-permute-start | bytes 1769480 | tf_op jit(solution)/shard_map/ppermute | solution.py:15
  1.5 16.6 %collective-permute-start.4 = (bf16[128,2048]{1,0:T(8,128)(2,1)}, bf16[128,2048]{1,0:T(8,128)(2,1)S(1)}, u32[]{:S(2)}, u32[]{:S(2)}) collective-permute-start(bf16[128,2048]{1,0:T(8,128)(2,1)} %refs_0_.2), channel_id=1, source_target_pairs={{0,8},{8,0},{1,9},{9,1},{2,10},{10,2},{3,11},{11,3},{4,12},{12,4},... | collective-permute-start | bytes 1572872 | tf_op jit(solution)/shard_map/ppermute | solution.py:19
  4.5 27.4 %collective-permute-start.2 = (bf16[256,1152]{1,0:T(8,128)(2,1)}, bf16[256,1152]{1,0:T(8,128)(2,1)S(1)}, u32[]{:S(2)}, u32[]{:S(2)}) collective-permute-start(bf16[256,1152]{1,0:T(8,128)(2,1)} %refs_0_.3), channel_id=1, source_target_pairs={{0,32},{32,64},{64,96},{96,0},{1,33},{33,65},{65,97},{97,1},{2,34}... | collective-permute-start | bytes 1769480 | tf_op jit(solution)/shard_map/ppermute | solution.py:15
  6.9 25.0 %collective-permute-start.3 = (bf16[256,1152]{1,0:T(8,128)(2,1)}, bf16[256,1152]{1,0:T(8,128)(2,1)S(1)}, u32[]{:S(2)}, u32[]{:S(2)}) collective-permute-start(bf16[256,1152]{1,0:T(8,128)(2,1)} %refs_0_.3), channel_id=1, source_target_pairs={{0,16},{16,0},{1,17},{17,1},{2,18},{18,2},{3,19},{19,3},{4,20},{20... | collective-permute-start | bytes 1769480 | tf_op jit(solution)/shard_map/ppermute | solution.py:19
  7.9 24.1 %collective-permute-start.1 = (bf16[256,1152]{1,0:T(8,128)(2,1)}, bf16[256,1152]{1,0:T(8,128)(2,1)S(1)}, u32[]{:S(2)}, u32[]{:S(2)}) collective-permute-start(bf16[256,1152]{1,0:T(8,128)(2,1)} %refs_0_.3), channel_id=1, source_target_pairs={{0,64},{32,96},{64,0},{96,32},{1,65},{33,97},{65,1},{97,33},{2,66}... | collective-permute-start | bytes 1769480 | tf_op jit(solution)/shard_map/ppermute | solution.py:15
  18.1 1.0 copy-start.2
  19.2 34.8 %copy-start.1 = (bf16[256,1152]{1,0:T(8,128)(2,1)S(1)}, bf16[256,1152]{1,0:T(8,128)(2,1)}, u32[]{:S(2)}) copy-start(bf16[256,1152]{1,0:T(8,128)(2,1)} %refs_0_.3) | copy-start | bytes 1769476
  19.2 22.3 %collective-permute-start.8 = (bf16[2,128,2048]{2,1,0:T(8,128)(2,1)S(1)}, bf16[2,128,2048]{2,1,0:T(8,128)(2,1)S(1)}, u32[]{:S(2)}, u32[]{:S(2)}) collective-permute-start(bf16[2,128,2048]{2,1,0:T(8,128)(2,1)S(1)} %pair.1.refs_1_.refs_0_), channel_id=1, source_target_pairs={{0,2},{2,4},{4,6},{6,0},{1,3},{3,5},{5,7},{7,1},{8,10},{10,12},{12... | collective-permute-start | bytes 3145736 | tf_op jit(solution)/shard_map/ppermute | solution.py:15
  29.8 24.0 %collective-permute-start.9 = (bf16[2,128,2048]{2,1,0:T(8,128)(2,1)S(1)}, bf16[2,128,2048]{2,1,0:T(8,128)(2,1)S(1)}, u32[]{:S(2)}, u32[]{:S(2)}) collective-permute-start(bf16[2,128,2048]{2,1,0:T(8,128)(2,1)S(1)} %pair.1.refs_1_.refs_0_), channel_id=1, source_target_pairs={{0,6},{2,0},{4,2},{6,4},{1,7},{3,1},{5,3},{7,5},{8,14},{10,8},{12,... | collective-permute-start | bytes 3145736 | tf_op jit(solution)/shard_map/ppermute | solution.py:15
  32.0 22.0 %collective-permute-start.5 = (bf16[256,1152]{1,0:T(8,128)(2,1)S(1)}, bf16[256,1152]{1,0:T(8,128)(2,1)S(1)}, u32[]{:S(2)}, u32[]{:S(2)}) collective-permute-start(bf16[256,1152]{1,0:T(8,128)(2,1)S(1)} %relay.1.refs_4_), channel_id=1, source_target_pairs={{0,96},{32,0},{64,32},{96,64},{1,97},{33,1},{65,33},{97,65},{2,98}... | collective-permute-start | bytes 1769480 | tf_op jit(solution)/shard_map/ppermute | solution.py:15
  32.1 21.9 %collective-permute-start.6 = (bf16[256,1152]{1,0:T(8,128)(2,1)S(1)}, bf16[256,1152]{1,0:T(8,128)(2,1)S(1)}, u32[]{:S(2)}, u32[]{:S(2)}) collective-permute-start(bf16[256,1152]{1,0:T(8,128)(2,1)S(1)} %collective-permute-done.1.refs_2_), channel_id=1, source_target_pairs={{0,16},{16,0},{1,17},{17,1},{2,18},{18,2},{3,19},{19,3},{4,20},{20... | collective-permute-start | bytes 1769480 | tf_op jit(solution)/shard_map/ppermute | solution.py:19
  33.2 20.8 %collective-permute-start.7 = (bf16[256,1152]{1,0:T(8,128)(2,1)S(1)}, bf16[256,1152]{1,0:T(8,128)(2,1)S(1)}, u32[]{:S(2)}, u32[]{:S(2)}) collective-permute-start(bf16[256,1152]{1,0:T(8,128)(2,1)S(1)} %relay.1.refs_4_), channel_id=1, source_target_pairs={{0,32},{32,64},{64,96},{96,0},{1,33},{33,65},{65,97},{97,1},{2,34}... | collective-permute-start | bytes 1769480 | tf_op jit(solution)/shard_map/ppermute | solution.py:15
  54.0 2.3 %copy-start.3 = (bf16[2048,1152]{1,0:T(8,128)(2,1)S(1)}, bf16[2048,1152]{1,0:T(8,128)(2,1)}, u32[]{:S(2)}) copy-start(bf16[2048,1152]{1,0:T(8,128)(2,1)} %param.4) | copy-start | bytes 14155780
  61.0 4.2 %collective-permute-start.10 = (bf16[1024,1024]{1,0:T(8,128)(2,1)S(1)}, bf16[1024,1024]{1,0:T(8,128)(2,1)S(1)}, u32[]{:S(2)}, u32[]{:S(2)}) collective-permute-start(bf16[1024,1024]{1,0:T(8,128)(2,1)S(1)} %fusion.4), channel_id=1, source_target_pairs={{0,1},{1,0},{2,3},{3,2},{4,5},{5,4},{6,7},{7,6},{8,9},{9,8},{10,11... | collective-permute-start | bytes 6291464 | tf_op jit(solution)/shard_map/ppermute | solution.py:19
  61.1 10.0 %collective-permute-start.16 = (bf16[512,1024]{1,0:T(8,128)(2,1)S(1)}, bf16[512,1024]{1,0:T(8,128)(2,1)S(1)}, u32[]{:S(2)}, u32[]{:S(2)}) collective-permute-start(bf16[512,1024]{1,0:T(8,128)(2,1)S(1)} %fusion.17), channel_id=1, source_target_pairs={{0,1},{1,0},{2,3},{3,2},{4,5},{5,4},{6,7},{7,6},{8,9},{9,8},{10,11... | collective-permute-start | bytes 3145736 | tf_op jit(solution)/shard_map/ppermute | solution.py:19
  63.2 35.8 %collective-permute-start.15 = (bf16[512,1024]{1,0:T(8,128)(2,1)S(1)}, bf16[512,1024]{1,0:T(8,128)(2,1)S(1)}, u32[]{:S(2)}, u32[]{:S(2)}) collective-permute-start(bf16[512,1024]{1,0:T(8,128)(2,1)S(1)} %fusion.20), channel_id=1, source_target_pairs={{0,1},{1,0},{2,3},{3,2},{4,5},{5,4},{6,7},{7,6},{8,9},{9,8},{10,11... | collective-permute-start | bytes 3145736 | tf_op jit(solution)/shard_map/ppermute | solution.py:19
  68.5 24.5 %collective-permute-start.11 = (bf16[2,128,1024]{2,1,0:T(8,128)(2,1)S(1)}, bf16[2,128,1024]{2,1,0:T(8,128)(2,1)S(1)}, u32[]{:S(2)}, u32[]{:S(2)}) collective-permute-start(bf16[2,128,1024]{2,1,0:T(8,128)(2,1)S(1)} %get-tuple-element.27), channel_id=1, source_target_pairs={{0,2},{2,4},{4,6},{6,0},{1,3},{3,5},{5,7},{7,1},{8,10},{10,12},{12... | collective-permute-start | bytes 1572872 | tf_op jit(solution)/shard_map/ppermute | solution.py:15
  71.1 23.6 %collective-permute-start.12 = (bf16[2,128,1024]{2,1,0:T(8,128)(2,1)S(1)}, bf16[2,128,1024]{2,1,0:T(8,128)(2,1)S(1)}, u32[]{:S(2)}, u32[]{:S(2)}) collective-permute-start(bf16[2,128,1024]{2,1,0:T(8,128)(2,1)S(1)} %get-tuple-element.28), channel_id=1, source_target_pairs={{0,4},{2,6},{4,0},{6,2},{1,5},{3,7},{5,1},{7,3},{8,12},{10,14},{12... | collective-permute-start | bytes 1572872 | tf_op jit(solution)/shard_map/ppermute | solution.py:15
  72.7 34.3 %collective-permute-start.17 = (bf16[4,128,1024]{2,1,0:T(8,128)(2,1)S(1)}, bf16[4,128,1024]{2,1,0:T(8,128)(2,1)S(1)}, u32[]{:S(2)}, u32[]{:S(2)}) collective-permute-start(bf16[4,128,1024]{2,1,0:T(8,128)(2,1)S(1)} %bitcast.32), channel_id=1, source_target_pairs={{0,8},{8,0},{1,9},{9,1},{2,10},{10,2},{3,11},{11,3},{4,12},{12,4},... | collective-permute-start | bytes 3145736 | tf_op jit(solution)/shard_map/ppermute | solution.py:19
  75.7 19.9 %collective-permute-start.13 = (bf16[2,128,1024]{2,1,0:T(8,128)(2,1)S(1)}, bf16[2,128,1024]{2,1,0:T(8,128)(2,1)S(1)}, u32[]{:S(2)}, u32[]{:S(2)}) collective-permute-start(bf16[2,128,1024]{2,1,0:T(8,128)(2,1)S(1)} %get-tuple-element.29), channel_id=1, source_target_pairs={{0,6},{2,0},{4,2},{6,4},{1,7},{3,1},{5,3},{7,5},{8,14},{10,8},{12,... | collective-permute-start | bytes 1572872 | tf_op jit(solution)/shard_map/ppermute | solution.py:15
  93.1 12.0 %collective-permute-start.18 = (bf16[2,64,2048]{2,1,0:T(8,128)(2,1)S(1)}, bf16[2,64,2048]{2,1,0:T(8,128)(2,1)S(1)}, u32[]{:S(2)}, u32[]{:S(2)}) collective-permute-start(bf16[2,64,2048]{2,1,0:T(8,128)(2,1)S(1)} %get-tuple-element.21.refs_8_), channel_id=1, source_target_pairs={{0,2},{2,4},{4,6},{6,0},{1,3},{3,5},{5,7},{7,1},{8,10},{10,12},{12... | collective-permute-start | bytes 1572872 | tf_op jit(solution)/shard_map/ppermute | solution.py:15
  94.7 12.3 %collective-permute-start.19 = (bf16[2,64,2048]{2,1,0:T(8,128)(2,1)S(1)}, bf16[2,64,2048]{2,1,0:T(8,128)(2,1)S(1)}, u32[]{:S(2)}, u32[]{:S(2)}) collective-permute-start(bf16[2,64,2048]{2,1,0:T(8,128)(2,1)S(1)} %get-tuple-element.35), channel_id=1, source_target_pairs={{0,6},{2,0},{4,2},{6,4},{1,7},{3,1},{5,3},{7,5},{8,14},{10,8},{12,... | collective-permute-start | bytes 1572872 | tf_op jit(solution)/shard_map/ppermute | solution.py:15
  95.9 11.3 %collective-permute-start.14 = (bf16[128,1024]{1,0:T(8,128)(2,1)S(1)}, bf16[128,1024]{1,0:T(8,128)(2,1)S(1)}, u32[]{:S(2)}, u32[]{:S(2)}) collective-permute-start(bf16[128,1024]{1,0:T(8,128)(2,1)S(1)} %get-tuple-element.31), channel_id=1, source_target_pairs={{0,8},{8,0},{1,9},{9,1},{2,10},{10,2},{3,11},{11,3},{4,12},{12,4},... | collective-permute-start | bytes 786440 | tf_op jit(solution)/shard_map/ppermute | solution.py:19
  107.5 13.3 %collective-permute-start.23 = (bf16[1024,2048]{1,0:T(8,128)(2,1)S(1)}, bf16[1024,2048]{1,0:T(8,128)(2,1)S(1)}, u32[]{:S(2)}, u32[]{:S(2)}) collective-permute-start(bf16[1024,2048]{1,0:T(8,128)(2,1)S(1)} %bitcast.22), channel_id=1, source_target_pairs={{0,1},{1,0},{2,3},{3,2},{4,5},{5,4},{6,7},{7,6},{8,9},{9,8},{10,11... | collective-permute-start | bytes 12582920 | tf_op jit(solution)/shard_map/ppermute | solution.py:19
  107.6 19.1 %collective-permute-start.20 = (bf16[128,1024]{1,0:T(8,128)(2,1)S(1)}, bf16[128,1024]{1,0:T(8,128)(2,1)S(1)}, u32[]{:S(2)}, u32[]{:S(2)}) collective-permute-start(bf16[128,1024]{1,0:T(8,128)(2,1)S(1)} %get-tuple-element.37.refs_5_), channel_id=1, source_target_pairs={{0,2},{2,4},{4,6},{6,0},{1,3},{3,5},{5,7},{7,1},{8,10},{10,12},{12... | collective-permute-start | bytes 786440 | tf_op jit(solution)/shard_map/ppermute | solution.py:15
  111.1 15.6 %collective-permute-start.21 = (bf16[128,1024]{1,0:T(8,128)(2,1)S(1)}, bf16[128,1024]{1,0:T(8,128)(2,1)S(1)}, u32[]{:S(2)}, u32[]{:S(2)}) collective-permute-start(bf16[128,1024]{1,0:T(8,128)(2,1)S(1)} %get-tuple-element.38), channel_id=1, source_target_pairs={{0,6},{2,0},{4,2},{6,4},{1,7},{3,1},{5,3},{7,5},{8,14},{10,8},{12,... | collective-permute-start | bytes 786440 | tf_op jit(solution)/shard_map/ppermute | solution.py:15
  111.1 15.6 %collective-permute-start.22 = (bf16[128,1024]{1,0:T(8,128)(2,1)S(1)}, bf16[128,1024]{1,0:T(8,128)(2,1)S(1)}, u32[]{:S(2)}, u32[]{:S(2)}) collective-permute-start(bf16[128,1024]{1,0:T(8,128)(2,1)S(1)} %get-tuple-element.39), channel_id=1, source_target_pairs={{0,4},{2,6},{4,0},{6,2},{1,5},{3,7},{5,1},{7,3},{8,12},{10,14},{12... | collective-permute-start | bytes 786440 | tf_op jit(solution)/shard_map/ppermute | solution.py:15
  126.7 3.9 %copy-start = (f32[2048,1152]{1,0:T(8,128)}, f32[2048,1152]{1,0:T(8,128)S(1)}, u32[]{:S(2)}) copy-start(f32[2048,1152]{1,0:T(8,128)S(1)} %bitcast_add_fusion.refs_6_) | copy-start | bytes 28311556

commit v3 on v2

--- a/solution.py
+++ b/solution.py
@@ -44,21 +44,60 @@
     )(*operands, *waits)
 
 
-def place_grads(g0, g1, g2, g3, h0, h1, h2, h3, mine, theirs, *parts):
-    x, zl, zh, y, core = (lax.axis_index(axis) for axis in AXES)
-    for i, block in enumerate((g0, g1, g2, g3, h0, h1, h2, h3)):
-        bx, bz = (x + i) & 3, zl ^ (i >> 2)
-        dz, dy = zh ^ (bx >> 1), (((bx & 1) << 1) + bz - y) & 3
-        first = block[pl.ds(pl.multiple_of(core * 128, 128), 128)]
-        second = block[pl.ds(pl.multiple_of(128 - core * 128, 128), 128)]
-        mine[dz * 4 + dy] = first
-        theirs[dz * 4 + dy] = second
-        for at in range(2):
-
-            @pl.when(dz == at)
+def distance(dx, dz):
+    x, zl, zh, y = (lax.axis_index(axis) for axis in AXES[:4])
+    bx, bz = (x + dx) & 3, zl ^ dz
+    return zh ^ (bx >> 1), (((bx & 1) << 1) + bz - y) & 3
+
+
+def by_core(*refs):
+    core = lax.axis_index("core")
+    for i, block in enumerate(refs[:4]):
+        refs[4][i] = block[pl.ds(pl.multiple_of(core * 128, 128), 128)]
+        refs[5][i] = block[pl.ds(pl.multiple_of(128 - core * 128, 128), 128)]
+
+
+def place_grads(early_mine, early_theirs, late_mine, late_theirs, mine, theirs, mine_opposite, theirs_opposite):
+    for late, part, other in ((0, early_mine, early_theirs), (1, late_mine, late_theirs)):
+        for i in range(4):
+            dz, dy = distance(i, late)
+
+            @pl.when(dy == 2)
             def _():
-                parts[at][dy] = first
-                parts[2 + at][dy] = second
+                mine_opposite[dz] = part[i]
+                theirs_opposite[dz] = other[i]
+
+            @pl.when(dy != 2)
+            def _():
+                mine[dz * 3 + dy - (dy >> 1)] = part[i]
+                theirs[dz * 3 + dy - (dy >> 1)] = other[i]
+
+
+def cut_a(early, late, first, second, q0, q1, q2, q3):
+    for is_late, part in ((0, early), (1, late)):
+        for i in range(4):
+            dz, dy = distance(i, is_late)
+            for at, out in enumerate((q0, q1, q2, q3)):
+
+                @pl.when(dy == at)
+                def _():
+                    out[dz] = part[i, :, :1024]
+
+    for out, half in ((q1, first), (q3, second)):
+        for dz in range(2):
+            out[2 + dz, :64] = half[dz, :, :1024]
+            out[2 + dz, 64:] = half[dz, :, 1024:]
+
+
+def cut_b(early, late, near, far):
+    for is_late, part, columns in ((0, early, slice(1024, 2048)), (1, late, slice(0, 1024))):
+        for i in range(4):
+            dz, dy = distance(i, is_late)
+            for at, out in enumerate((near, far)):
+
+                @pl.when(dz == at)
+                def _():
+                    out[dy] = part[i, :, columns]
 
 
 def sum_blocks(first, second, *outs):
@@ -93,61 +132,79 @@
     second[...] = ahead[:, 64:]
 
 
-def near_first(ab, ahead, behind, first, second, out):
+def near_first(ab, ahead, behind, out):
     for dz in range(2):
-        out[dz * 4] = ab[dz]
-        out[dz * 4 + 1] = ahead[dz]
-        out[dz * 4 + 2, :64] = first[dz]
-        out[dz * 4 + 2, 64:] = second[dz]
-        out[dz * 4 + 3] = behind[dz]
-
-
-def cut(p, *outs):
-    for i, out in enumerate(outs):
-        out[...] = p[:, i]
+        for i, block in enumerate((ab, ahead, behind)):
+            out[dz * 3 + i] = block[dz]
+
+
+def opposite(behind, ahead, out):
+    for rows, half in ((slice(0, 64), behind), (slice(64, 128), ahead)):
+        for dz in range(2):
+            out[dz, rows, :1024] = half[2 + dz, :64]
+            out[dz, rows, 1024:] = half[2 + dz, 64:]
+
+
+def pair_up(a0, a1, b0, b1, a, b):
+    for out, parts in ((a, (a0, a1)), (b, (b0, b1))):
+        for i, part in enumerate(parts):
+            out[2 * i] = part[0]
+            out[2 * i + 1] = part[1]
 
 
 def on_device(inputs, weight, out_grad):
     bf16, f32 = jnp.bfloat16, jnp.float32
 
     g, h = out_grad, swap(out_grad, "zl")
-    g1, g3, g2 = shift(g, "x", 1), shift(g, "x", -1), shift(g, "x", 2)
+    g2 = shift(g, "x", 2)
 
     (ab,) = kernel_of(pair, "pair", (inputs, swap(inputs, "zh")), [(2, 128, 2048)])
+    (g,) = kernel_of(relay, "relay_g", (g,), [(256, 1152)], (g2, ab))
+    g1, g3 = shift(g, "x", 1), shift(g, "x", -1)
     behind, ahead = shift(ab, "y", 1), shift(ab, "y", -1)
     first, second = kernel_of(halves, "halves", (behind, ahead), [(2, 64, 2048)] * 2)
 
     (h,) = kernel_of(relay, "relay", (h,), [(256, 1152)], (ab, g1, g3))
     h1, h3, h2 = shift(h, "x", 1), shift(h, "x", -1), swap(g2, "zl")
-    blocks = [(8, 128, 1152)] * 2 + [(4, 128, 1152)] * 4
-    grads = kernel_of(place_grads, "place_grads", (g, g3, g2, g1, h, h3, h2, h1), blocks, (first,))
-    mine, theirs, mine_near, mine_far, theirs_near, theirs_far = (part.reshape(-1, 1152) for part in grads)
-
     wa, wb = weight[:1024], weight[1024:]
-
-    def partial(rows, w, part):
-        return (dot_nt(rows, w) + part.astype(f32)).astype(bf16).reshape(-1, 4, 128, 1024)
-
-    tb1 = dot_nt(theirs_far, wb).astype(bf16)
-    ta = dot_nt(after(theirs, tb1), wa).astype(bf16)
-    pb1 = partial(mine_far, wb, swap(tb1, "core"))
-    pa = partial(after(mine, pb1), wa, swap(ta, "core"))
-    qb = swap(pb1[0], "zh")
-    q0, q1, q2, q3 = kernel_of(cut, "cut", (pa,), [(2, 128, 1024)] * 4)
+    blocks = [(4, 128, 1152)] * 2
+    early_mine, early_theirs = kernel_of(by_core, "by_core_early", (g, g3, g2, g1), blocks)
+
+    def theirs_of(part, w):
+        return dot_nt(part.reshape(512, 1152), w).astype(bf16)
+
+    def partial(part, w, other):
+        return (dot_nt(part.reshape(512, 1152), w) + other.astype(f32)).astype(bf16).reshape(4, 128, -1)
+
+    early = partial(early_mine, weight, swap(theirs_of(early_theirs, weight), "core"))
+    late_mine, late_theirs = kernel_of(by_core, "by_core_late", (h, h3, h2, h1), blocks, (first,))
+    late_b = theirs_of(late_theirs, wb)
+    late_a = theirs_of(after(late_theirs, late_b), wa)
+    late_b = partial(late_mine, wb, swap(late_b, "core"))
+    late_a = partial(after(late_mine, late_b), wa, swap(late_a, "core"))
+    near, far = kernel_of(cut_b, "cut_b", (early, late_b), [(4, 128, 1024)] * 2)
+    far = swap(far, "zh")
+    cuts = [(2, 128, 1024), (4, 128, 1024)] * 2
+    q0, q1, q2, q3 = kernel_of(cut_a, "cut_a", (early, late_a, first, second), cuts)
     q1, q3, q2 = shift(q1, "y", 1), shift(q3, "y", -1), shift(q2, "y", 2)
-    tb0 = dot_nt(theirs_near, wb).astype(bf16)
-    pb0 = partial(mine_near, wb, swap(tb0, "core"))
-
-    first, second = shift(first, "y", 1), shift(second, "y", -1)
-    waits = (q1, q2, q3, first, second)
-    s0, s1, s2, s3 = kernel_of(sum_blocks, "sum_zh", (pb0[0], qb), [(128, 1024)] * 4, waits)
+
+    (own,) = kernel_of(near_first, "near_first", (ab, ahead, behind), [(6, 128, 2048)], (q0,))
+    own = own.reshape(768, 2048)
+    parts = (early_mine, early_theirs, late_mine, late_theirs)
+    grads = kernel_of(place_grads, "place_grads", parts, [(6, 128, 1152)] * 2 + [(2, 128, 1152)] * 2, (q0,))
+    mine, theirs = (part.reshape(768, 1152) for part in grads[:2])
+    mine_opposite, theirs_opposite = grads[2:]
+    weight_grad = dot_tn(own, mine) + dot_tn(swap(own, "core"), theirs)
+
+    waits = (q1, q2, q3, far, weight_grad)
+    s0, s1, s2, s3 = kernel_of(sum_blocks, "sum_zh", (near, far), [(128, 1024)] * 4, waits)
     r1, r3, r2 = shift(s1, "y", 1), shift(s3, "y", -1), shift(s2, "y", 2)
-    a0, a1 = kernel_of(sum_four, "sum_y", (q0, q1, q2, q3), [(128, 1024)] * 2)
+    a0, a1 = kernel_of(sum_four, "sum_y", (q0, q1, q2, q3), [(128, 1024)] * 2, waits)
     a1 = swap(a1, "zh")
 
-    (own,) = kernel_of(near_first, "near_first", (ab, ahead, behind, first, second), [(8, 128, 2048)], (s1, a1))
-    own = own.reshape(1024, 2048)
-    weight_grad = dot_tn(own, mine) + dot_tn(swap(own, "core"), theirs)
+    (own,) = kernel_of(opposite, "opposite", (q1, q3), [(2, 128, 2048)], (s1,))
+    own, other = kernel_of(pair_up, "pair_up", (own, swap(own, "core"), mine_opposite, theirs_opposite), [(4, 128, 2048), (4, 128, 1152)])
+    weight_grad += dot_tn(own.reshape(512, 2048), other.reshape(512, 1152))
     weight_grad = with_layout_constraint(weight_grad, Layout((0, 1)))
 
     parts = (a0, a1, s0, r1, r3, r2)

time: 131 us -> 122 us (0.931)
  the two profiles are of different devices: /device:TPU:54 before, /device:TPU:24 now
where the time goes in v3:
time: 122 us
  waiting for transfers between devices  58.6 us (48%)
  matrix products  29.5 us (24%)
  starting transfers between devices  27.8 us (23%)
  Pallas kernels  3.75 us (3%)
    ppermute x13, waiting for transfers between devices, shift(): return lax.ppermute(value, axis, [(i, (i + step) % 4) for i in range(4)])  37.3 us
    ppermute x10, waiting for transfers between devices, swap(): return lax.ppermute(value, axis, [(0, 1), (1, 0)])  21.3 us
    dot_general x3, matrix products, dot_tn(): lax.dot_general(a, b, (((0,), (0,)), ((), ())), preferred_element_type=jn...  17 us
    ppermute x13, starting transfers between devices, shift(): return lax.ppermute(value, axis, [(i, (i + step) % 4) for i in range(4)])  16 us
    dot_general x6, matrix products, dot_nt(): lax.dot_general(a, b, (((1,), (1,)), ((), ())), preferred_element_type=jn...  12.5 us
    ppermute x10, starting transfers between devices, swap(): return lax.ppermute(value, axis, [(0, 1), (1, 0)])  11.7 us
    pallas_call x15, Pallas kernels, kernel_of(): pl.pallas_call(lambda *refs: kernel(*refs[:n], *refs[n + len(waits):]), n...  3.75 us
  transfers between devices with their start and end apart: 23, of which 14 were waited for; matrix products, arithmetic and copies ran while one was open for 22% of the time, Pallas kernels for 2%

profile of v3, /device:TPU:24, one launch (start us, length us, event | category | flops | bytes accessed | tf_op | source)
XLA Modules:
  0.0 121.6 jit_solution(17766045556225060312)
XLA Ops:
  0.6 3.1 %collective-permute-start = (bf16[256,1152]{1,0:T(8,128)(2,1)}, bf16[256,1152]{1,0:T(8,128)(2,1)S(1)}, u32[]{:S(2)}, u32[]{:S(2)}) collective-permute-start(bf16[256,1152]{1,0:T(8,128)(2,1)} %refs_0_.3), channel_id=1, source_target_pairs={{0,64},{32,96},{64,0},{96,32},{1,65},{33,97},{65,1},{97,33},{2,66}... | collective-permute-start | bytes 1769480 | tf_op jit(solution)/shard_map/ppermute | solution.py:15
  3.7 3.9 %collective-permute-start.1 = (bf16[128,2048]{1,0:T(8,128)(2,1)}, bf16[128,2048]{1,0:T(8,128)(2,1)S(1)}, u32[]{:S(2)}, u32[]{:S(2)}) collective-permute-start(bf16[128,2048]{1,0:T(8,128)(2,1)} %refs_0_.2), channel_id=1, source_target_pairs={{0,8},{8,0},{1,9},{9,1},{2,10},{10,2},{3,11},{11,3},{4,12},{12,4},... | collective-permute-start | bytes 1572872 | tf_op jit(solution)/shard_map/ppermute | solution.py:19
  7.6 1.0 collective-permute-start.5
  8.6 12.0 %collective-permute-done.1.refs_1_ = bf16[128,2048]{1,0:T(8,128)(2,1)S(1)} collective-permute-done((bf16[128,2048]{1,0:T(8,128)(2,1)}, bf16[128,2048]{1,0:T(8,128)(2,1)S(1)}, u32[]{:S(2)}, u32[]{:S(2)}) %collective-permute-start.1) | collective-permute-done | bytes 524320 | tf_op jit(solution)/shard_map/ppermute | solution.py:19
  20.6 1.0 copy-done.2
  21.7 0.1 pair.1.refs_2_.refs_1_.refs_0_
  21.7 0.0 collective-permute-done.refs_1_.refs_2_
  21.8 0.0 copy-start.3
  21.8 1.2 collective-permute-start.2
  23.0 0.9 collective-permute-start.3
  23.9 0.2 collective-permute-start.9
  24.1 1.8 %collective-permute-start.10 = (bf16[2,128,2048]{2,1,0:T(8,128)(2,1)S(1)}, bf16[2,128,2048]{2,1,0:T(8,128)(2,1)S(1)}, u32[]{:S(2)}, u32[]{:S(2)}) collective-permute-start(bf16[2,128,2048]{2,1,0:T(8,128)(2,1)S(1)} %pair.1.refs_2_.refs_1_.refs_0_), channel_id=1, source_target_pairs={{0,6},{2,0},{4,2},{6,4},{1,7},{3,1},{5,3},{7,5},{8,14},{10,8},{12,... | collective-permute-start | bytes 3145736 | tf_op jit(solution)/shard_map/ppermute | solution.py:15
  25.9 6.9 %collective-permute-done.5.refs_0_ = bf16[256,1152]{1,0:T(8,128)(2,1)S(1)} collective-permute-done((bf16[256,1152]{1,0:T(8,128)(2,1)}, bf16[256,1152]{1,0:T(8,128)(2,1)S(1)}, u32[]{:S(2)}, u32[]{:S(2)}) %collective-permute-start.5) | collective-permute-done | bytes 589856 | tf_op jit(solution)/shard_map/ppermute | solution.py:19
  32.8 1.0 collective-permute-start.7
  33.9 1.1 collective-permute-done.2.refs_1_.refs_3_
  34.9 2.1 %collective-permute-done.3.refs_3_.refs_2_ = bf16[256,1152]{1,0:T(8,128)(2,1)S(1)} collective-permute-done((bf16[256,1152]{1,0:T(8,128)(2,1)S(1)}, bf16[256,1152]{1,0:T(8,128)(2,1)S(1)}, u32[]{:S(2)}, u32[]{:S(2)}) %collective-permute-start.3) | collective-permute-done | bytes 589856 | tf_op jit(solution)/shard_map/ppermute | solution.py:15
  37.1 0.4 collective-permute-start.6
  37.4 1.7 %collective-permute-start.8 = (bf16[256,1152]{1,0:T(8,128)(2,1)S(1)}, bf16[256,1152]{1,0:T(8,128)(2,1)S(1)}, u32[]{:S(2)}, u32[]{:S(2)}) collective-permute-start(bf16[256,1152]{1,0:T(8,128)(2,1)S(1)} %relay.1.refs_0_), channel_id=1, source_target_pairs={{0,32},{32,64},{64,96},{96,0},{1,33},{33,65},{65,97},{97,1},{2,34}... | collective-permute-start | bytes 1769480 | tf_op jit(solution)/shard_map/ppermute | solution.py:15
  39.1 0.2 by_core_early.1
  39.3 3.1 %convolution_convert_fusion = bf16[512,2048]{1,0:T(8,128)(2,1)S(1)} fusion(bf16[512,1152]{1,0:T(8,128)(2,1)S(1)} %bitcast.33, bf16[2048,1152]{1,0:T(8,128)(2,1)S(1)} %copy-done.3), kind=kOutput, calls=%fused_computation.3 | convolution fusion | flops 2416967680 | bytes 7995392 | tf_op jit(solution)/shard_map/dot_general | solution.py:27
  42.5 3.7 %collective-permute-done.9.refs_0_.refs_2_ = bf16[2,128,2048]{2,1,0:T(8,128)(2,1)S(1)} collective-permute-done((bf16[2,128,2048]{2,1,0:T(8,128)(2,1)S(1)}, bf16[2,128,2048]{2,1,0:T(8,128)(2,1)S(1)}, u32[]{:S(2)}, u32[]{:S(2)}) %collective-permute-start.9) | collective-permute-done | bytes 1048608 | tf_op jit(solution)/shard_map/ppermute | solution.py:15
  46.2 0.0 collective-permute-start.4
  46.2 1.2 collective-permute-done.10.refs_1_
  47.4 0.1 halves.1
  47.5 0.0 collective-permute-done.7.refs_2_
  47.5 1.4 %collective-permute-done.6.refs_1_ = bf16[256,1152]{1,0:T(8,128)(2,1)S(1)} collective-permute-done((bf16[256,1152]{1,0:T(8,128)(2,1)S(1)}, bf16[256,1152]{1,0:T(8,128)(2,1)S(1)}, u32[]{:S(2)}, u32[]{:S(2)}) %collective-permute-start.6) | collective-permute-done | bytes 589856 | tf_op jit(solution)/shard_map/ppermute | solution.py:15
  49.0 1.5 %collective-permute-done.8.refs_3_ = bf16[256,1152]{1,0:T(8,128)(2,1)S(1)} collective-permute-done((bf16[256,1152]{1,0:T(8,128)(2,1)S(1)}, bf16[256,1152]{1,0:T(8,128)(2,1)S(1)}, u32[]{:S(2)}, u32[]{:S(2)}) %collective-permute-start.8) | collective-permute-done | bytes 589856 | tf_op jit(solution)/shard_map/ppermute | solution.py:15
  50.5 0.2 by_core_late.1
  50.6 1.6 %fusion.8 = bf16[512,1024]{1,0:T(8,128)(2,1)S(1)} fusion(bf16[512,1152]{1,0:T(8,128)(2,1)S(1)} %bitcast.36, bf16[2048,1152]{1,0:T(8,128)(2,1)S(1)} %copy-done.3), kind=kOutput, calls=%fused_computation.14 | convolution fusion | flops 1208483840 | bytes 4587520 | tf_op jit(solution)/shard_map/dot_general | solution.py:27
  52.2 0.1 collective-permute-start.11
  52.3 1.6 %fusion.11 = bf16[512,1024]{1,0:T(8,128)(2,1)S(1)} fusion(bf16[512,1152]{1,0:T(8,128)(2,1)S(1)} %bitcast.37, bf16[2048,1152]{1,0:T(8,128)(2,1)S(1)} %copy-done.3), kind=kOutput, calls=%fused_computation.15 | convolution fusion | flops 1208483840 | bytes 4587520 | tf_op jit(solution)/shard_map/dot_general | solution.py:27
  53.9 0.6 collective-permute-start.12
  54.4 0.5 collective-permute-done.11
  54.9 1.5 %add_convert_fusion.2 = bf16[512,1024]{1,0:T(8,128)(2,1)S(1)} fusion(bf16[512,1024]{1,0:T(8,128)(2,1)S(1)} %collective-permute-done.11, bf16[512,1152]{1,0:T(8,128)(2,1)S(1)} %bitcast.34, bf16[2048,1152]{1,0:T(8,128)(2,1)S(1)} %copy-done.3), kind=kOutput, calls=%fused_computation.5 | convolution fusion | flops 1209532416 | bytes 5636096 | tf_op jit(solution)/shard_map/dot_general | solution.py:27
  56.5 0.2 collective-permute-done.12
  56.7 1.6 %add_convert_fusion.1 = bf16[512,1024]{1,0:T(8,128)(2,1)S(1)} fusion(bf16[512,1024]{1,0:T(8,128)(2,1)S(1)} %collective-permute-done.12, bf16[512,1152]{1,0:T(8,128)(2,1)S(1)} %bitcast.35, bf16[2048,1152]{1,0:T(8,128)(2,1)S(1)} %copy-done.3), kind=kOutput, calls=%fused_computation.4 | convolution fusion | flops 1209532416 | bytes 5636096 | tf_op jit(solution)/shard_map/dot_general | solution.py:27
  58.3 0.0 collective-permute-done.4
  58.3 3.2 %add_convert_fusion = bf16[512,2048]{1,0:T(8,128)(2,1)S(1)} fusion(bf16[512,2048]{1,0:T(8,128)(2,1)S(1)} %collective-permute-done.4, bf16[512,1152]{1,0:T(8,128)(2,1)S(1)} %bitcast.32, bf16[2048,1152]{1,0:T(8,128)(2,1)S(1)} %copy-done.3), kind=kOutput, calls=%fused_computation.2 | convolution fusion | flops 2419064832 | bytes 10092544 | tf_op jit(solution)/shard_map/dot_general | solution.py:27
  61.4 0.4 cut_a.1
  61.8 0.2 near_first.1
  62.1 0.4 collective-permute-start.17
  62.5 0.4 cut_b.1
  62.9 0.5 place_grads.1
  63.3 0.3 collective-permute-start.13
  63.6 2.6 %collective-permute-start.14 = (bf16[2,128,1024]{2,1,0:T(8,128)(2,1)S(1)}, bf16[2,128,1024]{2,1,0:T(8,128)(2,1)S(1)}, u32[]{:S(2)}, u32[]{:S(2)}) collective-permute-start(bf16[2,128,1024]{2,1,0:T(8,128)(2,1)S(1)} %get-tuple-element.38), channel_id=1, source_target_pairs={{0,4},{2,6},{4,0},{6,2},{1,5},{3,7},{5,1},{7,3},{8,12},{10,14},{12... | collective-permute-start | bytes 1572872 | tf_op jit(solution)/shard_map/ppermute | solution.py:15
  66.2 2.3 %collective-permute-start.16 = (bf16[4,128,1024]{2,1,0:T(8,128)(2,1)S(1)}, bf16[4,128,1024]{2,1,0:T(8,128)(2,1)S(1)}, u32[]{:S(2)}, u32[]{:S(2)}) collective-permute-start(bf16[4,128,1024]{2,1,0:T(8,128)(2,1)S(1)} %get-tuple-element.40), channel_id=1, source_target_pairs={{0,8},{8,0},{1,9},{9,1},{2,10},{10,2},{3,11},{11,3},{4,12},{12,4},... | collective-permute-start | bytes 3145736 | tf_op jit(solution)/shard_map/ppermute | solution.py:19
  68.5 6.8 %fusion.18 = f32[2048,1152,1]{1,0,2:T(8,128)} fusion(bf16[6,128,2048]{2,1,0:T(8,128)(2,1)S(1)} %near_first.1, bf16[6,128,1152]{2,1,0:T(8,128)(2,1)S(1)} %get-tuple-element.41), kind=kOutput, calls=%fused_computation.16 | convolution fusion | flops 3623878656 | bytes 14352384 | tf_op jit(solution)/shard_map/dot_general | solution.py:31
  75.3 7.1 %bitcast_add_fusion.1.refs_8_.refs_6_ = f32[2048,1152]{1,0:T(8,128)S(1)} fusion(f32[2048,1152,1]{1,0,2:T(8,128)} %fusion.18, bf16[768,2048]{1,0:T(8,128)(2,1)S(1)} %collective-permute-done.17, bf16[768,1152]{1,0:T(8,128)(2,1)S(1)} %bitcast.40), kind=kOutput, calls=%fused_computation.1 | convolution fusion | flops 3626237952 | bytes 23789568 | tf_op jit(solution)/shard_map/dot_general | solution.py:31
  82.5 6.9 %collective-permute-done.13.refs_1_.refs_4_.refs_2_.refs_0_ = bf16[4,128,1024]{2,1,0:T(8,128)(2,1)S(1)} collective-permute-done((bf16[4,128,1024]{2,1,0:T(8,128)(2,1)S(1)}, bf16[4,128,1024]{2,1,0:T(8,128)(2,1)S(1)}, u32[]{:S(2)}, u32[]{:S(2)}) %collective-permute-start.13) | collective-permute-done | bytes 1048608 | tf_op jit(solution)/shard_map/ppermute | solution.py:15
  89.4 12.0 %collective-permute-done.15.refs_3_.refs_6_.refs_4_.refs_1_ = bf16[4,128,1024]{2,1,0:T(8,128)(2,1)S(1)} collective-permute-done((bf16[4,128,1024]{2,1,0:T(8,128)(2,1)S(1)}, bf16[4,128,1024]{2,1,0:T(8,128)(2,1)S(1)}, u32[]{:S(2)}, u32[]{:S(2)}) %collective-permute-start.15) | collective-permute-done | bytes 1048608 | tf_op jit(solution)/shard_map/ppermute | solution.py:15
  101.5 0.2 sum_zh.1
  101.7 0.1 opposite.1.refs_0_
  101.8 0.1 collective-permute-start.22
  101.9 1.2 collective-permute-start.19
  103.0 0.3 sum_y.1
  103.3 2.4 %collective-permute-start.18 = (bf16[128,1024]{1,0:T(8,128)(2,1)S(1)}, bf16[128,1024]{1,0:T(8,128)(2,1)S(1)}, u32[]{:S(2)}, u32[]{:S(2)}) collective-permute-start(bf16[128,1024]{1,0:T(8,128)(2,1)S(1)} %get-tuple-element.44), channel_id=1, source_target_pairs={{0,8},{8,0},{1,9},{9,1},{2,10},{10,2},{3,11},{11,3},{4,12},{12,4},... | collective-permute-start | bytes 786440 | tf_op jit(solution)/shard_map/ppermute | solution.py:19
  105.7 0.9 collective-permute-start.20
  106.6 1.7 %collective-permute-start.21 = (bf16[128,1024]{1,0:T(8,128)(2,1)S(1)}, bf16[128,1024]{1,0:T(8,128)(2,1)S(1)}, u32[]{:S(2)}, u32[]{:S(2)}) collective-permute-start(bf16[128,1024]{1,0:T(8,128)(2,1)S(1)} %get-tuple-element.49), channel_id=1, source_target_pairs={{0,4},{2,6},{4,0},{6,2},{1,5},{3,7},{5,1},{7,3},{8,12},{10,14},{12... | collective-permute-start | bytes 786440 | tf_op jit(solution)/shard_map/ppermute | solution.py:15
  108.3 0.2 pair_up.1
  108.6 3.0 %bitcast_add_fusion.refs_6_ = f32[2048,1152]{1,0:T(8,128)S(1)} fusion(f32[2048,1152]{1,0:T(8,128)S(1)} %bitcast_add_fusion.1.refs_8_.refs_6_, bf16[4,128,2048]{2,1,0:T(8,128)(2,1)S(1)} %get-tuple-element.52, bf16[4,128,1152]{2,1,0:T(8,128)(2,1)S(1)} %get-tuple-element.53), kind=kOutput, calls=%fused_computation | convolution fusion | flops 2418278400 | bytes 22151168 | tf_op jit(solution)/shard_map/dot_general | solution.py:31
  111.6 0.0 copy-start
  111.6 1.6 %collective-permute-done.18.refs_1_ = bf16[128,1024]{1,0:T(8,128)(2,1)S(1)} collective-permute-done((bf16[128,1024]{1,0:T(8,128)(2,1)S(1)}, bf16[128,1024]{1,0:T(8,128)(2,1)S(1)}, u32[]{:S(2)}, u32[]{:S(2)}) %collective-permute-start.18) | collective-permute-done | bytes 262176 | tf_op jit(solution)/shard_map/ppermute | solution.py:19
  113.3 7.3 %collective-permute-done.20.refs_4_ = bf16[128,1024]{1,0:T(8,128)(2,1)S(1)} collective-permute-done((bf16[128,1024]{1,0:T(8,128)(2,1)S(1)}, bf16[128,1024]{1,0:T(8,128)(2,1)S(1)}, u32[]{:S(2)}, u32[]{:S(2)}) %collective-permute-start.20) | collective-permute-done | bytes 262176 | tf_op jit(solution)/shard_map/ppermute | solution.py:15
  120.6 1.0 sum_last.1
  (14 shorter events, 0.1 us)
Async XLA Ops:
  0.6 21.1 %copy-start.1 = (bf16[256,1152]{1,0:T(8,128)(2,1)S(1)}, bf16[256,1152]{1,0:T(8,128)(2,1)}, u32[]{:S(2)}) copy-start(bf16[256,1152]{1,0:T(8,128)(2,1)} %refs_0_.3) | copy-start | bytes 1769476
  0.6 21.1 %collective-permute-start = (bf16[256,1152]{1,0:T(8,128)(2,1)}, bf16[256,1152]{1,0:T(8,128)(2,1)S(1)}, u32[]{:S(2)}, u32[]{:S(2)}) collective-permute-start(bf16[256,1152]{1,0:T(8,128)(2,1)} %refs_0_.3), channel_id=1, source_target_pairs={{0,64},{32,96},{64,0},{96,32},{1,65},{33,97},{65,1},{97,33},{2,66}... | collective-permute-start | bytes 1769480 | tf_op jit(solution)/shard_map/ppermute | solution.py:15
  3.7 16.9 %collective-permute-start.1 = (bf16[128,2048]{1,0:T(8,128)(2,1)}, bf16[128,2048]{1,0:T(8,128)(2,1)S(1)}, u32[]{:S(2)}, u32[]{:S(2)}) collective-permute-start(bf16[128,2048]{1,0:T(8,128)(2,1)} %refs_0_.2), channel_id=1, source_target_pairs={{0,8},{8,0},{1,9},{9,1},{2,10},{10,2},{3,11},{11,3},{4,12},{12,4},... | collective-permute-start | bytes 1572872 | tf_op jit(solution)/shard_map/ppermute | solution.py:19
  7.6 25.2 %collective-permute-start.5 = (bf16[256,1152]{1,0:T(8,128)(2,1)}, bf16[256,1152]{1,0:T(8,128)(2,1)S(1)}, u32[]{:S(2)}, u32[]{:S(2)}) collective-permute-start(bf16[256,1152]{1,0:T(8,128)(2,1)} %refs_0_.3), channel_id=1, source_target_pairs={{0,16},{16,0},{1,17},{17,1},{2,18},{18,2},{3,19},{19,3},{4,20},{20... | collective-permute-start | bytes 1769480 | tf_op jit(solution)/shard_map/ppermute | solution.py:19
  20.6 1.0 copy-start.2
  21.8 17.5 %copy-start.3 = (bf16[2048,1152]{1,0:T(8,128)(2,1)S(1)}, bf16[2048,1152]{1,0:T(8,128)(2,1)}, u32[]{:S(2)}) copy-start(bf16[2048,1152]{1,0:T(8,128)(2,1)} %param.4) | copy-start | bytes 14155780
  21.8 13.1 %collective-permute-start.2 = (bf16[256,1152]{1,0:T(8,128)(2,1)S(1)}, bf16[256,1152]{1,0:T(8,128)(2,1)S(1)}, u32[]{:S(2)}, u32[]{:S(2)}) collective-permute-start(bf16[256,1152]{1,0:T(8,128)(2,1)S(1)} %relay_g.1.refs_0_), channel_id=1, source_target_pairs={{0,96},{32,0},{64,32},{96,64},{1,97},{33,1},{65,33},{97,65},{2,98}... | collective-permute-start | bytes 1769480 | tf_op jit(solution)/shard_map/ppermute | solution.py:15
  23.0 14.0 %collective-permute-start.3 = (bf16[256,1152]{1,0:T(8,128)(2,1)S(1)}, bf16[256,1152]{1,0:T(8,128)(2,1)S(1)}, u32[]{:S(2)}, u32[]{:S(2)}) collective-permute-start(bf16[256,1152]{1,0:T(8,128)(2,1)S(1)} %relay_g.1.refs_0_), channel_id=1, source_target_pairs={{0,32},{32,64},{64,96},{96,0},{1,33},{33,65},{65,97},{97,1},{2,34}... | collective-permute-start | bytes 1769480 | tf_op jit(solution)/shard_map/ppermute | solution.py:15
  23.9 22.3 %collective-permute-start.9 = (bf16[2,128,2048]{2,1,0:T(8,128)(2,1)S(1)}, bf16[2,128,2048]{2,1,0:T(8,128)(2,1)S(1)}, u32[]{:S(2)}, u32[]{:S(2)}) collective-permute-start(bf16[2,128,2048]{2,1,0:T(8,128)(2,1)S(1)} %pair.1.refs_2_.refs_1_.refs_0_), channel_id=1, source_target_pairs={{0,2},{2,4},{4,6},{6,0},{1,3},{3,5},{5,7},{7,1},{8,10},{10,12},{12... | collective-permute-start | bytes 3145736 | tf_op jit(solution)/shard_map/ppermute | solution.py:15
  24.1 23.3 %collective-permute-start.10 = (bf16[2,128,2048]{2,1,0:T(8,128)(2,1)S(1)}, bf16[2,128,2048]{2,1,0:T(8,128)(2,1)S(1)}, u32[]{:S(2)}, u32[]{:S(2)}) collective-permute-start(bf16[2,128,2048]{2,1,0:T(8,128)(2,1)S(1)} %pair.1.refs_2_.refs_1_.refs_0_), channel_id=1, source_target_pairs={{0,6},{2,0},{4,2},{6,4},{1,7},{3,1},{5,3},{7,5},{8,14},{10,8},{12,... | collective-permute-start | bytes 3145736 | tf_op jit(solution)/shard_map/ppermute | solution.py:15
  32.8 14.7 %collective-permute-start.7 = (bf16[256,1152]{1,0:T(8,128)(2,1)S(1)}, bf16[256,1152]{1,0:T(8,128)(2,1)S(1)}, u32[]{:S(2)}, u32[]{:S(2)}) collective-permute-start(bf16[256,1152]{1,0:T(8,128)(2,1)S(1)} %collective-permute-done.refs_1_.refs_2_), channel_id=1, source_target_pairs={{0,16},{16,0},{1,17},{17,1},{2,18},{18,2},{3,19},{19,3},{4,20},{20... | collective-permute-start | bytes 1769480 | tf_op jit(solution)/shard_map/ppermute | solution.py:19
  37.1 11.9 %collective-permute-start.6 = (bf16[256,1152]{1,0:T(8,128)(2,1)S(1)}, bf16[256,1152]{1,0:T(8,128)(2,1)S(1)}, u32[]{:S(2)}, u32[]{:S(2)}) collective-permute-start(bf16[256,1152]{1,0:T(8,128)(2,1)S(1)} %relay.1.refs_0_), channel_id=1, source_target_pairs={{0,96},{32,0},{64,32},{96,64},{1,97},{33,1},{65,33},{97,65},{2,98}... | collective-permute-start | bytes 1769480 | tf_op jit(solution)/shard_map/ppermute | solution.py:15
  37.4 13.1 %collective-permute-start.8 = (bf16[256,1152]{1,0:T(8,128)(2,1)S(1)}, bf16[256,1152]{1,0:T(8,128)(2,1)S(1)}, u32[]{:S(2)}, u32[]{:S(2)}) collective-permute-start(bf16[256,1152]{1,0:T(8,128)(2,1)S(1)} %relay.1.refs_0_), channel_id=1, source_target_pairs={{0,32},{32,64},{64,96},{96,0},{1,33},{33,65},{65,97},{97,1},{2,34}... | collective-permute-start | bytes 1769480 | tf_op jit(solution)/shard_map/ppermute | solution.py:15
  46.2 12.0 %collective-permute-start.4 = (bf16[512,2048]{1,0:T(8,128)(2,1)S(1)}, bf16[512,2048]{1,0:T(8,128)(2,1)S(1)}, u32[]{:S(2)}, u32[]{:S(2)}) collective-permute-start(bf16[512,2048]{1,0:T(8,128)(2,1)S(1)} %convolution_convert_fusion), channel_id=1, source_target_pairs={{0,1},{1,0},{2,3},{3,2},{4,5},{5,4},{6,7},{7,6},{8,9},{9,8},{10,11... | collective-permute-start | bytes 6291464 | tf_op jit(solution)/shard_map/ppermute | solution.py:19
  52.2 2.7 %collective-permute-start.11 = (bf16[512,1024]{1,0:T(8,128)(2,1)S(1)}, bf16[512,1024]{1,0:T(8,128)(2,1)S(1)}, u32[]{:S(2)}, u32[]{:S(2)}) collective-permute-start(bf16[512,1024]{1,0:T(8,128)(2,1)S(1)} %fusion.8), channel_id=1, source_target_pairs={{0,1},{1,0},{2,3},{3,2},{4,5},{5,4},{6,7},{7,6},{8,9},{9,8},{10,11... | collective-permute-start | bytes 3145736 | tf_op jit(solution)/shard_map/ppermute | solution.py:19
  53.9 2.9 %collective-permute-start.12 = (bf16[512,1024]{1,0:T(8,128)(2,1)S(1)}, bf16[512,1024]{1,0:T(8,128)(2,1)S(1)}, u32[]{:S(2)}, u32[]{:S(2)}) collective-permute-start(bf16[512,1024]{1,0:T(8,128)(2,1)S(1)} %fusion.11), channel_id=1, source_target_pairs={{0,1},{1,0},{2,3},{3,2},{4,5},{5,4},{6,7},{7,6},{8,9},{9,8},{10,11... | collective-permute-start | bytes 3145736 | tf_op jit(solution)/shard_map/ppermute | solution.py:19
  62.1 13.3 %collective-permute-start.17 = (bf16[768,2048]{1,0:T(8,128)(2,1)S(1)}, bf16[768,2048]{1,0:T(8,128)(2,1)S(1)}, u32[]{:S(2)}, u32[]{:S(2)}) collective-permute-start(bf16[768,2048]{1,0:T(8,128)(2,1)S(1)} %bitcast.31), channel_id=1, source_target_pairs={{0,1},{1,0},{2,3},{3,2},{4,5},{5,4},{6,7},{7,6},{8,9},{9,8},{10,11... | collective-permute-start | bytes 9437192 | tf_op jit(solution)/shard_map/ppermute | solution.py:19
  63.3 26.1 %collective-permute-start.13 = (bf16[4,128,1024]{2,1,0:T(8,128)(2,1)S(1)}, bf16[4,128,1024]{2,1,0:T(8,128)(2,1)S(1)}, u32[]{:S(2)}, u32[]{:S(2)}) collective-permute-start(bf16[4,128,1024]{2,1,0:T(8,128)(2,1)S(1)} %get-tuple-element.37), channel_id=1, source_target_pairs={{0,2},{2,4},{4,6},{6,0},{1,3},{3,5},{5,7},{7,1},{8,10},{10,12},{12... | collective-permute-start | bytes 3145736 | tf_op jit(solution)/shard_map/ppermute | solution.py:15
  63.6 18.9 %collective-permute-start.14 = (bf16[2,128,1024]{2,1,0:T(8,128)(2,1)S(1)}, bf16[2,128,1024]{2,1,0:T(8,128)(2,1)S(1)}, u32[]{:S(2)}, u32[]{:S(2)}) collective-permute-start(bf16[2,128,1024]{2,1,0:T(8,128)(2,1)S(1)} %get-tuple-element.38), channel_id=1, source_target_pairs={{0,4},{2,6},{4,0},{6,2},{1,5},{3,7},{5,1},{7,3},{8,12},{10,14},{12... | collective-permute-start | bytes 1572872 | tf_op jit(solution)/shard_map/ppermute | solution.py:15
  66.2 35.2 %collective-permute-start.15 = (bf16[4,128,1024]{2,1,0:T(8,128)(2,1)S(1)}, bf16[4,128,1024]{2,1,0:T(8,128)(2,1)S(1)}, u32[]{:S(2)}, u32[]{:S(2)}) collective-permute-start(bf16[4,128,1024]{2,1,0:T(8,128)(2,1)S(1)} %get-tuple-element.39), channel_id=1, source_target_pairs={{0,6},{2,0},{4,2},{6,4},{1,7},{3,1},{5,3},{7,5},{8,14},{10,8},{12,... | collective-permute-start | bytes 3145736 | tf_op jit(solution)/shard_map/ppermute | solution.py:15
  66.2 35.2 %collective-permute-start.16 = (bf16[4,128,1024]{2,1,0:T(8,128)(2,1)S(1)}, bf16[4,128,1024]{2,1,0:T(8,128)(2,1)S(1)}, u32[]{:S(2)}, u32[]{:S(2)}) collective-permute-start(bf16[4,128,1024]{2,1,0:T(8,128)(2,1)S(1)} %get-tuple-element.40), channel_id=1, source_target_pairs={{0,8},{8,0},{1,9},{9,1},{2,10},{10,2},{3,11},{11,3},{4,12},{12,4},... | collective-permute-start | bytes 3145736 | tf_op jit(solution)/shard_map/ppermute | solution.py:19
  101.8 6.6 %collective-permute-start.22 = (bf16[2,128,2048]{2,1,0:T(8,128)(2,1)S(1)}, bf16[2,128,2048]{2,1,0:T(8,128)(2,1)S(1)}, u32[]{:S(2)}, u32[]{:S(2)}) collective-permute-start(bf16[2,128,2048]{2,1,0:T(8,128)(2,1)S(1)} %opposite.1.refs_0_), channel_id=1, source_target_pairs={{0,1},{1,0},{2,3},{3,2},{4,5},{5,4},{6,7},{7,6},{8,9},{9,8},{10,11... | collective-permute-start | bytes 3145736 | tf_op jit(solution)/shard_map/ppermute | solution.py:19
  101.9 11.4 %collective-permute-start.19 = (bf16[128,1024]{1,0:T(8,128)(2,1)S(1)}, bf16[128,1024]{1,0:T(8,128)(2,1)S(1)}, u32[]{:S(2)}, u32[]{:S(2)}) collective-permute-start(bf16[128,1024]{1,0:T(8,128)(2,1)S(1)} %get-tuple-element.47.refs_2_), channel_id=1, source_target_pairs={{0,2},{2,4},{4,6},{6,0},{1,3},{3,5},{5,7},{7,1},{8,10},{10,12},{12... | collective-permute-start | bytes 786440 | tf_op jit(solution)/shard_map/ppermute | solution.py:15
  103.3 10.0 %collective-permute-start.18 = (bf16[128,1024]{1,0:T(8,128)(2,1)S(1)}, bf16[128,1024]{1,0:T(8,128)(2,1)S(1)}, u32[]{:S(2)}, u32[]{:S(2)}) collective-permute-start(bf16[128,1024]{1,0:T(8,128)(2,1)S(1)} %get-tuple-element.44), channel_id=1, source_target_pairs={{0,8},{8,0},{1,9},{9,1},{2,10},{10,2},{3,11},{11,3},{4,12},{12,4},... | collective-permute-start | bytes 786440 | tf_op jit(solution)/shard_map/ppermute | solution.py:19
  105.7 14.9 %collective-permute-start.20 = (bf16[128,1024]{1,0:T(8,128)(2,1)S(1)}, bf16[128,1024]{1,0:T(8,128)(2,1)S(1)}, u32[]{:S(2)}, u32[]{:S(2)}) collective-permute-start(bf16[128,1024]{1,0:T(8,128)(2,1)S(1)} %get-tuple-element.48), channel_id=1, source_target_pairs={{0,6},{2,0},{4,2},{6,4},{1,7},{3,1},{5,3},{7,5},{8,14},{10,8},{12,... | collective-permute-start | bytes 786440 | tf_op jit(solution)/shard_map/ppermute | solution.py:15
  106.6 14.0 %collective-permute-start.21 = (bf16[128,1024]{1,0:T(8,128)(2,1)S(1)}, bf16[128,1024]{1,0:T(8,128)(2,1)S(1)}, u32[]{:S(2)}, u32[]{:S(2)}) collective-permute-start(bf16[128,1024]{1,0:T(8,128)(2,1)S(1)} %get-tuple-element.49), channel_id=1, source_target_pairs={{0,4},{2,6},{4,0},{6,2},{1,5},{3,7},{5,1},{7,3},{8,12},{10,14},{12... | collective-permute-start | bytes 786440 | tf_op jit(solution)/shard_map/ppermute | solution.py:15
  111.6 10.0 %copy-start = (f32[2048,1152]{1,0:T(8,128)}, f32[2048,1152]{1,0:T(8,128)S(1)}, u32[]{:S(2)}) copy-start(f32[2048,1152]{1,0:T(8,128)S(1)} %bitcast_add_fusion.refs_6_) | copy-start | bytes 28311556

commit v4 on v3

--- a/solution.py
+++ b/solution.py
@@ -9,6 +9,12 @@
 
 AXES = ("x", "zl", "zh", "y", "core")
 SIZES = (4, 2, 2, 4, 2)
+
+
+NEAR = 896
+PACKED = [((slice(0, 64), slice(512 * i, 512 * i + 512)), (slice(64 * i, 64 * i + 64), slice(0, 512))) for i in range(2)]
+PACKED += [((slice(64, 96), slice(256 * i, 256 * i + 256)), (slice(32 * i, 32 * i + 32), slice(512, 768))) for i in range(4)]
+PACKED += [((slice(96, 112), slice(128 * i, 128 * i + 128)), (slice(16 * i, 16 * i + 16), slice(768, 896))) for i in range(8)]
 
 
 def shift(value, axis, step):
@@ -81,16 +87,20 @@
 
                 @pl.when(dy == at)
                 def _():
-                    out[dz] = part[i, :, :1024]
+                    if at % 2 == 0:
+                        out[dz] = part[i, :, :NEAR]
+                    else:
+                        for there, here in PACKED:
+                            out[dz, *there] = part[i, *here]
 
     for out, half in ((q1, first), (q3, second)):
         for dz in range(2):
-            out[2 + dz, :64] = half[dz, :, :1024]
-            out[2 + dz, 64:] = half[dz, :, 1024:]
+            out[dz, 112:176] = half[dz, :, :1024]
+            out[dz, 176:] = half[dz, :, 1024:]
 
 
 def cut_b(early, late, near, far):
-    for is_late, part, columns in ((0, early, slice(1024, 2048)), (1, late, slice(0, 1024))):
+    for is_late, part, columns in ((0, early, slice(NEAR, 2048)), (1, late, slice(0, 2048 - NEAR))):
         for i in range(4):
             dz, dy = distance(i, is_late)
             for at, out in enumerate((near, far)):
@@ -107,15 +117,17 @@
 
 def sum_four(q0, q1, q2, q3, *outs):
     for i, out in enumerate(outs):
-        total = sum(q[i].astype(jnp.float32) for q in (q0, q1, q2, q3))
-        out[...] = total.astype(jnp.bfloat16)
+        for there, here in PACKED:
+            total = q0[i, *here].astype(jnp.float32) + q2[i, *here].astype(jnp.float32)
+            total += q1[i, *there].astype(jnp.float32) + q3[i, *there].astype(jnp.float32)
+            out[here] = total.astype(jnp.bfloat16)
 
 
 def sum_last(a0, a1, b0, b1, b2, b3, out):
     f32 = jnp.float32
-    out[:, :1024] = (a0[...].astype(f32) + a1[...].astype(f32)).astype(jnp.bfloat16)
+    out[:, :NEAR] = (a0[...].astype(f32) + a1[...].astype(f32)).astype(jnp.bfloat16)
     total = b0[...].astype(f32) + b1[...].astype(f32) + b2[...].astype(f32) + b3[...].astype(f32)
-    out[:, 1024:] = total.astype(jnp.bfloat16)
+    out[:, NEAR:] = total.astype(jnp.bfloat16)
 
 
 def relay(block, out):
@@ -141,8 +153,8 @@
 def opposite(behind, ahead, out):
     for rows, half in ((slice(0, 64), behind), (slice(64, 128), ahead)):
         for dz in range(2):
-            out[dz, rows, :1024] = half[2 + dz, :64]
-            out[dz, rows, 1024:] = half[2 + dz, 64:]
+            out[dz, rows, :1024] = half[dz, 112:176]
+            out[dz, rows, 1024:] = half[dz, 176:]
 
 
 def pair_up(a0, a1, b0, b1, a, b):
@@ -166,7 +178,7 @@
 
     (h,) = kernel_of(relay, "relay", (h,), [(256, 1152)], (ab, g1, g3))
     h1, h3, h2 = shift(h, "x", 1), shift(h, "x", -1), swap(g2, "zl")
-    wa, wb = weight[:1024], weight[1024:]
+    wa, wb = weight[:NEAR], weight[NEAR:]
     blocks = [(4, 128, 1152)] * 2
     early_mine, early_theirs = kernel_of(by_core, "by_core_early", (g, g3, g2, g1), blocks)
 
@@ -182,9 +194,9 @@
     late_a = theirs_of(after(late_theirs, late_b), wa)
     late_b = partial(late_mine, wb, swap(late_b, "core"))
     late_a = partial(after(late_mine, late_b), wa, swap(late_a, "core"))
-    near, far = kernel_of(cut_b, "cut_b", (early, late_b), [(4, 128, 1024)] * 2)
+    near, far = kernel_of(cut_b, "cut_b", (early, late_b), [(4, 128, 2048 - NEAR)] * 2)
     far = swap(far, "zh")
-    cuts = [(2, 128, 1024), (4, 128, 1024)] * 2
+    cuts = [(2, 128, NEAR), (2, 240, 1024)] * 2
     q0, q1, q2, q3 = kernel_of(cut_a, "cut_a", (early, late_a, first, second), cuts)
     q1, q3, q2 = shift(q1, "y", 1), shift(q3, "y", -1), shift(q2, "y", 2)
 
@@ -197,9 +209,9 @@
     weight_grad = dot_tn(own, mine) + dot_tn(swap(own, "core"), theirs)
 
     waits = (q1, q2, q3, far, weight_grad)
-    s0, s1, s2, s3 = kernel_of(sum_blocks, "sum_zh", (near, far), [(128, 1024)] * 4, waits)
+    s0, s1, s2, s3 = kernel_of(sum_blocks, "sum_zh", (near, far), [(128, 2048 - NEAR)] * 4, waits)
     r1, r3, r2 = shift(s1, "y", 1), shift(s3, "y", -1), shift(s2, "y", 2)
-    a0, a1 = kernel_of(sum_four, "sum_y", (q0, q1, q2, q3), [(128, 1024)] * 2, waits)
+    a0, a1 = kernel_of(sum_four, "sum_y", (q0, q1, q2, q3), [(128, NEAR)] * 2, waits)
     a1 = swap(a1, "zh")
 
     (own,) = kernel_of(opposite, "opposite", (q1, q3), [(2, 128, 2048)], (s1,))

time: 122 us -> 121 us (level)
  transfers between devices with their start and end apart: 23 -> 23, of which waited for: 14 -> 13; matrix products, arithmetic and copies ran while one was open for 22% -> 22% of each run, Pallas kernels for 2% -> 1%
where the time goes in v4:
time: 121 us
  waiting for transfers between devices  57.4 us (47%)
  matrix products  30 us (25%)
  starting transfers between devices  27.6 us (23%)
  Pallas kernels  3.81 us (3%)
    ppermute x13, waiting for transfers between devices, shift(): return lax.ppermute(value, axis, [(i, (i + step) % 4) for i in range(4)])  36.8 us
    ppermute x10, waiting for transfers between devices, swap(): return lax.ppermute(value, axis, [(0, 1), (1, 0)])  20.6 us
    dot_general x3, matrix products, dot_tn(): lax.dot_general(a, b, (((0,), (0,)), ((), ())), preferred_element_type=jn...  17 us
    ppermute x13, starting transfers between devices, shift(): return lax.ppermute(value, axis, [(i, (i + step) % 4) for i in range(4)])  16.1 us
    dot_general x6, matrix products, dot_nt(): lax.dot_general(a, b, (((1,), (1,)), ((), ())), preferred_element_type=jn...  13 us
    ppermute x10, starting transfers between devices, swap(): return lax.ppermute(value, axis, [(0, 1), (1, 0)])  11.5 us
    pallas_call x15, Pallas kernels, kernel_of(): pl.pallas_call(lambda *refs: kernel(*refs[:n], *refs[n + len(waits):]), n...  3.81 us
  transfers between devices with their start and end apart: 23, of which 13 were waited for; matrix products, arithmetic and copies ran while one was open for 22% of the time, Pallas kernels for 1%

profile of v4, /device:TPU:24, one launch (start us, length us, event | category | flops | bytes accessed | tf_op | source)
XLA Modules:
  0.0 120.8 jit_solution(15221833187097961691)
XLA Ops:
  0.6 3.1 %collective-permute-start = (bf16[256,1152]{1,0:T(8,128)(2,1)}, bf16[256,1152]{1,0:T(8,128)(2,1)S(1)}, u32[]{:S(2)}, u32[]{:S(2)}) collective-permute-start(bf16[256,1152]{1,0:T(8,128)(2,1)} %refs_0_.3), channel_id=1, source_target_pairs={{0,64},{32,96},{64,0},{96,32},{1,65},{33,97},{65,1},{97,33},{2,66}... | collective-permute-start | bytes 1769480 | tf_op jit(solution)/shard_map/ppermute | solution.py:21
  3.7 3.9 %collective-permute-start.1 = (bf16[128,2048]{1,0:T(8,128)(2,1)}, bf16[128,2048]{1,0:T(8,128)(2,1)S(1)}, u32[]{:S(2)}, u32[]{:S(2)}) collective-permute-start(bf16[128,2048]{1,0:T(8,128)(2,1)} %refs_0_.2), channel_id=1, source_target_pairs={{0,8},{8,0},{1,9},{9,1},{2,10},{10,2},{3,11},{11,3},{4,12},{12,4},... | collective-permute-start | bytes 1572872 | tf_op jit(solution)/shard_map/ppermute | solution.py:25
  7.6 1.0 collective-permute-start.5
  8.6 12.0 %collective-permute-done.1.refs_1_ = bf16[128,2048]{1,0:T(8,128)(2,1)S(1)} collective-permute-done((bf16[128,2048]{1,0:T(8,128)(2,1)}, bf16[128,2048]{1,0:T(8,128)(2,1)S(1)}, u32[]{:S(2)}, u32[]{:S(2)}) %collective-permute-start.1) | collective-permute-done | bytes 524320 | tf_op jit(solution)/shard_map/ppermute | solution.py:25
  20.6 1.0 copy-done.2
  21.7 0.1 pair.1.refs_2_.refs_1_.refs_0_
  21.7 0.0 collective-permute-done.refs_1_.refs_2_
  21.8 0.0 copy-start.3
  21.8 1.2 %collective-permute-start.2 = (bf16[256,1152]{1,0:T(8,128)(2,1)S(1)}, bf16[256,1152]{1,0:T(8,128)(2,1)S(1)}, u32[]{:S(2)}, u32[]{:S(2)}) collective-permute-start(bf16[256,1152]{1,0:T(8,128)(2,1)S(1)} %relay_g.1.refs_0_), channel_id=1, source_target_pairs={{0,96},{32,0},{64,32},{96,64},{1,97},{33,1},{65,33},{97,65},{2,98}... | collective-permute-start | bytes 1769480 | tf_op jit(solution)/shard_map/ppermute | solution.py:21
  23.0 0.9 collective-permute-start.3
  23.9 0.2 collective-permute-start.9
  24.1 1.8 %collective-permute-start.10 = (bf16[2,128,2048]{2,1,0:T(8,128)(2,1)S(1)}, bf16[2,128,2048]{2,1,0:T(8,128)(2,1)S(1)}, u32[]{:S(2)}, u32[]{:S(2)}) collective-permute-start(bf16[2,128,2048]{2,1,0:T(8,128)(2,1)S(1)} %pair.1.refs_2_.refs_1_.refs_0_), channel_id=1, source_target_pairs={{0,6},{2,0},{4,2},{6,4},{1,7},{3,1},{5,3},{7,5},{8,14},{10,8},{12,... | collective-permute-start | bytes 3145736 | tf_op jit(solution)/shard_map/ppermute | solution.py:21
  25.9 6.9 %collective-permute-done.5.refs_0_ = bf16[256,1152]{1,0:T(8,128)(2,1)S(1)} collective-permute-done((bf16[256,1152]{1,0:T(8,128)(2,1)}, bf16[256,1152]{1,0:T(8,128)(2,1)S(1)}, u32[]{:S(2)}, u32[]{:S(2)}) %collective-permute-start.5) | collective-permute-done | bytes 589856 | tf_op jit(solution)/shard_map/ppermute | solution.py:25
  32.8 1.0 collective-permute-start.7
  33.9 1.1 collective-permute-done.2.refs_1_.refs_3_
  34.9 2.1 %collective-permute-done.3.refs_3_.refs_2_ = bf16[256,1152]{1,0:T(8,128)(2,1)S(1)} collective-permute-done((bf16[256,1152]{1,0:T(8,128)(2,1)S(1)}, bf16[256,1152]{1,0:T(8,128)(2,1)S(1)}, u32[]{:S(2)}, u32[]{:S(2)}) %collective-permute-start.3) | collective-permute-done | bytes 589856 | tf_op jit(solution)/shard_map/ppermute | solution.py:21
  37.1 0.4 collective-permute-start.6
  37.4 1.7 %collective-permute-start.8 = (bf16[256,1152]{1,0:T(8,128)(2,1)S(1)}, bf16[256,1152]{1,0:T(8,128)(2,1)S(1)}, u32[]{:S(2)}, u32[]{:S(2)}) collective-permute-start(bf16[256,1152]{1,0:T(8,128)(2,1)S(1)} %relay.1.refs_0_), channel_id=1, source_target_pairs={{0,32},{32,64},{64,96},{96,0},{1,33},{33,65},{65,97},{97,1},{2,34}... | collective-permute-start | bytes 1769480 | tf_op jit(solution)/shard_map/ppermute | solution.py:21
  39.1 0.2 by_core_early.1
  39.3 3.1 %convolution_convert_fusion.1 = bf16[512,2048]{1,0:T(8,128)(2,1)S(1)} fusion(bf16[512,1152]{1,0:T(8,128)(2,1)S(1)} %bitcast.33, bf16[2048,1152]{1,0:T(8,128)(2,1)S(1)} %copy-done.3), kind=kOutput, calls=%fused_computation.6 | convolution fusion | flops 2416967680 | bytes 7995392 | tf_op jit(solution)/shard_map/dot_general | solution.py:33
  42.5 3.7 %collective-permute-done.9.refs_0_.refs_2_ = bf16[2,128,2048]{2,1,0:T(8,128)(2,1)S(1)} collective-permute-done((bf16[2,128,2048]{2,1,0:T(8,128)(2,1)S(1)}, bf16[2,128,2048]{2,1,0:T(8,128)(2,1)S(1)}, u32[]{:S(2)}, u32[]{:S(2)}) %collective-permute-start.9) | collective-permute-done | bytes 1048608 | tf_op jit(solution)/shard_map/ppermute | solution.py:21
  46.2 0.0 collective-permute-start.4
  46.2 1.2 %collective-permute-done.10.refs_1_ = bf16[2,128,2048]{2,1,0:T(8,128)(2,1)S(1)} collective-permute-done((bf16[2,128,2048]{2,1,0:T(8,128)(2,1)S(1)}, bf16[2,128,2048]{2,1,0:T(8,128)(2,1)S(1)}, u32[]{:S(2)}, u32[]{:S(2)}) %collective-permute-start.10) | collective-permute-done | bytes 1048608 | tf_op jit(solution)/shard_map/ppermute | solution.py:21
  47.4 0.1 halves.1
  47.5 0.0 collective-permute-done.7.refs_2_
  47.5 1.4 %collective-permute-done.6.refs_1_ = bf16[256,1152]{1,0:T(8,128)(2,1)S(1)} collective-permute-done((bf16[256,1152]{1,0:T(8,128)(2,1)S(1)}, bf16[256,1152]{1,0:T(8,128)(2,1)S(1)}, u32[]{:S(2)}, u32[]{:S(2)}) %collective-permute-start.6) | collective-permute-done | bytes 589856 | tf_op jit(solution)/shard_map/ppermute | solution.py:21
  49.0 1.5 %collective-permute-done.8.refs_3_ = bf16[256,1152]{1,0:T(8,128)(2,1)S(1)} collective-permute-done((bf16[256,1152]{1,0:T(8,128)(2,1)S(1)}, bf16[256,1152]{1,0:T(8,128)(2,1)S(1)}, u32[]{:S(2)}, u32[]{:S(2)}) %collective-permute-start.8) | collective-permute-done | bytes 589856 | tf_op jit(solution)/shard_map/ppermute | solution.py:21
  50.5 0.2 by_core_late.1
  50.6 1.9 %convolution_convert_fusion = bf16[512,1152]{1,0:T(8,128)(2,1)S(1)} fusion(bf16[512,1152]{1,0:T(8,128)(2,1)S(1)} %bitcast.36, bf16[2048,1152]{1,0:T(8,128)(2,1)S(1)} %copy-done.3), kind=kOutput, calls=%fused_computation.5 | convolution fusion | flops 1359544320 | bytes 5013504 | tf_op jit(solution)/shard_map/dot_general | solution.py:33
  52.5 0.1 collective-permute-start.11
  52.6 1.5 %fusion.7 = bf16[512,896]{1,0:T(8,128)(2,1)S(1)} fusion(bf16[512,1152]{1,0:T(8,128)(2,1)S(1)} %bitcast.37, bf16[2048,1152]{1,0:T(8,128)(2,1)S(1)} %copy-done.3), kind=kOutput, calls=%fused_computation.14 | convolution fusion | flops 1057423360 | bytes 4161536 | tf_op jit(solution)/shard_map/dot_general | solution.py:33
  54.1 0.6 collective-permute-start.12
  54.7 0.8 collective-permute-done.11
  55.4 1.9 %fusion = bf16[512,1152]{1,0:T(8,128)(2,1)S(1)} fusion(bf16[512,1152]{1,0:T(8,128)(2,1)S(1)} %bitcast.34, bf16[512,1152]{1,0:T(8,128)(2,1)S(1)} %collective-permute-done.11, bf16[2048,1152]{1,0:T(8,128)(2,1)S(1)} %copy-done.3), kind=kOutput, calls=%fused_computation.4 | convolution fusion | flops 1360723968 | bytes 6193152 | tf_op jit(solution)/shard_map/dot_general | solution.py:33
  57.3 0.0 collective-permute-done.12
  57.3 1.5 %add_convert_fusion.1 = bf16[512,896]{1,0:T(8,128)(2,1)S(1)} fusion(bf16[512,896]{1,0:T(8,128)(2,1)S(1)} %collective-permute-done.12, bf16[512,1152]{1,0:T(8,128)(2,1)S(1)} %bitcast.35, bf16[2048,1152]{1,0:T(8,128)(2,1)S(1)} %copy-done.3), kind=kOutput, calls=%fused_computation.9 | convolution fusion | flops 1058340864 | bytes 5079040 | tf_op jit(solution)/shard_map/dot_general | solution.py:33
  58.9 3.1 %add_convert_fusion = bf16[512,2048]{1,0:T(8,128)(2,1)S(1)} fusion(bf16[512,2048]{1,0:T(8,128)(2,1)S(1)} %collective-permute-done.4, bf16[512,1152]{1,0:T(8,128)(2,1)S(1)} %bitcast.32, bf16[2048,1152]{1,0:T(8,128)(2,1)S(1)} %copy-done.3), kind=kOutput, calls=%fused_computation.2 | convolution fusion | flops 2419064832 | bytes 10092544 | tf_op jit(solution)/shard_map/dot_general | solution.py:33
  62.0 0.6 cut_a.1
  62.6 0.2 near_first.1
  62.8 0.2 collective-permute-start.17
  63.0 0.2 cut_b.1
  63.3 0.5 place_grads.1
  63.7 0.3 collective-permute-start.13
  64.0 2.6 %collective-permute-start.14 = (bf16[2,128,896]{2,1,0:T(8,128)(2,1)S(1)}, bf16[2,128,896]{2,1,0:T(8,128)(2,1)S(1)}, u32[]{:S(2)}, u32[]{:S(2)}) collective-permute-start(bf16[2,128,896]{2,1,0:T(8,128)(2,1)S(1)} %get-tuple-element.38), channel_id=1, source_target_pairs={{0,4},{2,6},{4,0},{6,2},{1,5},{3,7},{5,1},{7,3},{8,12},{10,14},{12... | collective-permute-start | bytes 1376264 | tf_op jit(solution)/shard_map/ppermute | solution.py:21
  66.6 2.3 %collective-permute-start.16 = (bf16[4,128,1152]{2,1,0:T(8,128)(2,1)S(1)}, bf16[4,128,1152]{2,1,0:T(8,128)(2,1)S(1)}, u32[]{:S(2)}, u32[]{:S(2)}) collective-permute-start(bf16[4,128,1152]{2,1,0:T(8,128)(2,1)S(1)} %get-tuple-element.40), channel_id=1, source_target_pairs={{0,8},{8,0},{1,9},{9,1},{2,10},{10,2},{3,11},{11,3},{4,12},{12,4},... | collective-permute-start | bytes 3538952 | tf_op jit(solution)/shard_map/ppermute | solution.py:25
  68.9 6.8 %fusion.12 = f32[2048,1152,1]{1,0,2:T(8,128)} fusion(bf16[6,128,2048]{2,1,0:T(8,128)(2,1)S(1)} %near_first.1, bf16[6,128,1152]{2,1,0:T(8,128)(2,1)S(1)} %get-tuple-element.41), kind=kOutput, calls=%fused_computation.15 | convolution fusion | flops 3623878656 | bytes 14352384 | tf_op jit(solution)/shard_map/dot_general | solution.py:37
  75.8 7.1 %bitcast_add_fusion.1.refs_8_.refs_6_ = f32[2048,1152]{1,0:T(8,128)S(1)} fusion(f32[2048,1152,1]{1,0,2:T(8,128)} %fusion.12, bf16[768,2048]{1,0:T(8,128)(2,1)S(1)} %collective-permute-done.17, bf16[768,1152]{1,0:T(8,128)(2,1)S(1)} %bitcast.40), kind=kOutput, calls=%fused_computation.1 | convolution fusion | flops 3626237952 | bytes 23789568 | tf_op jit(solution)/shard_map/dot_general | solution.py:37
  82.9 5.5 %collective-permute-done.13.refs_1_.refs_4_.refs_2_.refs_0_ = bf16[2,240,1024]{2,1,0:T(8,128)(2,1)S(1)} collective-permute-done((bf16[2,240,1024]{2,1,0:T(8,128)(2,1)S(1)}, bf16[2,240,1024]{2,1,0:T(8,128)(2,1)S(1)}, u32[]{:S(2)}, u32[]{:S(2)}) %collective-permute-start.13) | collective-permute-done | bytes 983072 | tf_op jit(solution)/shard_map/ppermute | solution.py:21
  88.4 10.9 %collective-permute-done.15.refs_3_.refs_6_.refs_4_.refs_1_ = bf16[2,240,1024]{2,1,0:T(8,128)(2,1)S(1)} collective-permute-done((bf16[2,240,1024]{2,1,0:T(8,128)(2,1)S(1)}, bf16[2,240,1024]{2,1,0:T(8,128)(2,1)S(1)}, u32[]{:S(2)}, u32[]{:S(2)}) %collective-permute-start.15) | collective-permute-done | bytes 983072 | tf_op jit(solution)/shard_map/ppermute | solution.py:21
  99.3 0.3 sum_zh.1
  99.5 0.1 opposite.1.refs_0_
  99.6 0.1 collective-permute-start.22
  99.7 1.2 collective-permute-start.19
  100.9 0.2 sum_y.1
  101.1 2.4 %collective-permute-start.18 = (bf16[128,896]{1,0:T(8,128)(2,1)S(1)}, bf16[128,896]{1,0:T(8,128)(2,1)S(1)}, u32[]{:S(2)}, u32[]{:S(2)}) collective-permute-start(bf16[128,896]{1,0:T(8,128)(2,1)S(1)} %get-tuple-element.44), channel_id=1, source_target_pairs={{0,8},{8,0},{1,9},{9,1},{2,10},{10,2},{3,11},{11,3},{4,12},{12,4},... | collective-permute-start | bytes 688136 | tf_op jit(solution)/shard_map/ppermute | solution.py:25
  103.5 0.9 collective-permute-start.20
  104.4 1.7 %collective-permute-start.21 = (bf16[128,1152]{1,0:T(8,128)(2,1)S(1)}, bf16[128,1152]{1,0:T(8,128)(2,1)S(1)}, u32[]{:S(2)}, u32[]{:S(2)}) collective-permute-start(bf16[128,1152]{1,0:T(8,128)(2,1)S(1)} %get-tuple-element.49), channel_id=1, source_target_pairs={{0,4},{2,6},{4,0},{6,2},{1,5},{3,7},{5,1},{7,3},{8,12},{10,14},{12... | collective-permute-start | bytes 884744 | tf_op jit(solution)/shard_map/ppermute | solution.py:21
  106.2 0.2 pair_up.1
  106.4 3.0 %bitcast_add_fusion.refs_6_ = f32[2048,1152]{1,0:T(8,128)S(1)} fusion(f32[2048,1152]{1,0:T(8,128)S(1)} %bitcast_add_fusion.1.refs_8_.refs_6_, bf16[4,128,2048]{2,1,0:T(8,128)(2,1)S(1)} %get-tuple-element.52, bf16[4,128,1152]{2,1,0:T(8,128)(2,1)S(1)} %get-tuple-element.53), kind=kOutput, calls=%fused_computation | convolution fusion | flops 2418278400 | bytes 22151168 | tf_op jit(solution)/shard_map/dot_general | solution.py:37
  109.4 0.0 copy-start
  109.4 0.9 collective-permute-done.18.refs_1_
  110.4 9.4 %collective-permute-done.20.refs_4_ = bf16[128,1152]{1,0:T(8,128)(2,1)S(1)} collective-permute-done((bf16[128,1152]{1,0:T(8,128)(2,1)S(1)}, bf16[128,1152]{1,0:T(8,128)(2,1)S(1)}, u32[]{:S(2)}, u32[]{:S(2)}) %collective-permute-start.20) | collective-permute-done | bytes 294944 | tf_op jit(solution)/shard_map/ppermute | solution.py:21
  119.8 0.0 collective-permute-done.21.refs_5_
  119.8 1.0 sum_last.1
  (14 shorter events, 0.1 us)
Async XLA Ops:
  0.6 21.1 %copy-start.1 = (bf16[256,1152]{1,0:T(8,128)(2,1)S(1)}, bf16[256,1152]{1,0:T(8,128)(2,1)}, u32[]{:S(2)}) copy-start(bf16[256,1152]{1,0:T(8,128)(2,1)} %refs_0_.3) | copy-start | bytes 1769476
  0.6 21.1 %collective-permute-start = (bf16[256,1152]{1,0:T(8,128)(2,1)}, bf16[256,1152]{1,0:T(8,128)(2,1)S(1)}, u32[]{:S(2)}, u32[]{:S(2)}) collective-permute-start(bf16[256,1152]{1,0:T(8,128)(2,1)} %refs_0_.3), channel_id=1, source_target_pairs={{0,64},{32,96},{64,0},{96,32},{1,65},{33,97},{65,1},{97,33},{2,66}... | collective-permute-start | bytes 1769480 | tf_op jit(solution)/shard_map/ppermute | solution.py:21
  3.7 16.9 %collective-permute-start.1 = (bf16[128,2048]{1,0:T(8,128)(2,1)}, bf16[128,2048]{1,0:T(8,128)(2,1)S(1)}, u32[]{:S(2)}, u32[]{:S(2)}) collective-permute-start(bf16[128,2048]{1,0:T(8,128)(2,1)} %refs_0_.2), channel_id=1, source_target_pairs={{0,8},{8,0},{1,9},{9,1},{2,10},{10,2},{3,11},{11,3},{4,12},{12,4},... | collective-permute-start | bytes 1572872 | tf_op jit(solution)/shard_map/ppermute | solution.py:25
  7.6 25.2 %collective-permute-start.5 = (bf16[256,1152]{1,0:T(8,128)(2,1)}, bf16[256,1152]{1,0:T(8,128)(2,1)S(1)}, u32[]{:S(2)}, u32[]{:S(2)}) collective-permute-start(bf16[256,1152]{1,0:T(8,128)(2,1)} %refs_0_.3), channel_id=1, source_target_pairs={{0,16},{16,0},{1,17},{17,1},{2,18},{18,2},{3,19},{19,3},{4,20},{20... | collective-permute-start | bytes 1769480 | tf_op jit(solution)/shard_map/ppermute | solution.py:25
  20.6 1.0 copy-start.2
  21.8 17.5 %copy-start.3 = (bf16[2048,1152]{1,0:T(8,128)(2,1)S(1)}, bf16[2048,1152]{1,0:T(8,128)(2,1)}, u32[]{:S(2)}) copy-start(bf16[2048,1152]{1,0:T(8,128)(2,1)} %param.4) | copy-start | bytes 14155780
  21.8 13.1 %collective-permute-start.2 = (bf16[256,1152]{1,0:T(8,128)(2,1)S(1)}, bf16[256,1152]{1,0:T(8,128)(2,1)S(1)}, u32[]{:S(2)}, u32[]{:S(2)}) collective-permute-start(bf16[256,1152]{1,0:T(8,128)(2,1)S(1)} %relay_g.1.refs_0_), channel_id=1, source_target_pairs={{0,96},{32,0},{64,32},{96,64},{1,97},{33,1},{65,33},{97,65},{2,98}... | collective-permute-start | bytes 1769480 | tf_op jit(solution)/shard_map/ppermute | solution.py:21
  23.0 14.0 %collective-permute-start.3 = (bf16[256,1152]{1,0:T(8,128)(2,1)S(1)}, bf16[256,1152]{1,0:T(8,128)(2,1)S(1)}, u32[]{:S(2)}, u32[]{:S(2)}) collective-permute-start(bf16[256,1152]{1,0:T(8,128)(2,1)S(1)} %relay_g.1.refs_0_), channel_id=1, source_target_pairs={{0,32},{32,64},{64,96},{96,0},{1,33},{33,65},{65,97},{97,1},{2,34}... | collective-permute-start | bytes 1769480 | tf_op jit(solution)/shard_map/ppermute | solution.py:21
  23.9 22.3 %collective-permute-start.9 = (bf16[2,128,2048]{2,1,0:T(8,128)(2,1)S(1)}, bf16[2,128,2048]{2,1,0:T(8,128)(2,1)S(1)}, u32[]{:S(2)}, u32[]{:S(2)}) collective-permute-start(bf16[2,128,2048]{2,1,0:T(8,128)(2,1)S(1)} %pair.1.refs_2_.refs_1_.refs_0_), channel_id=1, source_target_pairs={{0,2},{2,4},{4,6},{6,0},{1,3},{3,5},{5,7},{7,1},{8,10},{10,12},{12... | collective-permute-start | bytes 3145736 | tf_op jit(solution)/shard_map/ppermute | solution.py:21
  24.1 23.3 %collective-permute-start.10 = (bf16[2,128,2048]{2,1,0:T(8,128)(2,1)S(1)}, bf16[2,128,2048]{2,1,0:T(8,128)(2,1)S(1)}, u32[]{:S(2)}, u32[]{:S(2)}) collective-permute-start(bf16[2,128,2048]{2,1,0:T(8,128)(2,1)S(1)} %pair.1.refs_2_.refs_1_.refs_0_), channel_id=1, source_target_pairs={{0,6},{2,0},{4,2},{6,4},{1,7},{3,1},{5,3},{7,5},{8,14},{10,8},{12,... | collective-permute-start | bytes 3145736 | tf_op jit(solution)/shard_map/ppermute | solution.py:21
  32.8 14.7 %collective-permute-start.7 = (bf16[256,1152]{1,0:T(8,128)(2,1)S(1)}, bf16[256,1152]{1,0:T(8,128)(2,1)S(1)}, u32[]{:S(2)}, u32[]{:S(2)}) collective-permute-start(bf16[256,1152]{1,0:T(8,128)(2,1)S(1)} %collective-permute-done.refs_1_.refs_2_), channel_id=1, source_target_pairs={{0,16},{16,0},{1,17},{17,1},{2,18},{18,2},{3,19},{19,3},{4,20},{20... | collective-permute-start | bytes 1769480 | tf_op jit(solution)/shard_map/ppermute | solution.py:25
  37.1 11.9 %collective-permute-start.6 = (bf16[256,1152]{1,0:T(8,128)(2,1)S(1)}, bf16[256,1152]{1,0:T(8,128)(2,1)S(1)}, u32[]{:S(2)}, u32[]{:S(2)}) collective-permute-start(bf16[256,1152]{1,0:T(8,128)(2,1)S(1)} %relay.1.refs_0_), channel_id=1, source_target_pairs={{0,96},{32,0},{64,32},{96,64},{1,97},{33,1},{65,33},{97,65},{2,98}... | collective-permute-start | bytes 1769480 | tf_op jit(solution)/shard_map/ppermute | solution.py:21
  37.4 13.1 %collective-permute-start.8 = (bf16[256,1152]{1,0:T(8,128)(2,1)S(1)}, bf16[256,1152]{1,0:T(8,128)(2,1)S(1)}, u32[]{:S(2)}, u32[]{:S(2)}) collective-permute-start(bf16[256,1152]{1,0:T(8,128)(2,1)S(1)} %relay.1.refs_0_), channel_id=1, source_target_pairs={{0,32},{32,64},{64,96},{96,0},{1,33},{33,65},{65,97},{97,1},{2,34}... | collective-permute-start | bytes 1769480 | tf_op jit(solution)/shard_map/ppermute | solution.py:21
  46.2 12.6 %collective-permute-start.4 = (bf16[512,2048]{1,0:T(8,128)(2,1)S(1)}, bf16[512,2048]{1,0:T(8,128)(2,1)S(1)}, u32[]{:S(2)}, u32[]{:S(2)}) collective-permute-start(bf16[512,2048]{1,0:T(8,128)(2,1)S(1)} %convolution_convert_fusion.1), channel_id=1, source_target_pairs={{0,1},{1,0},{2,3},{3,2},{4,5},{5,4},{6,7},{7,6},{8,9},{9,8},{10,11... | collective-permute-start | bytes 6291464 | tf_op jit(solution)/shard_map/ppermute | solution.py:25
  52.5 2.9 %collective-permute-start.11 = (bf16[512,1152]{1,0:T(8,128)(2,1)S(1)}, bf16[512,1152]{1,0:T(8,128)(2,1)S(1)}, u32[]{:S(2)}, u32[]{:S(2)}) collective-permute-start(bf16[512,1152]{1,0:T(8,128)(2,1)S(1)} %convolution_convert_fusion), channel_id=1, source_target_pairs={{0,1},{1,0},{2,3},{3,2},{4,5},{5,4},{6,7},{7,6},{8,9},{9,8},{10,11... | collective-permute-start | bytes 3538952 | tf_op jit(solution)/shard_map/ppermute | solution.py:25
  54.1 3.2 %collective-permute-start.12 = (bf16[512,896]{1,0:T(8,128)(2,1)S(1)}, bf16[512,896]{1,0:T(8,128)(2,1)S(1)}, u32[]{:S(2)}, u32[]{:S(2)}) collective-permute-start(bf16[512,896]{1,0:T(8,128)(2,1)S(1)} %fusion.7), channel_id=1, source_target_pairs={{0,1},{1,0},{2,3},{3,2},{4,5},{5,4},{6,7},{7,6},{8,9},{9,8},{10,11... | collective-permute-start | bytes 2752520 | tf_op jit(solution)/shard_map/ppermute | solution.py:25
  62.8 12.9 %collective-permute-start.17 = (bf16[768,2048]{1,0:T(8,128)(2,1)S(1)}, bf16[768,2048]{1,0:T(8,128)(2,1)S(1)}, u32[]{:S(2)}, u32[]{:S(2)}) collective-permute-start(bf16[768,2048]{1,0:T(8,128)(2,1)S(1)} %bitcast.31), channel_id=1, source_target_pairs={{0,1},{1,0},{2,3},{3,2},{4,5},{5,4},{6,7},{7,6},{8,9},{9,8},{10,11... | collective-permute-start | bytes 9437192 | tf_op jit(solution)/shard_map/ppermute | solution.py:25
  63.7 24.7 %collective-permute-start.13 = (bf16[2,240,1024]{2,1,0:T(8,128)(2,1)S(1)}, bf16[2,240,1024]{2,1,0:T(8,128)(2,1)S(1)}, u32[]{:S(2)}, u32[]{:S(2)}) collective-permute-start(bf16[2,240,1024]{2,1,0:T(8,128)(2,1)S(1)} %get-tuple-element.37), channel_id=1, source_target_pairs={{0,2},{2,4},{4,6},{6,0},{1,3},{3,5},{5,7},{7,1},{8,10},{10,12},{12... | collective-permute-start | bytes 2949128 | tf_op jit(solution)/shard_map/ppermute | solution.py:21
  64.0 18.9 %collective-permute-start.14 = (bf16[2,128,896]{2,1,0:T(8,128)(2,1)S(1)}, bf16[2,128,896]{2,1,0:T(8,128)(2,1)S(1)}, u32[]{:S(2)}, u32[]{:S(2)}) collective-permute-start(bf16[2,128,896]{2,1,0:T(8,128)(2,1)S(1)} %get-tuple-element.38), channel_id=1, source_target_pairs={{0,4},{2,6},{4,0},{6,2},{1,5},{3,7},{5,1},{7,3},{8,12},{10,14},{12... | collective-permute-start | bytes 1376264 | tf_op jit(solution)/shard_map/ppermute | solution.py:21
  66.6 32.6 %collective-permute-start.15 = (bf16[2,240,1024]{2,1,0:T(8,128)(2,1)S(1)}, bf16[2,240,1024]{2,1,0:T(8,128)(2,1)S(1)}, u32[]{:S(2)}, u32[]{:S(2)}) collective-permute-start(bf16[2,240,1024]{2,1,0:T(8,128)(2,1)S(1)} %get-tuple-element.39), channel_id=1, source_target_pairs={{0,6},{2,0},{4,2},{6,4},{1,7},{3,1},{5,3},{7,5},{8,14},{10,8},{12,... | collective-permute-start | bytes 2949128 | tf_op jit(solution)/shard_map/ppermute | solution.py:21
  66.6 32.6 %collective-permute-start.16 = (bf16[4,128,1152]{2,1,0:T(8,128)(2,1)S(1)}, bf16[4,128,1152]{2,1,0:T(8,128)(2,1)S(1)}, u32[]{:S(2)}, u32[]{:S(2)}) collective-permute-start(bf16[4,128,1152]{2,1,0:T(8,128)(2,1)S(1)} %get-tuple-element.40), channel_id=1, source_target_pairs={{0,8},{8,0},{1,9},{9,1},{2,10},{10,2},{3,11},{11,3},{4,12},{12,4},... | collective-permute-start | bytes 3538952 | tf_op jit(solution)/shard_map/ppermute | solution.py:25
  99.6 6.5 %collective-permute-start.22 = (bf16[2,128,2048]{2,1,0:T(8,128)(2,1)S(1)}, bf16[2,128,2048]{2,1,0:T(8,128)(2,1)S(1)}, u32[]{:S(2)}, u32[]{:S(2)}) collective-permute-start(bf16[2,128,2048]{2,1,0:T(8,128)(2,1)S(1)} %opposite.1.refs_0_), channel_id=1, source_target_pairs={{0,1},{1,0},{2,3},{3,2},{4,5},{5,4},{6,7},{7,6},{8,9},{9,8},{10,11... | collective-permute-start | bytes 3145736 | tf_op jit(solution)/shard_map/ppermute | solution.py:25
  99.7 10.6 %collective-permute-start.19 = (bf16[128,1152]{1,0:T(8,128)(2,1)S(1)}, bf16[128,1152]{1,0:T(8,128)(2,1)S(1)}, u32[]{:S(2)}, u32[]{:S(2)}) collective-permute-start(bf16[128,1152]{1,0:T(8,128)(2,1)S(1)} %get-tuple-element.47.refs_2_), channel_id=1, source_target_pairs={{0,2},{2,4},{4,6},{6,0},{1,3},{3,5},{5,7},{7,1},{8,10},{10,12},{12... | collective-permute-start | bytes 884744 | tf_op jit(solution)/shard_map/ppermute | solution.py:21
  101.1 9.3 %collective-permute-start.18 = (bf16[128,896]{1,0:T(8,128)(2,1)S(1)}, bf16[128,896]{1,0:T(8,128)(2,1)S(1)}, u32[]{:S(2)}, u32[]{:S(2)}) collective-permute-start(bf16[128,896]{1,0:T(8,128)(2,1)S(1)} %get-tuple-element.44), channel_id=1, source_target_pairs={{0,8},{8,0},{1,9},{9,1},{2,10},{10,2},{3,11},{11,3},{4,12},{12,4},... | collective-permute-start | bytes 688136 | tf_op jit(solution)/shard_map/ppermute | solution.py:25
  103.5 16.3 %collective-permute-start.20 = (bf16[128,1152]{1,0:T(8,128)(2,1)S(1)}, bf16[128,1152]{1,0:T(8,128)(2,1)S(1)}, u32[]{:S(2)}, u32[]{:S(2)}) collective-permute-start(bf16[128,1152]{1,0:T(8,128)(2,1)S(1)} %get-tuple-element.48), channel_id=1, source_target_pairs={{0,6},{2,0},{4,2},{6,4},{1,7},{3,1},{5,3},{7,5},{8,14},{10,8},{12,... | collective-permute-start | bytes 884744 | tf_op jit(solution)/shard_map/ppermute | solution.py:21
  104.4 15.4 %collective-permute-start.21 = (bf16[128,1152]{1,0:T(8,128)(2,1)S(1)}, bf16[128,1152]{1,0:T(8,128)(2,1)S(1)}, u32[]{:S(2)}, u32[]{:S(2)}) collective-permute-start(bf16[128,1152]{1,0:T(8,128)(2,1)S(1)} %get-tuple-element.49), channel_id=1, source_target_pairs={{0,4},{2,6},{4,0},{6,2},{1,5},{3,7},{5,1},{7,3},{8,12},{10,14},{12... | collective-permute-start | bytes 884744 | tf_op jit(solution)/shard_map/ppermute | solution.py:21
  109.4 11.4 %copy-start = (f32[2048,1152]{1,0:T(8,128)}, f32[2048,1152]{1,0:T(8,128)S(1)}, u32[]{:S(2)}) copy-start(f32[2048,1152]{1,0:T(8,128)S(1)} %bitcast_add_fusion.refs_6_) | copy-start | bytes 28311556

commit v5 on v4

--- a/solution.py
+++ b/solution.py
@@ -176,7 +176,7 @@
     behind, ahead = shift(ab, "y", 1), shift(ab, "y", -1)
     first, second = kernel_of(halves, "halves", (behind, ahead), [(2, 64, 2048)] * 2)
 
-    (h,) = kernel_of(relay, "relay", (h,), [(256, 1152)], (ab, g1, g3))
+    (h,) = kernel_of(relay, "relay", (h,), [(256, 1152)], (ab, g1))
     h1, h3, h2 = shift(h, "x", 1), shift(h, "x", -1), swap(g2, "zl")
     wa, wb = weight[:NEAR], weight[NEAR:]
     blocks = [(4, 128, 1152)] * 2
@@ -209,7 +209,7 @@
     weight_grad = dot_tn(own, mine) + dot_tn(swap(own, "core"), theirs)
 
     waits = (q1, q2, q3, far, weight_grad)
-    s0, s1, s2, s3 = kernel_of(sum_blocks, "sum_zh", (near, far), [(128, 2048 - NEAR)] * 4, waits)
+    s0, s1, s2, s3 = kernel_of(sum_blocks, "sum_zh", (near, far), [(128, 2048 - NEAR)] * 4, (q2, weight_grad))
     r1, r3, r2 = shift(s1, "y", 1), shift(s3, "y", -1), shift(s2, "y", 2)
     a0, a1 = kernel_of(sum_four, "sum_y", (q0, q1, q2, q3), [(128, NEAR)] * 2, waits)
     a1 = swap(a1, "zh")

time: 121 us -> 121 us (level)
  waiting for transfers between devices: 57.4 us -> 56 us
    ppermute x13, waiting for transfers between devices: 36.8 us -> 24.1 us  [shift(): return lax.ppermute(value, axis, [(i, (i + step) % 4) for i in range(4)])]
    ppermute x10, waiting for transfers between devices: 20.6 us -> 31.9 us  [swap(): return lax.ppermute(value, axis, [(0, 1), (1, 0)])]
  transfers between devices with their start and end apart: 23 -> 23, of which waited for: 13 -> 12; matrix products, arithmetic and copies ran while one was open for 22% -> 22% of each run, Pallas kernels for 1% -> 2%
where the time goes in v5:
time: 121 us; the launch traced here: 120 us
  waiting for transfers between devices  56 us (46%)
  matrix products  30 us (25%)
  starting transfers between devices  28.6 us (24%)
  Pallas kernels  3.81 us (3%)
    ppermute x10, waiting for transfers between devices, swap(): return lax.ppermute(value, axis, [(0, 1), (1, 0)])  31.9 us
    ppermute x13, waiting for transfers between devices, shift(): return lax.ppermute(value, axis, [(i, (i + step) % 4) for i in range(4)])  24.1 us
    dot_general x3, matrix products, dot_tn(): lax.dot_general(a, b, (((0,), (0,)), ((), ())), preferred_element_type=jn...  17 us
    ppermute x13, starting transfers between devices, shift(): return lax.ppermute(value, axis, [(i, (i + step) % 4) for i in range(4)])  16.4 us
    dot_general x6, matrix products, dot_nt(): lax.dot_general(a, b, (((1,), (1,)), ((), ())), preferred_element_type=jn...  13 us
    ppermute x10, starting transfers between devices, swap(): return lax.ppermute(value, axis, [(0, 1), (1, 0)])  12.2 us
    pallas_call x15, Pallas kernels, kernel_of(): pl.pallas_call(lambda *refs: kernel(*refs[:n], *refs[n + len(waits):]), n...  3.81 us
  transfers between devices with their start and end apart: 23, of which 12 were waited for; matrix products, arithmetic and copies ran while one was open for 22% of the time, Pallas kernels for 2%

profile of v5, /device:TPU:24, one launch (start us, length us, event | category | flops | bytes accessed | tf_op | source)
XLA Modules:
  0.0 120.4 jit_solution(11802967885734324577)
XLA Ops:
  0.6 3.1 %collective-permute-start = (bf16[256,1152]{1,0:T(8,128)(2,1)}, bf16[256,1152]{1,0:T(8,128)(2,1)S(1)}, u32[]{:S(2)}, u32[]{:S(2)}) collective-permute-start(bf16[256,1152]{1,0:T(8,128)(2,1)} %refs_0_.3), channel_id=1, source_target_pairs={{0,64},{32,96},{64,0},{96,32},{1,65},{33,97},{65,1},{97,33},{2,66}... | collective-permute-start | bytes 1769480 | tf_op jit(solution)/shard_map/ppermute | solution.py:21
  3.7 3.9 %collective-permute-start.1 = (bf16[128,2048]{1,0:T(8,128)(2,1)}, bf16[128,2048]{1,0:T(8,128)(2,1)S(1)}, u32[]{:S(2)}, u32[]{:S(2)}) collective-permute-start(bf16[128,2048]{1,0:T(8,128)(2,1)} %refs_0_.2), channel_id=1, source_target_pairs={{0,8},{8,0},{1,9},{9,1},{2,10},{10,2},{3,11},{11,3},{4,12},{12,4},... | collective-permute-start | bytes 1572872 | tf_op jit(solution)/shard_map/ppermute | solution.py:25
  7.6 1.0 collective-permute-start.5
  8.6 12.0 %collective-permute-done.1.refs_1_ = bf16[128,2048]{1,0:T(8,128)(2,1)S(1)} collective-permute-done((bf16[128,2048]{1,0:T(8,128)(2,1)}, bf16[128,2048]{1,0:T(8,128)(2,1)S(1)}, u32[]{:S(2)}, u32[]{:S(2)}) %collective-permute-start.1) | collective-permute-done | bytes 524320 | tf_op jit(solution)/shard_map/ppermute | solution.py:25
  20.6 1.0 copy-done.2
  21.7 0.1 pair.1.refs_2_.refs_1_.refs_0_
  21.7 0.0 collective-permute-done.refs_1_.refs_2_
  21.8 0.0 copy-start.3
  21.8 0.7 collective-permute-start.3
  22.5 2.6 %collective-permute-start.2 = (bf16[256,1152]{1,0:T(8,128)(2,1)S(1)}, bf16[256,1152]{1,0:T(8,128)(2,1)S(1)}, u32[]{:S(2)}, u32[]{:S(2)}) collective-permute-start(bf16[256,1152]{1,0:T(8,128)(2,1)S(1)} %relay_g.1.refs_0_), channel_id=1, source_target_pairs={{0,96},{32,0},{64,32},{96,64},{1,97},{33,1},{65,33},{97,65},{2,98}... | collective-permute-start | bytes 1769480 | tf_op jit(solution)/shard_map/ppermute | solution.py:21
  25.1 0.2 collective-permute-start.9
  25.3 1.8 %collective-permute-start.10 = (bf16[2,128,2048]{2,1,0:T(8,128)(2,1)S(1)}, bf16[2,128,2048]{2,1,0:T(8,128)(2,1)S(1)}, u32[]{:S(2)}, u32[]{:S(2)}) collective-permute-start(bf16[2,128,2048]{2,1,0:T(8,128)(2,1)S(1)} %pair.1.refs_2_.refs_1_.refs_0_), channel_id=1, source_target_pairs={{0,6},{2,0},{4,2},{6,4},{1,7},{3,1},{5,3},{7,5},{8,14},{10,8},{12,... | collective-permute-start | bytes 3145736 | tf_op jit(solution)/shard_map/ppermute | solution.py:21
  27.1 5.7 %collective-permute-done.5.refs_0_ = bf16[256,1152]{1,0:T(8,128)(2,1)S(1)} collective-permute-done((bf16[256,1152]{1,0:T(8,128)(2,1)}, bf16[256,1152]{1,0:T(8,128)(2,1)S(1)}, u32[]{:S(2)}, u32[]{:S(2)}) %collective-permute-start.5) | collective-permute-done | bytes 589856 | tf_op jit(solution)/shard_map/ppermute | solution.py:25
  32.8 1.0 collective-permute-start.7
  33.9 2.3 %collective-permute-done.3.refs_3_.refs_2_ = bf16[256,1152]{1,0:T(8,128)(2,1)S(1)} collective-permute-done((bf16[256,1152]{1,0:T(8,128)(2,1)S(1)}, bf16[256,1152]{1,0:T(8,128)(2,1)S(1)}, u32[]{:S(2)}, u32[]{:S(2)}) %collective-permute-start.3) | collective-permute-done | bytes 589856 | tf_op jit(solution)/shard_map/ppermute | solution.py:21
  36.2 0.1 collective-permute-start.6
  36.3 0.9 collective-permute-done.2.refs_1_
  37.2 1.1 collective-permute-start.8
  38.3 0.2 by_core_early.1
  38.5 3.1 %convolution_convert_fusion.1 = bf16[512,2048]{1,0:T(8,128)(2,1)S(1)} fusion(bf16[512,1152]{1,0:T(8,128)(2,1)S(1)} %bitcast.33, bf16[2048,1152]{1,0:T(8,128)(2,1)S(1)} %copy-done.3), kind=kOutput, calls=%fused_computation.6 | convolution fusion | flops 2416967680 | bytes 7995392 | tf_op jit(solution)/shard_map/dot_general | solution.py:33
  41.6 5.8 %collective-permute-done.9.refs_0_.refs_2_ = bf16[2,128,2048]{2,1,0:T(8,128)(2,1)S(1)} collective-permute-done((bf16[2,128,2048]{2,1,0:T(8,128)(2,1)S(1)}, bf16[2,128,2048]{2,1,0:T(8,128)(2,1)S(1)}, u32[]{:S(2)}, u32[]{:S(2)}) %collective-permute-start.9) | collective-permute-done | bytes 1048608 | tf_op jit(solution)/shard_map/ppermute | solution.py:21
  47.4 1.2 %collective-permute-done.10.refs_1_ = bf16[2,128,2048]{2,1,0:T(8,128)(2,1)S(1)} collective-permute-done((bf16[2,128,2048]{2,1,0:T(8,128)(2,1)S(1)}, bf16[2,128,2048]{2,1,0:T(8,128)(2,1)S(1)}, u32[]{:S(2)}, u32[]{:S(2)}) %collective-permute-start.10) | collective-permute-done | bytes 1048608 | tf_op jit(solution)/shard_map/ppermute | solution.py:21
  48.7 0.1 halves.1
  48.7 0.0 collective-permute-done.7.refs_2_
  48.8 0.9 collective-permute-done.8.refs_3_
  49.7 0.2 by_core_late.1
  49.9 1.9 %convolution_convert_fusion = bf16[512,1152]{1,0:T(8,128)(2,1)S(1)} fusion(bf16[512,1152]{1,0:T(8,128)(2,1)S(1)} %bitcast.36, bf16[2048,1152]{1,0:T(8,128)(2,1)S(1)} %copy-done.3), kind=kOutput, calls=%fused_computation.5 | convolution fusion | flops 1359544320 | bytes 5013504 | tf_op jit(solution)/shard_map/dot_general | solution.py:33
  51.7 0.1 collective-permute-start.11
  51.8 1.5 %fusion.7 = bf16[512,896]{1,0:T(8,128)(2,1)S(1)} fusion(bf16[512,1152]{1,0:T(8,128)(2,1)S(1)} %bitcast.37, bf16[2048,1152]{1,0:T(8,128)(2,1)S(1)} %copy-done.3), kind=kOutput, calls=%fused_computation.14 | convolution fusion | flops 1057423360 | bytes 4161536 | tf_op jit(solution)/shard_map/dot_general | solution.py:33
  53.3 0.6 collective-permute-start.12
  53.9 0.8 collective-permute-done.11
  54.7 1.9 %fusion = bf16[512,1152]{1,0:T(8,128)(2,1)S(1)} fusion(bf16[512,1152]{1,0:T(8,128)(2,1)S(1)} %bitcast.34, bf16[512,1152]{1,0:T(8,128)(2,1)S(1)} %collective-permute-done.11, bf16[2048,1152]{1,0:T(8,128)(2,1)S(1)} %copy-done.3), kind=kOutput, calls=%fused_computation.4 | convolution fusion | flops 1360723968 | bytes 6193152 | tf_op jit(solution)/shard_map/dot_general | solution.py:33
  56.6 0.0 collective-permute-done.12
  56.6 1.5 %add_convert_fusion.1 = bf16[512,896]{1,0:T(8,128)(2,1)S(1)} fusion(bf16[512,896]{1,0:T(8,128)(2,1)S(1)} %collective-permute-done.12, bf16[512,1152]{1,0:T(8,128)(2,1)S(1)} %bitcast.35, bf16[2048,1152]{1,0:T(8,128)(2,1)S(1)} %copy-done.3), kind=kOutput, calls=%fused_computation.9 | convolution fusion | flops 1058340864 | bytes 5079040 | tf_op jit(solution)/shard_map/dot_general | solution.py:33
  58.1 0.0 collective-permute-done.4
  58.1 3.1 %add_convert_fusion = bf16[512,2048]{1,0:T(8,128)(2,1)S(1)} fusion(bf16[512,2048]{1,0:T(8,128)(2,1)S(1)} %collective-permute-done.4, bf16[512,1152]{1,0:T(8,128)(2,1)S(1)} %bitcast.32, bf16[2048,1152]{1,0:T(8,128)(2,1)S(1)} %copy-done.3), kind=kOutput, calls=%fused_computation.2 | convolution fusion | flops 2419064832 | bytes 10092544 | tf_op jit(solution)/shard_map/dot_general | solution.py:33
  61.2 0.6 cut_a.1
  61.8 0.2 near_first.1
  62.0 0.2 collective-permute-start.17
  62.2 0.2 cut_b.1
  62.5 0.5 place_grads.1
  63.0 0.3 collective-permute-start.13
  63.3 2.6 %collective-permute-start.14 = (bf16[2,128,896]{2,1,0:T(8,128)(2,1)S(1)}, bf16[2,128,896]{2,1,0:T(8,128)(2,1)S(1)}, u32[]{:S(2)}, u32[]{:S(2)}) collective-permute-start(bf16[2,128,896]{2,1,0:T(8,128)(2,1)S(1)} %get-tuple-element.38), channel_id=1, source_target_pairs={{0,4},{2,6},{4,0},{6,2},{1,5},{3,7},{5,1},{7,3},{8,12},{10,14},{12... | collective-permute-start | bytes 1376264 | tf_op jit(solution)/shard_map/ppermute | solution.py:21
  65.9 0.0 collective-permute-start.15
  65.9 2.6 %collective-permute-start.16 = (bf16[4,128,1152]{2,1,0:T(8,128)(2,1)S(1)}, bf16[4,128,1152]{2,1,0:T(8,128)(2,1)S(1)}, u32[]{:S(2)}, u32[]{:S(2)}) collective-permute-start(bf16[4,128,1152]{2,1,0:T(8,128)(2,1)S(1)} %get-tuple-element.40), channel_id=1, source_target_pairs={{0,8},{8,0},{1,9},{9,1},{2,10},{10,2},{3,11},{11,3},{4,12},{12,4},... | collective-permute-start | bytes 3538952 | tf_op jit(solution)/shard_map/ppermute | solution.py:25
  68.5 6.8 %fusion.12 = f32[2048,1152,1]{1,0,2:T(8,128)} fusion(bf16[6,128,2048]{2,1,0:T(8,128)(2,1)S(1)} %near_first.1, bf16[6,128,1152]{2,1,0:T(8,128)(2,1)S(1)} %get-tuple-element.41), kind=kOutput, calls=%fused_computation.15 | convolution fusion | flops 3623878656 | bytes 14352384 | tf_op jit(solution)/shard_map/dot_general | solution.py:37
  75.3 0.0 collective-permute-done.17
  75.3 7.1 %bitcast_add_fusion.1.refs_8_.refs_3_ = f32[2048,1152]{1,0:T(8,128)S(1)} fusion(f32[2048,1152,1]{1,0,2:T(8,128)} %fusion.12, bf16[768,2048]{1,0:T(8,128)(2,1)S(1)} %collective-permute-done.17, bf16[768,1152]{1,0:T(8,128)(2,1)S(1)} %bitcast.40), kind=kOutput, calls=%fused_computation.1 | convolution fusion | flops 3626237952 | bytes 23789568 | tf_op jit(solution)/shard_map/dot_general | solution.py:37
  82.5 12.6 %collective-permute-done.16.refs_7_.refs_1_ = bf16[4,128,1152]{2,1,0:T(8,128)(2,1)S(1)} collective-permute-done((bf16[4,128,1152]{2,1,0:T(8,128)(2,1)S(1)}, bf16[4,128,1152]{2,1,0:T(8,128)(2,1)S(1)}, u32[]{:S(2)}, u32[]{:S(2)}) %collective-permute-start.16) | collective-permute-done | bytes 1179680 | tf_op jit(solution)/shard_map/ppermute | solution.py:25
  95.0 0.3 sum_zh.1
  95.3 3.2 %collective-permute-done.15.refs_3_.refs_6_.refs_1_ = bf16[2,240,1024]{2,1,0:T(8,128)(2,1)S(1)} collective-permute-done((bf16[2,240,1024]{2,1,0:T(8,128)(2,1)S(1)}, bf16[2,240,1024]{2,1,0:T(8,128)(2,1)S(1)}, u32[]{:S(2)}, u32[]{:S(2)}) %collective-permute-start.15) | collective-permute-done | bytes 983072 | tf_op jit(solution)/shard_map/ppermute | solution.py:21
  98.5 0.1 opposite.1.refs_0_
  98.6 0.1 collective-permute-start.22
  98.7 1.4 %collective-permute-start.19 = (bf16[128,1152]{1,0:T(8,128)(2,1)S(1)}, bf16[128,1152]{1,0:T(8,128)(2,1)S(1)}, u32[]{:S(2)}, u32[]{:S(2)}) collective-permute-start(bf16[128,1152]{1,0:T(8,128)(2,1)S(1)} %get-tuple-element.47.refs_2_), channel_id=1, source_target_pairs={{0,2},{2,4},{4,6},{6,0},{1,3},{3,5},{5,7},{7,1},{8,10},{10,12},{12... | collective-permute-start | bytes 884744 | tf_op jit(solution)/shard_map/ppermute | solution.py:21
  100.1 0.2 sum_y.1
  100.3 2.7 %collective-permute-start.18 = (bf16[128,896]{1,0:T(8,128)(2,1)S(1)}, bf16[128,896]{1,0:T(8,128)(2,1)S(1)}, u32[]{:S(2)}, u32[]{:S(2)}) collective-permute-start(bf16[128,896]{1,0:T(8,128)(2,1)S(1)} %get-tuple-element.44), channel_id=1, source_target_pairs={{0,8},{8,0},{1,9},{9,1},{2,10},{10,2},{3,11},{11,3},{4,12},{12,4},... | collective-permute-start | bytes 688136 | tf_op jit(solution)/shard_map/ppermute | solution.py:25
  103.0 0.7 collective-permute-start.20
  103.7 1.7 %collective-permute-start.21 = (bf16[128,1152]{1,0:T(8,128)(2,1)S(1)}, bf16[128,1152]{1,0:T(8,128)(2,1)S(1)}, u32[]{:S(2)}, u32[]{:S(2)}) collective-permute-start(bf16[128,1152]{1,0:T(8,128)(2,1)S(1)} %get-tuple-element.49), channel_id=1, source_target_pairs={{0,4},{2,6},{4,0},{6,2},{1,5},{3,7},{5,1},{7,3},{8,12},{10,14},{12... | collective-permute-start | bytes 884744 | tf_op jit(solution)/shard_map/ppermute | solution.py:21
  105.5 0.2 pair_up.1
  105.7 3.0 %bitcast_add_fusion.refs_6_ = f32[2048,1152]{1,0:T(8,128)S(1)} fusion(f32[2048,1152]{1,0:T(8,128)S(1)} %bitcast_add_fusion.1.refs_8_.refs_3_, bf16[4,128,2048]{2,1,0:T(8,128)(2,1)S(1)} %get-tuple-element.52, bf16[4,128,1152]{2,1,0:T(8,128)(2,1)S(1)} %get-tuple-element.53), kind=kOutput, calls=%fused_computation | convolution fusion | flops 2418278400 | bytes 22151168 | tf_op jit(solution)/shard_map/dot_general | solution.py:37
  108.7 0.0 copy-start
  108.7 0.8 collective-permute-done.18.refs_1_
  109.6 9.8 %collective-permute-done.20.refs_4_ = bf16[128,1152]{1,0:T(8,128)(2,1)S(1)} collective-permute-done((bf16[128,1152]{1,0:T(8,128)(2,1)S(1)}, bf16[128,1152]{1,0:T(8,128)(2,1)S(1)}, u32[]{:S(2)}, u32[]{:S(2)}) %collective-permute-start.20) | collective-permute-done | bytes 294944 | tf_op jit(solution)/shard_map/ppermute | solution.py:21
  119.4 1.0 sum_last.1
  (14 shorter events, 0.1 us)
Async XLA Ops:
  0.6 21.1 %copy-start.1 = (bf16[256,1152]{1,0:T(8,128)(2,1)S(1)}, bf16[256,1152]{1,0:T(8,128)(2,1)}, u32[]{:S(2)}) copy-start(bf16[256,1152]{1,0:T(8,128)(2,1)} %refs_0_.3) | copy-start | bytes 1769476
  0.6 21.1 %collective-permute-start = (bf16[256,1152]{1,0:T(8,128)(2,1)}, bf16[256,1152]{1,0:T(8,128)(2,1)S(1)}, u32[]{:S(2)}, u32[]{:S(2)}) collective-permute-start(bf16[256,1152]{1,0:T(8,128)(2,1)} %refs_0_.3), channel_id=1, source_target_pairs={{0,64},{32,96},{64,0},{96,32},{1,65},{33,97},{65,1},{97,33},{2,66}... | collective-permute-start | bytes 1769480 | tf_op jit(solution)/shard_map/ppermute | solution.py:21
  3.7 16.9 %collective-permute-start.1 = (bf16[128,2048]{1,0:T(8,128)(2,1)}, bf16[128,2048]{1,0:T(8,128)(2,1)S(1)}, u32[]{:S(2)}, u32[]{:S(2)}) collective-permute-start(bf16[128,2048]{1,0:T(8,128)(2,1)} %refs_0_.2), channel_id=1, source_target_pairs={{0,8},{8,0},{1,9},{9,1},{2,10},{10,2},{3,11},{11,3},{4,12},{12,4},... | collective-permute-start | bytes 1572872 | tf_op jit(solution)/shard_map/ppermute | solution.py:25
  7.6 25.2 %collective-permute-start.5 = (bf16[256,1152]{1,0:T(8,128)(2,1)}, bf16[256,1152]{1,0:T(8,128)(2,1)S(1)}, u32[]{:S(2)}, u32[]{:S(2)}) collective-permute-start(bf16[256,1152]{1,0:T(8,128)(2,1)} %refs_0_.3), channel_id=1, source_target_pairs={{0,16},{16,0},{1,17},{17,1},{2,18},{18,2},{3,19},{19,3},{4,20},{20... | collective-permute-start | bytes 1769480 | tf_op jit(solution)/shard_map/ppermute | solution.py:25
  20.6 1.0 copy-start.2
  21.8 16.7 %copy-start.3 = (bf16[2048,1152]{1,0:T(8,128)(2,1)S(1)}, bf16[2048,1152]{1,0:T(8,128)(2,1)}, u32[]{:S(2)}) copy-start(bf16[2048,1152]{1,0:T(8,128)(2,1)} %param.4) | copy-start | bytes 14155780
  21.8 14.3 %collective-permute-start.3 = (bf16[256,1152]{1,0:T(8,128)(2,1)S(1)}, bf16[256,1152]{1,0:T(8,128)(2,1)S(1)}, u32[]{:S(2)}, u32[]{:S(2)}) collective-permute-start(bf16[256,1152]{1,0:T(8,128)(2,1)S(1)} %relay_g.1.refs_0_), channel_id=1, source_target_pairs={{0,32},{32,64},{64,96},{96,0},{1,33},{33,65},{65,97},{97,1},{2,34}... | collective-permute-start | bytes 1769480 | tf_op jit(solution)/shard_map/ppermute | solution.py:21
  22.5 14.7 %collective-permute-start.2 = (bf16[256,1152]{1,0:T(8,128)(2,1)S(1)}, bf16[256,1152]{1,0:T(8,128)(2,1)S(1)}, u32[]{:S(2)}, u32[]{:S(2)}) collective-permute-start(bf16[256,1152]{1,0:T(8,128)(2,1)S(1)} %relay_g.1.refs_0_), channel_id=1, source_target_pairs={{0,96},{32,0},{64,32},{96,64},{1,97},{33,1},{65,33},{97,65},{2,98}... | collective-permute-start | bytes 1769480 | tf_op jit(solution)/shard_map/ppermute | solution.py:21
  25.1 22.3 %collective-permute-start.9 = (bf16[2,128,2048]{2,1,0:T(8,128)(2,1)S(1)}, bf16[2,128,2048]{2,1,0:T(8,128)(2,1)S(1)}, u32[]{:S(2)}, u32[]{:S(2)}) collective-permute-start(bf16[2,128,2048]{2,1,0:T(8,128)(2,1)S(1)} %pair.1.refs_2_.refs_1_.refs_0_), channel_id=1, source_target_pairs={{0,2},{2,4},{4,6},{6,0},{1,3},{3,5},{5,7},{7,1},{8,10},{10,12},{12... | collective-permute-start | bytes 3145736 | tf_op jit(solution)/shard_map/ppermute | solution.py:21
  25.3 23.3 %collective-permute-start.10 = (bf16[2,128,2048]{2,1,0:T(8,128)(2,1)S(1)}, bf16[2,128,2048]{2,1,0:T(8,128)(2,1)S(1)}, u32[]{:S(2)}, u32[]{:S(2)}) collective-permute-start(bf16[2,128,2048]{2,1,0:T(8,128)(2,1)S(1)} %pair.1.refs_2_.refs_1_.refs_0_), channel_id=1, source_target_pairs={{0,6},{2,0},{4,2},{6,4},{1,7},{3,1},{5,3},{7,5},{8,14},{10,8},{12,... | collective-permute-start | bytes 3145736 | tf_op jit(solution)/shard_map/ppermute | solution.py:21
  32.8 15.9 %collective-permute-start.7 = (bf16[256,1152]{1,0:T(8,128)(2,1)S(1)}, bf16[256,1152]{1,0:T(8,128)(2,1)S(1)}, u32[]{:S(2)}, u32[]{:S(2)}) collective-permute-start(bf16[256,1152]{1,0:T(8,128)(2,1)S(1)} %collective-permute-done.refs_1_.refs_2_), channel_id=1, source_target_pairs={{0,16},{16,0},{1,17},{17,1},{2,18},{18,2},{3,19},{19,3},{4,20},{20... | collective-permute-start | bytes 1769480 | tf_op jit(solution)/shard_map/ppermute | solution.py:25
  36.2 12.6 %collective-permute-start.6 = (bf16[256,1152]{1,0:T(8,128)(2,1)S(1)}, bf16[256,1152]{1,0:T(8,128)(2,1)S(1)}, u32[]{:S(2)}, u32[]{:S(2)}) collective-permute-start(bf16[256,1152]{1,0:T(8,128)(2,1)S(1)} %relay.1.refs_0_), channel_id=1, source_target_pairs={{0,96},{32,0},{64,32},{96,64},{1,97},{33,1},{65,33},{97,65},{2,98}... | collective-permute-start | bytes 1769480 | tf_op jit(solution)/shard_map/ppermute | solution.py:21
  37.2 12.5 %collective-permute-start.8 = (bf16[256,1152]{1,0:T(8,128)(2,1)S(1)}, bf16[256,1152]{1,0:T(8,128)(2,1)S(1)}, u32[]{:S(2)}, u32[]{:S(2)}) collective-permute-start(bf16[256,1152]{1,0:T(8,128)(2,1)S(1)} %relay.1.refs_0_), channel_id=1, source_target_pairs={{0,32},{32,64},{64,96},{96,0},{1,33},{33,65},{65,97},{97,1},{2,34}... | collective-permute-start | bytes 1769480 | tf_op jit(solution)/shard_map/ppermute | solution.py:21
  47.4 10.6 %collective-permute-start.4 = (bf16[512,2048]{1,0:T(8,128)(2,1)S(1)}, bf16[512,2048]{1,0:T(8,128)(2,1)S(1)}, u32[]{:S(2)}, u32[]{:S(2)}) collective-permute-start(bf16[512,2048]{1,0:T(8,128)(2,1)S(1)} %convolution_convert_fusion.1), channel_id=1, source_target_pairs={{0,1},{1,0},{2,3},{3,2},{4,5},{5,4},{6,7},{7,6},{8,9},{9,8},{10,11... | collective-permute-start | bytes 6291464 | tf_op jit(solution)/shard_map/ppermute | solution.py:25
  51.7 2.9 %collective-permute-start.11 = (bf16[512,1152]{1,0:T(8,128)(2,1)S(1)}, bf16[512,1152]{1,0:T(8,128)(2,1)S(1)}, u32[]{:S(2)}, u32[]{:S(2)}) collective-permute-start(bf16[512,1152]{1,0:T(8,128)(2,1)S(1)} %convolution_convert_fusion), channel_id=1, source_target_pairs={{0,1},{1,0},{2,3},{3,2},{4,5},{5,4},{6,7},{7,6},{8,9},{9,8},{10,11... | collective-permute-start | bytes 3538952 | tf_op jit(solution)/shard_map/ppermute | solution.py:25
  53.3 3.2 %collective-permute-start.12 = (bf16[512,896]{1,0:T(8,128)(2,1)S(1)}, bf16[512,896]{1,0:T(8,128)(2,1)S(1)}, u32[]{:S(2)}, u32[]{:S(2)}) collective-permute-start(bf16[512,896]{1,0:T(8,128)(2,1)S(1)} %fusion.7), channel_id=1, source_target_pairs={{0,1},{1,0},{2,3},{3,2},{4,5},{5,4},{6,7},{7,6},{8,9},{9,8},{10,11... | collective-permute-start | bytes 2752520 | tf_op jit(solution)/shard_map/ppermute | solution.py:25
  62.0 13.3 %collective-permute-start.17 = (bf16[768,2048]{1,0:T(8,128)(2,1)S(1)}, bf16[768,2048]{1,0:T(8,128)(2,1)S(1)}, u32[]{:S(2)}, u32[]{:S(2)}) collective-permute-start(bf16[768,2048]{1,0:T(8,128)(2,1)S(1)} %bitcast.31), channel_id=1, source_target_pairs={{0,1},{1,0},{2,3},{3,2},{4,5},{5,4},{6,7},{7,6},{8,9},{9,8},{10,11... | collective-permute-start | bytes 9437192 | tf_op jit(solution)/shard_map/ppermute | solution.py:25
  63.0 32.4 %collective-permute-start.13 = (bf16[2,240,1024]{2,1,0:T(8,128)(2,1)S(1)}, bf16[2,240,1024]{2,1,0:T(8,128)(2,1)S(1)}, u32[]{:S(2)}, u32[]{:S(2)}) collective-permute-start(bf16[2,240,1024]{2,1,0:T(8,128)(2,1)S(1)} %get-tuple-element.37), channel_id=1, source_target_pairs={{0,2},{2,4},{4,6},{6,0},{1,3},{3,5},{5,7},{7,1},{8,10},{10,12},{12... | collective-permute-start | bytes 2949128 | tf_op jit(solution)/shard_map/ppermute | solution.py:21
  63.3 19.2 %collective-permute-start.14 = (bf16[2,128,896]{2,1,0:T(8,128)(2,1)S(1)}, bf16[2,128,896]{2,1,0:T(8,128)(2,1)S(1)}, u32[]{:S(2)}, u32[]{:S(2)}) collective-permute-start(bf16[2,128,896]{2,1,0:T(8,128)(2,1)S(1)} %get-tuple-element.38), channel_id=1, source_target_pairs={{0,4},{2,6},{4,0},{6,2},{1,5},{3,7},{5,1},{7,3},{8,12},{10,14},{12... | collective-permute-start | bytes 1376264 | tf_op jit(solution)/shard_map/ppermute | solution.py:21
  65.9 32.6 %collective-permute-start.15 = (bf16[2,240,1024]{2,1,0:T(8,128)(2,1)S(1)}, bf16[2,240,1024]{2,1,0:T(8,128)(2,1)S(1)}, u32[]{:S(2)}, u32[]{:S(2)}) collective-permute-start(bf16[2,240,1024]{2,1,0:T(8,128)(2,1)S(1)} %get-tuple-element.39), channel_id=1, source_target_pairs={{0,6},{2,0},{4,2},{6,4},{1,7},{3,1},{5,3},{7,5},{8,14},{10,8},{12,... | collective-permute-start | bytes 2949128 | tf_op jit(solution)/shard_map/ppermute | solution.py:21
  65.9 29.2 %collective-permute-start.16 = (bf16[4,128,1152]{2,1,0:T(8,128)(2,1)S(1)}, bf16[4,128,1152]{2,1,0:T(8,128)(2,1)S(1)}, u32[]{:S(2)}, u32[]{:S(2)}) collective-permute-start(bf16[4,128,1152]{2,1,0:T(8,128)(2,1)S(1)} %get-tuple-element.40), channel_id=1, source_target_pairs={{0,8},{8,0},{1,9},{9,1},{2,10},{10,2},{3,11},{11,3},{4,12},{12,4},... | collective-permute-start | bytes 3538952 | tf_op jit(solution)/shard_map/ppermute | solution.py:25
  98.6 6.9 %collective-permute-start.22 = (bf16[2,128,2048]{2,1,0:T(8,128)(2,1)S(1)}, bf16[2,128,2048]{2,1,0:T(8,128)(2,1)S(1)}, u32[]{:S(2)}, u32[]{:S(2)}) collective-permute-start(bf16[2,128,2048]{2,1,0:T(8,128)(2,1)S(1)} %opposite.1.refs_0_), channel_id=1, source_target_pairs={{0,1},{1,0},{2,3},{3,2},{4,5},{5,4},{6,7},{7,6},{8,9},{9,8},{10,11... | collective-permute-start | bytes 3145736 | tf_op jit(solution)/shard_map/ppermute | solution.py:25
  98.7 10.9 %collective-permute-start.19 = (bf16[128,1152]{1,0:T(8,128)(2,1)S(1)}, bf16[128,1152]{1,0:T(8,128)(2,1)S(1)}, u32[]{:S(2)}, u32[]{:S(2)}) collective-permute-start(bf16[128,1152]{1,0:T(8,128)(2,1)S(1)} %get-tuple-element.47.refs_2_), channel_id=1, source_target_pairs={{0,2},{2,4},{4,6},{6,0},{1,3},{3,5},{5,7},{7,1},{8,10},{10,12},{12... | collective-permute-start | bytes 884744 | tf_op jit(solution)/shard_map/ppermute | solution.py:21
  100.3 9.3 %collective-permute-start.18 = (bf16[128,896]{1,0:T(8,128)(2,1)S(1)}, bf16[128,896]{1,0:T(8,128)(2,1)S(1)}, u32[]{:S(2)}, u32[]{:S(2)}) collective-permute-start(bf16[128,896]{1,0:T(8,128)(2,1)S(1)} %get-tuple-element.44), channel_id=1, source_target_pairs={{0,8},{8,0},{1,9},{9,1},{2,10},{10,2},{3,11},{11,3},{4,12},{12,4},... | collective-permute-start | bytes 688136 | tf_op jit(solution)/shard_map/ppermute | solution.py:25
  103.0 16.3 %collective-permute-start.20 = (bf16[128,1152]{1,0:T(8,128)(2,1)S(1)}, bf16[128,1152]{1,0:T(8,128)(2,1)S(1)}, u32[]{:S(2)}, u32[]{:S(2)}) collective-permute-start(bf16[128,1152]{1,0:T(8,128)(2,1)S(1)} %get-tuple-element.48), channel_id=1, source_target_pairs={{0,6},{2,0},{4,2},{6,4},{1,7},{3,1},{5,3},{7,5},{8,14},{10,8},{12,... | collective-permute-start | bytes 884744 | tf_op jit(solution)/shard_map/ppermute | solution.py:21
  103.7 15.6 %collective-permute-start.21 = (bf16[128,1152]{1,0:T(8,128)(2,1)S(1)}, bf16[128,1152]{1,0:T(8,128)(2,1)S(1)}, u32[]{:S(2)}, u32[]{:S(2)}) collective-permute-start(bf16[128,1152]{1,0:T(8,128)(2,1)S(1)} %get-tuple-element.49), channel_id=1, source_target_pairs={{0,4},{2,6},{4,0},{6,2},{1,5},{3,7},{5,1},{7,3},{8,12},{10,14},{12... | collective-permute-start | bytes 884744 | tf_op jit(solution)/shard_map/ppermute | solution.py:21
  108.7 11.6 %copy-start = (f32[2048,1152]{1,0:T(8,128)}, f32[2048,1152]{1,0:T(8,128)S(1)}, u32[]{:S(2)}) copy-start(f32[2048,1152]{1,0:T(8,128)S(1)} %bitcast_add_fusion.refs_6_) | copy-start | bytes 28311556
